TPU v7x, 128 devices: a whole 4x4x4 slice. The times are simulated.
128 devices in a mesh: gx: 4 (over z), gy: 4 (over y), gz: 8 (over x, core).
Axes of the slice: x: 4, y: 4, z: 4, core: 2. Of those that a mesh axis runs over, the one named last changes fastest.
Arguments:
- coarse_state: float32 [64, 10, 64, 1024], P('gx', None, 'gy', 'gz'), may hold values from -6 to 6
- fine_state: float32 [2048, 16, 10, 256], P(('gx', 'gy', 'gz')), may hold values from -6 to 6
- flux_jacobians: float32 [3, 10, 10], replicated, may hold values from -2 to 2
- fine_owner: int32 [1024], replicated, may hold values from 0 to 2047, as said below
- fine_offset: int32 [1024, 3], replicated, may hold values from 1 to 7
Outputs:
- coarse_out: float32 [64, 10, 64, 1024], P('gx', None, 'gy', 'gz')
- fine_out: float32 [2048, 16, 10, 256], P(('gx', 'gy', 'gz'))
Inputs may be any that keep to these rules, and one draw needn't show every extreme that they name: `fine_owner`: every fine box has a slot of its own. The 8 fine boxes over one device's coarse boxes are held by 8 different devices with that device's gz index, and the fine boxes that one device holds lie over coarse boxes of different devices. A device's fine boxes fill its first slots, and in every gx-gy plane one device holds 16.
All inputs are finite; a program needn't handle non-finite values.
Results may differ from a plain program's by a relative error of at most 0.0003.
Values sent between devices are 32-bit elements; how exact they have to be, the bound alone decides.
No kernel may reach another device: no remote copies, remote signals or barrier semaphores. Data moves between devices by JAX's collectives and lax.ppermute only.
A program may use at most 256 MiB of HBM per device.

v0:
```python
import functools

import jax
import jax.numpy as jnp
import ml_dtypes
import numpy as np
from jax import lax
from jax.experimental import pallas as pl
from jax.experimental.pallas import tpu as pltpu
from jax.sharding import PartitionSpec as P

F = 10
B = 16
BOXES = 8
H = 8
FSLOTS = 16
LINES = 8
GROUP = 16
ROWS = F * B
HALF = F * H
F32 = jnp.float32
BF16 = jnp.bfloat16
VMEM_LIMIT = 40 * 1024 * 1024


def dot(a, b):
    return jnp.dot(a, b, preferred_element_type=F32)


def split(v):
    hi = v.astype(BF16)
    return hi, (v - hi.astype(F32)).astype(BF16)


def lanes_of(shape):
    return lax.broadcasted_iota(jnp.int32, shape, len(shape) - 1)


def expand_constants():
    rows = np.zeros((ROWS, 16), np.float32)
    for g in range(F):
        rows[g * B : (g + 1) * B, g] = 1
    first = np.zeros((128, 512), np.float32)
    second = np.zeros((128, 512), np.float32)
    mask_first = np.zeros((ROWS, 512), np.float32)
    mask_second = np.zeros((ROWS, 512), np.float32)
    for f in range(F):
        for x in range(B):
            first[f, f * B + x] = 1
            second[16 + f, f * B + x] = 1
            first[32 + f, ROWS + f * B + x] = 1
            first[48 + f, 2 * ROWS + f * B + x] = 1
            for g in range(F):
                if x > 0:
                    mask_first[g * B + x - 1, f * B + x] = 1
                if x < B - 1:
                    mask_second[g * B + x + 1, f * B + x] = 1
                mask_first[g * B + x, ROWS + f * B + x] = 1
                mask_first[g * B + x, 2 * ROWS + f * B + x] = 1
        first[16 + f, 3 * ROWS + f] = 1
        first[f, 3 * ROWS + 16 + f] = 1
        mask_first[0::B, 3 * ROWS + f] = 1
        mask_first[B - 1 :: B, 3 * ROWS + 16 + f] = 1
    return [a.astype(ml_dtypes.bfloat16) for a in (rows, first, second, mask_first, mask_second)]


def fine_constants():
    up = np.zeros((ROWS, 2 * HALF), np.float32)
    pair = np.zeros((HALF, 2 * ROWS), np.float32)
    for f in range(F):
        for x in range(B):
            for part in range(2):
                up[f * B + x, part * HALF + f * H + x // 2] = 1
                pair[f * H + x // 2, part * ROWS + f * B + x] = 0.125
    ghost = np.zeros((128, 768), np.float32)
    face = np.zeros((128, 256), np.float32)
    mean = np.zeros((512, 128), np.float32)
    for part in range(2):
        for t in range(2):
            for j in range(B):
                low, col = part * 64 + t * 32 + j // 2, t * 384
                ghost[low, col + j] = 1
                ghost[low + 8, col + 112 + j] = 1
                ghost[low + 16, col + 128 + j * B] = 1
                ghost[low + 24, col + 128 + j * B + B - 1] = 1
        for y in range(B):
            for z in range(B):
                face[part * 64 + y // 2 * H + z // 2, y * B + z] = 1
                mean[part * 256 + y * B + z, y // 2 * H + z // 2] = 1
    return [a.astype(ml_dtypes.bfloat16) for a in (up, pair, ghost, face, mean)]


def coefficients_kernel(jac_ref, rows_ref, first_ref, second_ref, mask1_ref, mask2_ref, out_ref, pad_ref):
    pad_ref[...] = jnp.zeros(pad_ref.shape, F32)
    for d in range(3):
        pad_ref[d, 0:F, 0:F] = jac_ref[d]
    shape = (16, 128)
    row = lax.broadcasted_iota(jnp.int32, shape, 0)
    eye = jnp.where((row == lanes_of(shape)) & (row < F), 0.125, 0.0).astype(F32)
    scaled = [0.125 * pad_ref[d] for d in range(3)]
    for level, (s, a, b) in enumerate(((1, 0, 2), (0, 1, 2))):
        coef = (
            (eye - scaled[s])
            + pltpu.roll(eye + scaled[s], 16, 1)
            - pltpu.roll(scaled[a], 32, 1)
            - pltpu.roll(scaled[b], 48, 1)
        )
        for part, value in enumerate(split(coef)):
            wide1 = dot(value, first_ref[...]).astype(BF16)
            wide2 = dot(value, second_ref[...]).astype(BF16)
            both = dot(rows_ref[...], wide1) * mask1_ref[...].astype(F32) + dot(
                rows_ref[...], wide2
            ) * mask2_ref[...].astype(F32)
            out_ref[level, part] = both.astype(BF16)


def faces_kernel(coarse_ref, x_lo, x_hi, y_lo, y_hi, z_lo, z_hi):
    x_lo[...] = coarse_ref[0:ROWS, :]
    x_hi[...] = coarse_ref[(B - 1) * ROWS : B * ROWS, :]
    for x in range(B):
        y_lo[x * F : x * F + F, :] = coarse_ref[pl.ds(x * ROWS, F, stride=B), :]
        y_hi[x * F : x * F + F, :] = coarse_ref[pl.ds(x * ROWS + B - 1, F, stride=B), :]
    lane = lanes_of((ROWS, 128))
    low = jnp.zeros((ROWS, 128), F32)
    high = jnp.zeros((ROWS, 128), F32)
    for x in range(B):
        plane = coarse_ref[x * ROWS : (x + 1) * ROWS, :]
        low = jnp.where(lane == x, pltpu.roll(plane, x, 1), low)
        high = jnp.where(lane == x, pltpu.roll(plane, x + 1, 1), high)
    z_lo[...] = low
    z_hi[...] = high


def coarse_kernel(
    place_ref, coarse_ref, x_lo, x_hi, y_lo, y_hi, z_lo, z_hi, coef_ref, new_ref, out_ref, mid_ref, hi_ref, lo_ref
):
    lane = lanes_of((ROWS, 128))
    ghost_zero = jnp.zeros((16 - F, 128), F32)
    for pair in range(B // 2):
        rest = []
        for side in range(2):
            x = 2 * pair + side
            cols = slice(side * 128, side * 128 + 128)
            p = coarse_ref[x * ROWS : (x + 1) * ROWS, :]
            xm = coarse_ref[(x - 1) * ROWS : x * ROWS, :] if x > 0 else x_lo[...]
            xp = coarse_ref[(x + 1) * ROWS : (x + 2) * ROWS, :] if x < B - 1 else x_hi[...]
            zm = jnp.where(lane == 0, pltpu.roll(z_lo[...], (128 - x) % 128, 1), pltpu.roll(p, 1, 1))
            zp = jnp.where(lane == 127, pltpu.roll(z_hi[...], 127 - x, 1), pltpu.roll(p, 127, 1))
            ghosts = jnp.concatenate(
                [y_lo[x * F : x * F + F, :], ghost_zero, y_hi[x * F : x * F + F, :], ghost_zero], axis=0
            )
            for at, value in ((0, p), (ROWS, xp - xm), (2 * ROWS, zp - zm), (3 * ROWS, ghosts)):
                hi, lo = split(value)
                hi_ref[at : at + value.shape[0], cols] = hi
                lo_ref[at : at + value.shape[0], cols] = lo
            rest.append(0.25 * p + 0.125 * ((xp + xm) + (zp + zm)))
        total = dot(coef_ref[0, 0], hi_ref[...]) + dot(coef_ref[0, 0], lo_ref[...]) + dot(coef_ref[0, 1], hi_ref[...])
        for side in range(2):
            x = 2 * pair + side
            new = rest[side] + total[:, side * 128 : side * 128 + 128]
            new_ref[x * ROWS : (x + 1) * ROWS, :] = new
            mid_ref[x * ROWS : (x + 1) * ROWS, :] = 0.5 * (coarse_ref[x * ROWS : (x + 1) * ROWS, :] + new)

    lane8 = lanes_of((8, 128))
    within = lane8 % 32
    base = jnp.where(within < 16, within % 8, jnp.where(within < 24, -1, 8))
    window = lane8 % 8

    def box(w, _):
        member = place_ref[w]
        ox, oy, oz = place_ref[8 + 3 * w], place_ref[9 + 3 * w], place_ref[10 + 3 * w]
        z0 = w * B + oz
        pick = base + z0
        pick_x = window + z0
        corner = ox * ROWS + oy - 1
        for f in range(F):
            acc = jnp.zeros((8, 128), F32)
            for t, ref in enumerate((coarse_ref, mid_ref)):
                for y in range(H + 2):
                    rows = ref[pl.ds(corner + f * B + y, H, stride=ROWS), :]
                    moved = jnp.take_along_axis(rows, pick, axis=1, mode="promise_in_bounds")
                    if y == 0:
                        put = (lane8 >= 32 * t) & (lane8 < 32 * t + 8)
                    elif y == H + 1:
                        put = (lane8 >= 32 * t + 8) & (lane8 < 32 * t + 16)
                    else:
                        put = (lane8 == 32 * t + 15 + y) | (lane8 == 32 * t + 23 + y)
                    acc = jnp.where(put, moved, acc)
            out_ref[member, f * 8 : f * 8 + 8, :] = acc
        for t, ref in enumerate((coarse_ref, mid_ref)):
            for side, x in enumerate((ox - 1, ox + H)):
                first = jnp.zeros((8, 128), F32)
                second = jnp.zeros((8, 128), F32)
                for y in range(H):
                    put = (lane8 >= 64 + y * 8) & (lane8 < 72 + y * 8)
                    at = x * ROWS + oy + y
                    rows = ref[pl.ds(at, 8, stride=B), :]
                    first = jnp.where(put, jnp.take_along_axis(rows, pick_x, axis=1, mode="promise_in_bounds"), first)
                    tail = jnp.concatenate(
                        [ref[pl.ds(at + 8 * B, F - 8, stride=B), :], jnp.zeros((16 - F, 128), F32)], axis=0
                    )
                    second = jnp.where(
                        put, jnp.take_along_axis(tail, pick_x, axis=1, mode="promise_in_bounds"), second
                    )
                at = (2 * t + side) * 16
                old = out_ref[member, at : at + 16, :]
                out_ref[member, at : at + 16, :] = jnp.where(
                    lanes_of((16, 128)) < 64, old, jnp.concatenate([first, second], axis=0)
                )
        return 0

    lax.fori_loop(0, BOXES, box, 0)


def fine_kernel(
    source_ref, fine_ref, arrived_ref, coef_ref, up_ref, pair_ref, ghost_ref, face_ref, mean_ref, out_ref, back_ref,
    hi_ref, lo_ref, wide_ref
):
    slot = pl.program_id(0)
    source = source_ref[slot]

    @pl.when(source < 0)
    def _():
        out_ref[...] = jnp.zeros(out_ref.shape, F32)

    @pl.when(source >= 0)
    def _():
        message = arrived_ref[source]
        m_hi, m_lo = split(message)
        lifted = dot(up_ref[...], jnp.concatenate([m_hi, m_lo], axis=0))
        lane = lanes_of((ROWS, 128))
        hi = lifted.astype(BF16).astype(F32)
        mixed = jnp.where(lane < 64, hi, pltpu.roll(lifted - hi, 64, 1)).astype(BF16)
        wide_ref[...] = dot(mixed, ghost_ref[...])
        top = message[0:64, :]
        hi = top.astype(BF16).astype(F32)
        mixed = jnp.where(lanes_of((64, 128)) < 64, pltpu.roll(top - hi, 64, 1), hi).astype(BF16)
        x_ghosts = dot(mixed, face_ref[...])
        p = fine_ref[0].reshape(ROWS, 256)
        column = lane % B
        for t in range(2):
            at = 384 * t
            gy = wide_ref[:, at : at + 128]
            gz_a = wide_ref[:, at + 128 : at + 256]
            gz_b = wide_ref[:, at + 256 : at + 384]
            a, b = p[:, 0:128], p[:, 128:256]
            a_up, b_up = pltpu.roll(a, 112, 1), pltpu.roll(b, 112, 1)
            a_down, b_down = pltpu.roll(a, 16, 1), pltpu.roll(b, 16, 1)
            yp = (jnp.where(lane < 112, a_up, b_up), jnp.where(lane < 112, b_up, gy))
            ym = (jnp.where(lane < 16, gy, a_down), jnp.where(lane < 16, a_down, b_down))
            zp = (
                jnp.where(column == B - 1, gz_a, pltpu.roll(a, 127, 1)),
                jnp.where(column == B - 1, gz_b, pltpu.roll(b, 127, 1)),
            )
            zm = (
                jnp.where(column == 0, gz_a, pltpu.roll(a, 1, 1)),
                jnp.where(column == 0, gz_b, pltpu.roll(b, 1, 1)),
            )
            rest = []
            for k, v in enumerate((a, b)):
                cols = slice(128 * k, 128 * k + 128)
                for start, value in ((0, v), (ROWS, yp[k] - ym[k]), (2 * ROWS, zp[k] - zm[k])):
                    v_hi, v_lo = split(value)
                    hi_ref[start : start + ROWS, cols] = v_hi
                    lo_ref[start : start + ROWS, cols] = v_lo
                rest.append(0.25 * v + 0.125 * ((yp[k] + ym[k]) + (zp[k] + zm[k])))
            g_hi, g_lo = split(x_ghosts[32 * t : 32 * t + 32, :])
            hi_ref[3 * ROWS : 3 * ROWS + 32, :] = g_hi
            lo_ref[3 * ROWS : 3 * ROWS + 32, :] = g_lo
            total = (
                dot(coef_ref[1, 0], hi_ref[...]) + dot(coef_ref[1, 0], lo_ref[...]) + dot(coef_ref[1, 1], hi_ref[...])
            )
            p = jnp.concatenate(rest, axis=1) + total
        out_ref[0] = p.reshape(F, B, 256)
        p_hi, p_lo = split(p)
        paired = dot(pair_ref[...], jnp.concatenate([p_hi, p_lo], axis=0))
        q_hi, q_lo = split(paired)
        means = dot(jnp.concatenate([q_hi, q_lo], axis=1), mean_ref[...])
        back_ref[source] = jnp.where(
            lanes_of((HALF // 2, 128)) < 64, means[: HALF // 2], pltpu.roll(means[HALF // 2 :], 64, 1)
        )


def place_kernel(place_ref, new_ref, back_ref, out_ref):
    out_ref[...] = new_ref[...]
    lane = lanes_of((8, 128))

    def box(w, _):
        member = place_ref[w]
        ox, oy, oz = place_ref[8 + 3 * w], place_ref[9 + 3 * w], place_ref[10 + 3 * w]
        z0 = w * B + oz
        inside = (lane >= z0) & (lane < z0 + H)
        pick = jnp.where(inside, lane - z0, 0)
        corner = ox * ROWS + oy
        for f in range(F):
            tile = back_ref[member, f % 5 * 8 : f % 5 * 8 + 8, :]
            for y in range(H):
                moved = jnp.take_along_axis(tile, pick + (f // 5 * 64 + y * 8), axis=1, mode="promise_in_bounds")
                rows = pl.ds(corner + f * B + y, H, stride=ROWS)
                out_ref[rows, :] = jnp.where(inside, moved, out_ref[rows, :])
        return 0

    lax.fori_loop(0, BOXES, box, 0)


def vmem():
    return pl.BlockSpec(memory_space=pltpu.VMEM)


def smem():
    return pl.BlockSpec(memory_space=pltpu.SMEM)


def call(kernel, ins, outs, scratch=()):
    return pl.pallas_call(
        kernel,
        in_specs=ins,
        out_specs=[vmem() for _ in outs],
        out_shape=[jax.ShapeDtypeStruct(*out) for out in outs],
        scratch_shapes=list(scratch),
        compiler_params=pltpu.CompilerParams(vmem_limit_bytes=VMEM_LIMIT),
    )


def local(coarse_state, fine_state, flux_jacobians, fine_owner, fine_offset):
    device = lax.axis_index(("gx", "gy", "gz"))
    rows = coarse_state.reshape(B * ROWS, 128)
    fine_rows = jnp.transpose(fine_state, (0, 2, 1, 3))

    my_member = lax.dynamic_slice_in_dim(fine_owner, device * BOXES, BOXES) // (FSLOTS * LINES)
    my_offset = lax.dynamic_slice_in_dim(fine_offset, device * BOXES, BOXES, 0)
    place = jnp.concatenate([my_member, my_offset.reshape(-1)])
    slot_ids = device * FSLOTS + jnp.arange(FSLOTS, dtype=jnp.int32)
    members = jnp.arange(fine_owner.shape[0], dtype=jnp.int32) // (BOXES * LINES)
    source = jnp.max(jnp.where(fine_owner[None, :] == slot_ids[:, None], members[None, :], -1), axis=1)

    consts = expand_constants()
    coef = call(
        coefficients_kernel,
        [vmem()] * 6,
        [((2, 2, ROWS, 512), BF16)],
        [pltpu.VMEM((3, 16, 128), F32)],
    )(flux_jacobians, *consts)[0]

    face = ((ROWS, 128), F32)
    x_first, x_last, y_first, y_last, z_first, z_last = call(faces_kernel, [vmem()], [face] * 6)(rows)

    def from_below(value, axis):
        n = lax.axis_size(axis)
        return lax.ppermute(value, axis, [(i, (i + 1) % n) for i in range(n)])

    def from_above(value, axis):
        n = lax.axis_size(axis)
        return lax.ppermute(value, axis, [((i + 1) % n, i) for i in range(n)])

    halo = (
        from_below(x_last, "gx"),
        from_above(x_first, "gx"),
        from_below(y_last, "gy"),
        from_above(y_first, "gy"),
        from_below(z_last, "gz"),
        from_above(z_first, "gz"),
    )
    new, outgoing = call(
        coarse_kernel,
        [smem()] + [vmem()] * 8,
        [((B * ROWS, 128), F32), ((GROUP, HALF, 128), F32)],
        [pltpu.VMEM((B * ROWS, 128), F32), pltpu.VMEM((512, 256), BF16), pltpu.VMEM((512, 256), BF16)],
    )(place, rows, *halo, coef)
    arrived = lax.all_to_all(outgoing, ("gx", "gy"), split_axis=0, concat_axis=0, tiled=True)

    whole = lambda shape: pl.BlockSpec(shape, lambda i: (0,) * len(shape))
    block = pl.BlockSpec((1, F, B, 256), lambda i: (i, 0, 0, 0))
    fconsts = fine_constants()
    fine_new, returning = pl.pallas_call(
        fine_kernel,
        grid=(FSLOTS,),
        in_specs=[smem(), block, whole((GROUP, HALF, 128)), whole((2, 2, ROWS, 512))]
        + [whole(c.shape) for c in fconsts],
        out_specs=[block, whole((GROUP, HALF // 2, 128))],
        out_shape=[
            jax.ShapeDtypeStruct((FSLOTS, F, B, 256), F32),
            jax.ShapeDtypeStruct((GROUP, HALF // 2, 128), F32),
        ],
        scratch_shapes=[
            pltpu.VMEM((512, 256), BF16),
            pltpu.VMEM((512, 256), BF16),
            pltpu.VMEM((ROWS, 768), F32),
        ],
        compiler_params=pltpu.CompilerParams(vmem_limit_bytes=VMEM_LIMIT),
    )(source, fine_rows, arrived, coef, *fconsts)
    came_back = lax.all_to_all(returning, ("gx", "gy"), split_axis=0, concat_axis=0, tiled=True)

    coarse_out = call(place_kernel, [smem(), vmem(), vmem()], [((B * ROWS, 128), F32)])(place, new, came_back)[0]
    return coarse_out.reshape(coarse_state.shape), jnp.transpose(fine_new, (0, 2, 1, 3))


def solution(mesh):
    in_specs = (P("gx", None, "gy", "gz"), P(("gx", "gy", "gz"), None, None, None), P(), P(), P())
    out_specs = (P("gx", None, "gy", "gz"), P(("gx", "gy", "gz"), None, None, None))
    return jax.shard_map(local, mesh=mesh, in_specs=in_specs, out_specs=out_specs, check_vma=False)
```

profile of v0, /device:TPU:4, one launch (start us, length us, event | category | flops | bytes accessed | tf_op | source)
XLA Modules:
  0.0 104.3 jit_solution(4613717577111468899)
XLA Ops:
  0.7 1.3 %copy-done.1 = f32[16,10,16,128]{3,2,1,0:T(8,128)S(1)} copy-done((f32[16,10,16,128]{3,2,1,0:T(8,128)S(1)}, f32[16,10,16,128]{3,2,1,0:T(8,128)}, u32[]{:S(2)}) %copy-start.1) | copy-done | bytes 1310744
  2.7 2.0 %collective-permute-start = (f32[160,128]{1,0:T(8,128)S(1)}, f32[160,128]{1,0:T(8,128)S(1)}, u32[]{:S(2)}, u32[]{:S(2)}) collective-permute-start(f32[160,128]{1,0:T(8,128)S(1)} %get-tuple-element.12), channel_id=1, source_target_pairs={{0,32},{32,64},{64,96},{96,0},{1,33},{33,65},{65,97},{97,1},{2,34}... | collective-permute-start | bytes 245768 | tf_op jit(solution)/shard_map/ppermute | solution.py:350
  4.7 2.2 %collective-permute-start.1 = (f32[160,128]{1,0:T(8,128)S(1)}, f32[160,128]{1,0:T(8,128)S(1)}, u32[]{:S(2)}, u32[]{:S(2)}) collective-permute-start(f32[160,128]{1,0:T(8,128)S(1)} %get-tuple-element.13), channel_id=1, source_target_pairs={{32,0},{64,32},{96,64},{0,96},{33,1},{65,33},{97,65},{1,97},{34,2}... | collective-permute-start | bytes 245768 | tf_op jit(solution)/shard_map/ppermute | solution.py:354
  6.9 1.6 %collective-permute-start.2 = (f32[160,128]{1,0:T(8,128)S(1)}, f32[160,128]{1,0:T(8,128)S(1)}, u32[]{:S(2)}, u32[]{:S(2)}) collective-permute-start(f32[160,128]{1,0:T(8,128)S(1)} %get-tuple-element.14), channel_id=1, source_target_pairs={{0,8},{8,16},{16,24},{24,0},{1,9},{9,17},{17,25},{25,1},{2,10},{10... | collective-permute-start | bytes 245768 | tf_op jit(solution)/shard_map/ppermute | solution.py:350
  8.5 1.7 %collective-permute-start.3 = (f32[160,128]{1,0:T(8,128)S(1)}, f32[160,128]{1,0:T(8,128)S(1)}, u32[]{:S(2)}, u32[]{:S(2)}) collective-permute-start(f32[160,128]{1,0:T(8,128)S(1)} %get-tuple-element.15), channel_id=1, source_target_pairs={{8,0},{16,8},{24,16},{0,24},{9,1},{17,9},{25,17},{1,25},{10,2},{18... | collective-permute-start | bytes 245768 | tf_op jit(solution)/shard_map/ppermute | solution.py:354
  11.1 0.9 copy-done.6
  12.1 0.9 copy-done.7
  13.0 0.9 copy-done.9
  13.9 0.9 copy-done.10
  14.8 1.1 %shard_map.159.coef_ref = bf16[2,2,160,512]{3,2,1,0:T(8,128)(2,1)S(1)} custom-call(f32[3,10,10]{2,1,0:T(8,128)S(1)} %copy.22.jac_ref, bf16[160,16]{1,0:T(8,128)(2,1)S(1)} %copy-done.24, bf16[128,512]{1,0:T(8,128)(2,1)S(1)} %copy-done.10, bf16[128,512]{1,0:T(8,128)(2,1)S(1)} %copy-done.9, bf16[160,512]{1,0:T(8,128)(2,1)S(1)} %copy-done.7, ...), custom_call_target="tpu_custom_call" | custom-call | tf_op jit(solution)/shard_map/pallas_call | solution.py:338
  17.3 1.7 %collective-permute-start.5 = (f32[160,128]{1,0:T(8,128)S(1)}, f32[160,128]{1,0:T(8,128)S(1)}, u32[]{:S(2)}, u32[]{:S(2)}) collective-permute-start(f32[160,128]{1,0:T(8,128)S(1)} %get-tuple-element.17), channel_id=1, source_target_pairs={{1,0},{2,1},{3,2},{4,3},{5,4},{6,5},{7,6},{0,7},{9,8},{10,9},{11,1... | collective-permute-start | bytes 245768 | tf_op jit(solution)/shard_map/ppermute | solution.py:354
  21.7 0.9 copy-done.12
  23.5 0.9 copy-done.16
  24.4 0.9 copy-done.18
  25.2 0.9 copy-done.20
  26.1 7.5 %shard_map.160 = (f32[2560,128]{1,0:T(8,128)S(1)}, f32[16,80,128]{2,1,0:T(8,128)S(1)}) custom-call(s32[32]{0:T(128)S(1)} %pad_add_fusion.place_ref, f32[2560,128]{1,0:T(8,128)S(1)} %bitcast.5, f32[160,128]{1,0:T(8,128)S(1)} %copy-done.12, f32[160,128]{1,0:T(8,128)S(1)} %copy-done.14, f32[160,128]{1,0:T(8,128)S(1)} %copy-done.16, f32[160,128]{1,0:T(8,128)S(1)} %copy-done.18, ...), custom_call_target="tpu_custom_call" | custom-call | tf_op jit(solution)/shard_map/pallas_call | solution.py:364
  35.0 4.7 %all-to-all-start = ((f32[16,80,128]{2,1,0:T(8,128)}), f32[16,80,128]{2,1,0:T(8,128)S(1)}, u32[]{:S(2)}, u32[]{:S(2)}) async-start(f32[16,80,128]{2,1,0:T(8,128)} %copy-done.4), calls=%async_computation | async-start | bytes 1310720 | tf_op jit(solution)/shard_map/all_to_all | solution.py:370
  40.6 13.2 %all-to-all-done.arrived_ref = f32[16,80,128]{2,1,0:T(8,128)S(1)} async-done(((f32[16,80,128]{2,1,0:T(8,128)}), f32[16,80,128]{2,1,0:T(8,128)S(1)}, u32[]{:S(2)}, u32[]{:S(2)}) %all-to-all-start) | async-done | bytes 655392 | tf_op jit(solution)/shard_map/all_to_all | solution.py:370
  53.8 1.7 %copy-done.3 = f32[16,16,10,256]{3,1,2,0:T(8,128)S(1)} copy-done((f32[16,16,10,256]{3,1,2,0:T(8,128)S(1)}, f32[16,16,10,256]{3,1,2,0:T(8,128)}, u32[]{:S(2)}) %copy-start.3) | copy-done | bytes 2621464
  55.5 0.9 copy-done.8
  56.4 0.9 copy-done.21
  58.2 16.5 %shard_map.161 = (f32[16,10,16,256]{3,2,1,0:T(8,128)}, f32[16,40,128]{2,1,0:T(8,128)S(1)}) custom-call(s32[16]{0:T(128)S(1)} %select_reduce_fusion.source_ref, f32[16,10,16,256]{3,2,1,0:T(8,128)S(1)} %bitcast.6, f32[16,80,128]{2,1,0:T(8,128)S(1)} %all-to-all-done.arrived_ref, bf16[2,2,160,512]{3,2,1,0:T(8,128)(2,1)S(1)} %shard_map.159.coef_ref, ...), custom_call_target="tpu_custom_call" | custom-call | tf_op jit(solution)/shard_map/pallas_call | solution.py:375
  74.7 24.4 %all_to_all.10.back_ref = f32[16,40,128]{2,1,0:T(8,128)S(1)} all-to-all(f32[16,40,128]{2,1,0:T(8,128)S(1)} %get-tuple-element.20), channel_id=1, replica_groups=mesh['gx'=4,'gy'=4,'gz'=8] {'gx','gy'}, dimensions={0} | all-to-all | bytes 655360 | tf_op jit(solution)/shard_map/all_to_all | solution.py:392
  99.1 5.2 %shard_map.162 = f32[2560,128]{1,0:T(8,128)} custom-call(s32[32]{0:T(128)S(1)} %copy-done.26, f32[2560,128]{1,0:T(8,128)S(1)} %get-tuple-element.18.new_ref, f32[16,40,128]{2,1,0:T(8,128)S(1)} %all_to_all.10.back_ref), custom_call_target="tpu_custom_call" | custom-call | tf_op jit(solution)/shard_map/pallas_call | solution.py:394
  (59 shorter events, 9.7 us)
Async XLA Ops:
  0.6 9.5 %copy-start = (s32[1024,3]{0,1:T(4,128)S(1)}, s32[1024,3]{0,1:T(4,128)}, u32[]{:S(2)}) copy-start(s32[1024,3]{0,1:T(4,128)} %param.19) | copy-start | bytes 36868
  0.6 1.3 %copy-start.1 = (f32[16,10,16,128]{3,2,1,0:T(8,128)S(1)}, f32[16,10,16,128]{3,2,1,0:T(8,128)}, u32[]{:S(2)}) copy-start(f32[16,10,16,128]{3,2,1,0:T(8,128)} %param.15) | copy-start | bytes 3932164
  2.0 9.2 %copy-start.24 = (bf16[160,16]{1,0:T(8,128)(2,1)S(1)}, bf16[160,16]{1,0:T(8,128)(2,1)}, u32[]{:S(2)}) copy-start(bf16[160,16]{1,0:T(8,128)(2,1)} %constant.75.clone.rows_ref) | copy-start | bytes 15364
  2.0 19.7 %copy-start.2 = (f32[16,10,16,128]{3,2,1,0:T(8,128)S(1)}, f32[16,10,16,128]{3,2,1,0:T(8,128)}, u32[]{:S(2)}) copy-start(f32[16,10,16,128]{3,2,1,0:T(8,128)} %param.15) | copy-start | bytes 3932164
  2.7 13.9 %collective-permute-start = (f32[160,128]{1,0:T(8,128)S(1)}, f32[160,128]{1,0:T(8,128)S(1)}, u32[]{:S(2)}, u32[]{:S(2)}) collective-permute-start(f32[160,128]{1,0:T(8,128)S(1)} %get-tuple-element.12), channel_id=1, source_target_pairs={{0,32},{32,64},{64,96},{96,0},{1,33},{33,65},{65,97},{97,1},{2,34}... | collective-permute-start | bytes 245768 | tf_op jit(solution)/shard_map/ppermute | solution.py:350
  4.7 14.4 %collective-permute-start.1 = (f32[160,128]{1,0:T(8,128)S(1)}, f32[160,128]{1,0:T(8,128)S(1)}, u32[]{:S(2)}, u32[]{:S(2)}) collective-permute-start(f32[160,128]{1,0:T(8,128)S(1)} %get-tuple-element.13), channel_id=1, source_target_pairs={{32,0},{64,32},{96,64},{0,96},{33,1},{65,33},{97,65},{1,97},{34,2}... | collective-permute-start | bytes 245768 | tf_op jit(solution)/shard_map/ppermute | solution.py:354
  6.9 12.9 %collective-permute-start.2 = (f32[160,128]{1,0:T(8,128)S(1)}, f32[160,128]{1,0:T(8,128)S(1)}, u32[]{:S(2)}, u32[]{:S(2)}) collective-permute-start(f32[160,128]{1,0:T(8,128)S(1)} %get-tuple-element.14), channel_id=1, source_target_pairs={{0,8},{8,16},{16,24},{24,0},{1,9},{9,17},{17,25},{25,1},{2,10},{10... | collective-permute-start | bytes 245768 | tf_op jit(solution)/shard_map/ppermute | solution.py:350
  8.5 11.9 %collective-permute-start.3 = (f32[160,128]{1,0:T(8,128)S(1)}, f32[160,128]{1,0:T(8,128)S(1)}, u32[]{:S(2)}, u32[]{:S(2)}) collective-permute-start(f32[160,128]{1,0:T(8,128)S(1)} %get-tuple-element.15), channel_id=1, source_target_pairs={{8,0},{16,8},{24,16},{0,24},{9,1},{17,9},{25,17},{1,25},{10,2},{18... | collective-permute-start | bytes 245768 | tf_op jit(solution)/shard_map/ppermute | solution.py:354
  10.2 10.9 %collective-permute-start.4 = (f32[160,128]{1,0:T(8,128)S(1)}, f32[160,128]{1,0:T(8,128)S(1)}, u32[]{:S(2)}, u32[]{:S(2)}) collective-permute-start(f32[160,128]{1,0:T(8,128)S(1)} %get-tuple-element.16), channel_id=1, source_target_pairs={{0,1},{1,2},{2,3},{3,4},{4,5},{5,6},{6,7},{7,0},{8,9},{9,10},{10,1... | collective-permute-start | bytes 245768 | tf_op jit(solution)/shard_map/ppermute | solution.py:350
  11.1 0.9 copy-start.6
  12.1 0.9 copy-start.7
  13.0 0.9 copy-start.9
  13.9 0.9 copy-start.10
  17.3 4.4 %collective-permute-start.5 = (f32[160,128]{1,0:T(8,128)S(1)}, f32[160,128]{1,0:T(8,128)S(1)}, u32[]{:S(2)}, u32[]{:S(2)}) collective-permute-start(f32[160,128]{1,0:T(8,128)S(1)} %get-tuple-element.17), channel_id=1, source_target_pairs={{1,0},{2,1},{3,2},{4,3},{5,4},{6,5},{7,6},{0,7},{9,8},{10,9},{11,1... | collective-permute-start | bytes 245768 | tf_op jit(solution)/shard_map/ppermute | solution.py:354
  19.1 34.6 %copy-start.5 = (bf16[128,768]{1,0:T(8,128)(2,1)S(1)}, bf16[128,768]{1,0:T(8,128)(2,1)}, u32[]{:S(2)}) copy-start(bf16[128,768]{1,0:T(8,128)(2,1)} %constant.82.clone.ghost_ref) | copy-start | bytes 589828
  21.7 0.9 copy-start.12
  22.6 0.9 copy-start.14
  23.5 0.9 copy-start.16
  24.4 0.9 copy-start.18
  26.1 27.7 %copy-start.22 = (bf16[128,256]{1,0:T(8,128)(2,1)S(1)}, bf16[128,256]{1,0:T(8,128)(2,1)}, u32[]{:S(2)}) copy-start(bf16[128,256]{1,0:T(8,128)(2,1)} %constant.83.clone.face_ref) | copy-start | bytes 196612
  35.0 18.8 %all-to-all-start = ((f32[16,80,128]{2,1,0:T(8,128)}), f32[16,80,128]{2,1,0:T(8,128)S(1)}, u32[]{:S(2)}, u32[]{:S(2)}) async-start(f32[16,80,128]{2,1,0:T(8,128)} %copy-done.4), calls=%async_computation | async-start | bytes 1310720 | tf_op jit(solution)/shard_map/all_to_all | solution.py:370
  53.8 1.7 %copy-start.3 = (f32[16,16,10,256]{3,1,2,0:T(8,128)S(1)}, f32[16,16,10,256]{3,1,2,0:T(8,128)}, u32[]{:S(2)}) copy-start(f32[16,16,10,256]{3,1,2,0:T(8,128)} %param.16) | copy-start | bytes 7864324
  55.5 0.9 copy-start.8
  58.2 41.0 %copy-start.26 = (s32[32]{0:T(128)S(1)}, s32[32]{0:T(128)}, u32[]{:S(2)}) copy-start(s32[32]{0:T(128)} %copy-done.25) | copy-start | bytes 388
  (10 other events, 7.1 us)
where the time goes:
time: 106 us; the launch traced here: 104 us
  Pallas kernels  31 us (29%)
  blocking collectives  24.4 us (23%)
  local copies, waits for them, and re-layouts  19.2 us (18%)
  starting transfers between devices  13.9 us (13%)
  waiting for transfers between devices  13.2 us (12%)
  other arithmetic  1.74 us (2%)
    all_to_all x1, blocking collectives, local(): lax.all_to_all(returning, ('gx', 'gy'), split_axis=0, concat_axis=0, tile...  24.4 us
    unnamed x55, local copies, waits for them, and re-layouts  19 us
    pallas_call x1, Pallas kernels, local(): pl.pallas_call(fine_kernel, grid=(FSLOTS,), in_specs=[smem(), block, whol...  16.5 us
    all_to_all x1, waiting for transfers between devices, local(): lax.all_to_all(outgoing, ('gx', 'gy'), split_axis=0, concat_axis=0, tiled...  13.2 us
    pallas_call x1, Pallas kernels, local(): call(coarse_kernel, [smem()] + [vmem()] * 8, [((B * ROWS, 128), F32), ((G...  7.46 us
    ppermute x3, starting transfers between devices, from_above(): return lax.ppermute(value, axis, [((i + 1) % n, i) for i in range(n)])  5.61 us
    pallas_call x1, Pallas kernels, local(): call(place_kernel, [smem(), vmem(), vmem()], [((B * ROWS, 128), F32)])  5.17 us
    all_to_all x1, starting transfers between devices, local(): lax.all_to_all(outgoing, ('gx', 'gy'), split_axis=0, concat_axis=0, tiled...  4.75 us
  transfers between devices with their start and end apart: 7, of which 1 were waited for; matrix products, arithmetic and copies ran while one was open for 3% of the time, Pallas kernels for 1%

commit v1 on v0

--- a/solution.py
+++ b/solution.py
@@ -20,7 +20,8 @@
 HALF = F * H
 F32 = jnp.float32
 BF16 = jnp.bfloat16
-VMEM_LIMIT = 40 * 1024 * 1024
+VMEM_LIMIT = 60 * 1024 * 1024
+BATCH = 8
 
 
 def dot(a, b):
@@ -61,7 +62,8 @@
         first[f, 3 * ROWS + 16 + f] = 1
         mask_first[0::B, 3 * ROWS + f] = 1
         mask_first[B - 1 :: B, 3 * ROWS + 16 + f] = 1
-    return [a.astype(ml_dtypes.bfloat16) for a in (rows, first, second, mask_first, mask_second)]
+    rows = np.pad(rows, ((0, 0), (0, 512 - 16)))
+    return np.concatenate([rows, mask_first, mask_second, first, second]).astype(ml_dtypes.bfloat16)
 
 
 def fine_constants():
@@ -90,7 +92,7 @@
     return [a.astype(ml_dtypes.bfloat16) for a in (up, pair, ghost, face, mean)]
 
 
-def coefficients_kernel(jac_ref, rows_ref, first_ref, second_ref, mask1_ref, mask2_ref, out_ref, pad_ref):
+def coefficients_kernel(jac_ref, const_ref, out_ref, pad_ref):
     pad_ref[...] = jnp.zeros(pad_ref.shape, F32)
     for d in range(3):
         pad_ref[d, 0:F, 0:F] = jac_ref[d]
@@ -106,11 +108,12 @@
             - pltpu.roll(scaled[b], 48, 1)
         )
         for part, value in enumerate(split(coef)):
-            wide1 = dot(value, first_ref[...]).astype(BF16)
-            wide2 = dot(value, second_ref[...]).astype(BF16)
-            both = dot(rows_ref[...], wide1) * mask1_ref[...].astype(F32) + dot(
-                rows_ref[...], wide2
-            ) * mask2_ref[...].astype(F32)
+            wide1 = dot(value, const_ref[3 * ROWS : 3 * ROWS + 128, :]).astype(BF16)
+            wide2 = dot(value, const_ref[3 * ROWS + 128 : 3 * ROWS + 256, :]).astype(BF16)
+            rows = const_ref[0:ROWS, 0:128]
+            pad = jnp.zeros((112, 512), BF16)
+            both = dot(rows, jnp.concatenate([wide1, pad], axis=0)) * const_ref[ROWS : 2 * ROWS, :].astype(F32)
+            both += dot(rows, jnp.concatenate([wide2, pad], axis=0)) * const_ref[2 * ROWS : 3 * ROWS, :].astype(F32)
             out_ref[level, part] = both.astype(BF16)
 
 
@@ -131,35 +134,58 @@
     z_hi[...] = high
 
 
+def product(coef_ref, level, hi_ref, lo_ref, total_ref):
+    both = dot(coef_ref[level].reshape(2 * ROWS, 512), hi_ref[...])
+    total_ref[...] = both[:ROWS] + both[ROWS:] + dot(coef_ref[level, 0], lo_ref[...])
+
+
+def put_parts(hi_ref, lo_ref, cols, parts):
+    for at, value in parts:
+        hi, lo = split(value)
+        hi_ref[at : at + value.shape[0], cols] = hi
+        lo_ref[at : at + value.shape[0], cols] = lo
+
+
 def coarse_kernel(
-    place_ref, coarse_ref, x_lo, x_hi, y_lo, y_hi, z_lo, z_hi, coef_ref, new_ref, out_ref, mid_ref, hi_ref, lo_ref
+    place_ref, coarse_ref, x_lo, x_hi, y_lo, y_hi, z_lo, z_hi, coef_ref, new_ref, out_ref, mid_ref, hi_ref, lo_ref,
+    rest_ref, total_ref
 ):
-    lane = lanes_of((ROWS, 128))
+    lane = lanes_of((B, 128))
     ghost_zero = jnp.zeros((16 - F, 128), F32)
     for pair in range(B // 2):
-        rest = []
         for side in range(2):
             x = 2 * pair + side
             cols = slice(side * 128, side * 128 + 128)
-            p = coarse_ref[x * ROWS : (x + 1) * ROWS, :]
-            xm = coarse_ref[(x - 1) * ROWS : x * ROWS, :] if x > 0 else x_lo[...]
-            xp = coarse_ref[(x + 1) * ROWS : (x + 2) * ROWS, :] if x < B - 1 else x_hi[...]
-            zm = jnp.where(lane == 0, pltpu.roll(z_lo[...], (128 - x) % 128, 1), pltpu.roll(p, 1, 1))
-            zp = jnp.where(lane == 127, pltpu.roll(z_hi[...], 127 - x, 1), pltpu.roll(p, 127, 1))
-            ghosts = jnp.concatenate(
-                [y_lo[x * F : x * F + F, :], ghost_zero, y_hi[x * F : x * F + F, :], ghost_zero], axis=0
-            )
-            for at, value in ((0, p), (ROWS, xp - xm), (2 * ROWS, zp - zm), (3 * ROWS, ghosts)):
-                hi, lo = split(value)
-                hi_ref[at : at + value.shape[0], cols] = hi
-                lo_ref[at : at + value.shape[0], cols] = lo
-            rest.append(0.25 * p + 0.125 * ((xp + xm) + (zp + zm)))
-        total = dot(coef_ref[0, 0], hi_ref[...]) + dot(coef_ref[0, 0], lo_ref[...]) + dot(coef_ref[0, 1], hi_ref[...])
+            for f in range(F):
+                row = slice(f * B, f * B + B)
+                here = x * ROWS + f * B
+                p = coarse_ref[here : here + B, :]
+                xm = coarse_ref[here - ROWS : here - ROWS + B, :] if x > 0 else x_lo[row, :]
+                xp = coarse_ref[here + ROWS : here + ROWS + B, :] if x < B - 1 else x_hi[row, :]
+                zm = jnp.where(lane == 0, pltpu.roll(z_lo[row, :], (128 - x) % 128, 1), pltpu.roll(p, 1, 1))
+                zp = jnp.where(lane == 127, pltpu.roll(z_hi[row, :], 127 - x, 1), pltpu.roll(p, 127, 1))
+                put_parts(
+                    hi_ref.at[pair],
+                    lo_ref.at[pair],
+                    cols,
+                    ((f * B, p), (ROWS + f * B, xp - xm), (2 * ROWS + f * B, zp - zm)),
+                )
+                rest_ref[pair, row, cols] = 0.25 * p + 0.125 * ((xp + xm) + (zp + zm))
+            low = jnp.concatenate([y_lo[x * F : x * F + F, :], ghost_zero], axis=0)
+            high = jnp.concatenate([y_hi[x * F : x * F + F, :], ghost_zero], axis=0)
+            put_parts(hi_ref.at[pair], lo_ref.at[pair], cols, ((3 * ROWS, low), (3 * ROWS + 16, high)))
+    for pair in range(B // 2):
+        product(coef_ref, 0, hi_ref.at[pair], lo_ref.at[pair], total_ref.at[pair])
+    for pair in range(B // 2):
         for side in range(2):
             x = 2 * pair + side
-            new = rest[side] + total[:, side * 128 : side * 128 + 128]
-            new_ref[x * ROWS : (x + 1) * ROWS, :] = new
-            mid_ref[x * ROWS : (x + 1) * ROWS, :] = 0.5 * (coarse_ref[x * ROWS : (x + 1) * ROWS, :] + new)
+            cols = slice(side * 128, side * 128 + 128)
+            for f in range(F):
+                row = slice(f * B, f * B + B)
+                here = slice(x * ROWS + f * B, x * ROWS + f * B + B)
+                new = rest_ref[pair, row, cols] + total_ref[pair, row, cols]
+                new_ref[here, :] = new
+                mid_ref[here, :] = 0.5 * (coarse_ref[here, :] + new)
 
     lane8 = lanes_of((8, 128))
     within = lane8 % 32
@@ -209,76 +235,109 @@
                 )
         return 0
 
-    lax.fori_loop(0, BOXES, box, 0)
+    lax.fori_loop(0, BOXES, box, 0, unroll=2)
 
 
 def fine_kernel(
     source_ref, fine_ref, arrived_ref, coef_ref, up_ref, pair_ref, ghost_ref, face_ref, mean_ref, out_ref, back_ref,
-    hi_ref, lo_ref, wide_ref
+    hi_ref, lo_ref, wide_ref, rest_ref, total_ref, value_ref, face_out_ref, parts_ref, mixed_ref, back_scratch
 ):
-    slot = pl.program_id(0)
-    source = source_ref[slot]
-
-    @pl.when(source < 0)
+    first_slot = pl.program_id(0) * BATCH
+    sources = [source_ref[first_slot + k] for k in range(BATCH)]
+
+    @pl.when(sources[0] < 0)
     def _():
         out_ref[...] = jnp.zeros(out_ref.shape, F32)
 
-    @pl.when(source >= 0)
+    @pl.when(sources[0] >= 0)
     def _():
-        message = arrived_ref[source]
-        m_hi, m_lo = split(message)
-        lifted = dot(up_ref[...], jnp.concatenate([m_hi, m_lo], axis=0))
-        lane = lanes_of((ROWS, 128))
-        hi = lifted.astype(BF16).astype(F32)
-        mixed = jnp.where(lane < 64, hi, pltpu.roll(lifted - hi, 64, 1)).astype(BF16)
-        wide_ref[...] = dot(mixed, ghost_ref[...])
-        top = message[0:64, :]
-        hi = top.astype(BF16).astype(F32)
-        mixed = jnp.where(lanes_of((64, 128)) < 64, pltpu.roll(top - hi, 64, 1), hi).astype(BF16)
-        x_ghosts = dot(mixed, face_ref[...])
-        p = fine_ref[0].reshape(ROWS, 256)
+        lane = lanes_of((B, 128))
         column = lane % B
+        for k in range(BATCH):
+            message = arrived_ref.at[jnp.maximum(sources[k], 0)]
+            for at in range(0, HALF, 16):
+                value = message[at : at + 16, :]
+                hi, lo = split(value)
+                parts_ref[k, at : at + 16, :] = hi
+                parts_ref[k, HALF + at : HALF + at + 16, :] = lo
+                if at < 64:
+                    hi = hi.astype(F32)
+                    mixed_ref[k, ROWS + at : ROWS + at + 16, :] = jnp.where(
+                        lane < 64, pltpu.roll(value - hi, 64, 1), hi
+                    ).astype(BF16)
+        for k in range(BATCH):
+            lifted = dot(up_ref[...], parts_ref[k])
+            for f in range(F):
+                value = lifted[f * B : f * B + B]
+                hi = value.astype(BF16).astype(F32)
+                mixed_ref[k, f * B : f * B + B, :] = jnp.where(lane < 64, hi, pltpu.roll(value - hi, 64, 1)).astype(
+                    BF16
+                )
+        for k in range(BATCH):
+            wide_ref[k] = dot(mixed_ref[k, 0:ROWS, :], ghost_ref[...])
+            face_out_ref[k] = dot(mixed_ref[k, ROWS : ROWS + 64, :], face_ref[...])
         for t in range(2):
             at = 384 * t
-            gy = wide_ref[:, at : at + 128]
-            gz_a = wide_ref[:, at + 128 : at + 256]
-            gz_b = wide_ref[:, at + 256 : at + 384]
-            a, b = p[:, 0:128], p[:, 128:256]
-            a_up, b_up = pltpu.roll(a, 112, 1), pltpu.roll(b, 112, 1)
-            a_down, b_down = pltpu.roll(a, 16, 1), pltpu.roll(b, 16, 1)
-            yp = (jnp.where(lane < 112, a_up, b_up), jnp.where(lane < 112, b_up, gy))
-            ym = (jnp.where(lane < 16, gy, a_down), jnp.where(lane < 16, a_down, b_down))
-            zp = (
-                jnp.where(column == B - 1, gz_a, pltpu.roll(a, 127, 1)),
-                jnp.where(column == B - 1, gz_b, pltpu.roll(b, 127, 1)),
+            for k in range(BATCH):
+                for f in range(F):
+                    row = slice(f * B, f * B + B)
+                    if t == 0:
+                        a, b = fine_ref[k, f, :, 0:128], fine_ref[k, f, :, 128:256]
+                    else:
+                        a, b = value_ref[k, row, 0:128], value_ref[k, row, 128:256]
+                    gy = wide_ref[k, row, at : at + 128]
+                    gz_a = wide_ref[k, row, at + 128 : at + 256]
+                    gz_b = wide_ref[k, row, at + 256 : at + 384]
+                    a_up, b_up = pltpu.roll(a, 112, 1), pltpu.roll(b, 112, 1)
+                    a_down, b_down = pltpu.roll(a, 16, 1), pltpu.roll(b, 16, 1)
+                    yp = (jnp.where(lane < 112, a_up, b_up), jnp.where(lane < 112, b_up, gy))
+                    ym = (jnp.where(lane < 16, gy, a_down), jnp.where(lane < 16, a_down, b_down))
+                    zp = (
+                        jnp.where(column == B - 1, gz_a, pltpu.roll(a, 127, 1)),
+                        jnp.where(column == B - 1, gz_b, pltpu.roll(b, 127, 1)),
+                    )
+                    zm = (
+                        jnp.where(column == 0, gz_a, pltpu.roll(a, 1, 1)),
+                        jnp.where(column == 0, gz_b, pltpu.roll(b, 1, 1)),
+                    )
+                    for h, v in enumerate((a, b)):
+                        cols = slice(128 * h, 128 * h + 128)
+                        put_parts(
+                            hi_ref.at[k],
+                            lo_ref.at[k],
+                            cols,
+                            ((f * B, v), (ROWS + f * B, yp[h] - ym[h]), (2 * ROWS + f * B, zp[h] - zm[h])),
+                        )
+                        rest_ref[k, row, cols] = 0.25 * v + 0.125 * ((yp[h] + ym[h]) + (zp[h] + zm[h]))
+                put_parts(
+                    hi_ref.at[k], lo_ref.at[k], slice(None), ((3 * ROWS, face_out_ref[k, 32 * t : 32 * t + 32, :]),)
+                )
+            for k in range(BATCH):
+                product(coef_ref, 1, hi_ref.at[k], lo_ref.at[k], total_ref.at[k])
+            for k in range(BATCH):
+                for f in range(F):
+                    row = slice(f * B, f * B + B)
+                    value = rest_ref[k, row, :] + total_ref[k, row, :]
+                    if t == 0:
+                        value_ref[k, row, :] = value
+                    else:
+                        out_ref[k, f] = jnp.where(sources[k] >= 0, value, 0.0)
+                        hi, lo = split(value)
+                        hi_ref[k, row, :] = hi
+                        hi_ref[k, ROWS + f * B : ROWS + f * B + B, :] = lo
+        for k in range(BATCH):
+            paired = dot(pair_ref[...], hi_ref[k, 0 : 2 * ROWS, :])
+            hi, lo = split(paired)
+            means = dot(jnp.concatenate([hi, lo], axis=1), mean_ref[...])
+            back_scratch[k] = jnp.where(
+                lanes_of((HALF // 2, 128)) < 64, means[: HALF // 2], pltpu.roll(means[HALF // 2 :], 64, 1)
             )
-            zm = (
-                jnp.where(column == 0, gz_a, pltpu.roll(a, 1, 1)),
-                jnp.where(column == 0, gz_b, pltpu.roll(b, 1, 1)),
-            )
-            rest = []
-            for k, v in enumerate((a, b)):
-                cols = slice(128 * k, 128 * k + 128)
-                for start, value in ((0, v), (ROWS, yp[k] - ym[k]), (2 * ROWS, zp[k] - zm[k])):
-                    v_hi, v_lo = split(value)
-                    hi_ref[start : start + ROWS, cols] = v_hi
-                    lo_ref[start : start + ROWS, cols] = v_lo
-                rest.append(0.25 * v + 0.125 * ((yp[k] + ym[k]) + (zp[k] + zm[k])))
-            g_hi, g_lo = split(x_ghosts[32 * t : 32 * t + 32, :])
-            hi_ref[3 * ROWS : 3 * ROWS + 32, :] = g_hi
-            lo_ref[3 * ROWS : 3 * ROWS + 32, :] = g_lo
-            total = (
-                dot(coef_ref[1, 0], hi_ref[...]) + dot(coef_ref[1, 0], lo_ref[...]) + dot(coef_ref[1, 1], hi_ref[...])
-            )
-            p = jnp.concatenate(rest, axis=1) + total
-        out_ref[0] = p.reshape(F, B, 256)
-        p_hi, p_lo = split(p)
-        paired = dot(pair_ref[...], jnp.concatenate([p_hi, p_lo], axis=0))
-        q_hi, q_lo = split(paired)
-        means = dot(jnp.concatenate([q_hi, q_lo], axis=1), mean_ref[...])
-        back_ref[source] = jnp.where(
-            lanes_of((HALF // 2, 128)) < 64, means[: HALF // 2], pltpu.roll(means[HALF // 2 :], 64, 1)
-        )
+
+    for k in range(BATCH):
+
+        @pl.when(sources[k] >= 0)
+        def _():
+            back_ref[sources[k]] = back_scratch[k]
 
 
 def place_kernel(place_ref, new_ref, back_ref, out_ref):
@@ -294,32 +353,35 @@
         corner = ox * ROWS + oy
         for f in range(F):
             tile = back_ref[member, f % 5 * 8 : f % 5 * 8 + 8, :]
+            rows = [pl.ds(corner + f * B + y, H, stride=ROWS) for y in range(H)]
+            before = [out_ref[r, :] for r in rows]
             for y in range(H):
                 moved = jnp.take_along_axis(tile, pick + (f // 5 * 64 + y * 8), axis=1, mode="promise_in_bounds")
-                rows = pl.ds(corner + f * B + y, H, stride=ROWS)
-                out_ref[rows, :] = jnp.where(inside, moved, out_ref[rows, :])
+                out_ref[rows[y], :] = jnp.where(inside, moved, before[y])
         return 0
 
     lax.fori_loop(0, BOXES, box, 0)
 
 
-def vmem():
-    return pl.BlockSpec(memory_space=pltpu.VMEM)
+def whole(shape):
+    return pl.BlockSpec(shape, lambda i: (0,) * len(shape))
 
 
 def smem():
     return pl.BlockSpec(memory_space=pltpu.SMEM)
 
 
-def call(kernel, ins, outs, scratch=()):
+def call(kernel, operands, outs, scratch=(), grid=(1,), blocks=(), out_blocks=()):
+    blocks, out_blocks = dict(blocks), dict(out_blocks)
     return pl.pallas_call(
         kernel,
-        in_specs=ins,
-        out_specs=[vmem() for _ in outs],
+        grid=grid,
+        in_specs=[blocks.get(i) or (smem() if a.ndim == 1 else whole(a.shape)) for i, a in enumerate(operands)],
+        out_specs=[out_blocks.get(i) or whole(shape) for i, (shape, _) in enumerate(outs)],
         out_shape=[jax.ShapeDtypeStruct(*out) for out in outs],
         scratch_shapes=list(scratch),
         compiler_params=pltpu.CompilerParams(vmem_limit_bytes=VMEM_LIMIT),
-    )
+    )(*operands)
 
 
 def local(coarse_state, fine_state, flux_jacobians, fine_owner, fine_offset):
@@ -334,16 +396,15 @@
     members = jnp.arange(fine_owner.shape[0], dtype=jnp.int32) // (BOXES * LINES)
     source = jnp.max(jnp.where(fine_owner[None, :] == slot_ids[:, None], members[None, :], -1), axis=1)
 
-    consts = expand_constants()
     coef = call(
         coefficients_kernel,
-        [vmem()] * 6,
+        (flux_jacobians, expand_constants()),
         [((2, 2, ROWS, 512), BF16)],
         [pltpu.VMEM((3, 16, 128), F32)],
-    )(flux_jacobians, *consts)[0]
+    )[0]
 
     face = ((ROWS, 128), F32)
-    x_first, x_last, y_first, y_last, z_first, z_last = call(faces_kernel, [vmem()], [face] * 6)(rows)
+    x_first, x_last, y_first, y_last, z_first, z_last = call(faces_kernel, (rows,), [face] * 6)
 
     def from_below(value, axis):
         n = lax.axis_size(axis)
@@ -363,35 +424,35 @@
     )
     new, outgoing = call(
         coarse_kernel,
-        [smem()] + [vmem()] * 8,
+        (place, rows, *halo, coef),
         [((B * ROWS, 128), F32), ((GROUP, HALF, 128), F32)],
-        [pltpu.VMEM((B * ROWS, 128), F32), pltpu.VMEM((512, 256), BF16), pltpu.VMEM((512, 256), BF16)],
-    )(place, rows, *halo, coef)
+        [pltpu.VMEM((B * ROWS, 128), F32)]
+        + [pltpu.VMEM((B // 2, 512, 256), BF16)] * 2
+        + [pltpu.VMEM((B // 2, ROWS, 256), F32)] * 2,
+    )
     arrived = lax.all_to_all(outgoing, ("gx", "gy"), split_axis=0, concat_axis=0, tiled=True)
 
-    whole = lambda shape: pl.BlockSpec(shape, lambda i: (0,) * len(shape))
-    block = pl.BlockSpec((1, F, B, 256), lambda i: (i, 0, 0, 0))
-    fconsts = fine_constants()
-    fine_new, returning = pl.pallas_call(
+    block = pl.BlockSpec((BATCH, F, B, 256), lambda i: (i, 0, 0, 0))
+    fine_new, returning = call(
         fine_kernel,
-        grid=(FSLOTS,),
-        in_specs=[smem(), block, whole((GROUP, HALF, 128)), whole((2, 2, ROWS, 512))]
-        + [whole(c.shape) for c in fconsts],
-        out_specs=[block, whole((GROUP, HALF // 2, 128))],
-        out_shape=[
-            jax.ShapeDtypeStruct((FSLOTS, F, B, 256), F32),
-            jax.ShapeDtypeStruct((GROUP, HALF // 2, 128), F32),
+        (source, fine_rows, arrived, coef, *fine_constants()),
+        [((FSLOTS, F, B, 256), F32), ((GROUP, HALF // 2, 128), F32)],
+        [pltpu.VMEM((BATCH, 512, 256), BF16)] * 2
+        + [pltpu.VMEM((BATCH, ROWS, 768), F32)]
+        + [pltpu.VMEM((BATCH, ROWS, 256), F32)] * 3
+        + [
+            pltpu.VMEM((BATCH, 64, 256), F32),
+            pltpu.VMEM((BATCH, 2 * HALF, 128), BF16),
+            pltpu.VMEM((BATCH, ROWS + 64, 128), BF16),
+            pltpu.VMEM((BATCH, HALF // 2, 128), F32),
         ],
-        scratch_shapes=[
-            pltpu.VMEM((512, 256), BF16),
-            pltpu.VMEM((512, 256), BF16),
-            pltpu.VMEM((ROWS, 768), F32),
-        ],
-        compiler_params=pltpu.CompilerParams(vmem_limit_bytes=VMEM_LIMIT),
-    )(source, fine_rows, arrived, coef, *fconsts)
+        grid=(FSLOTS // BATCH,),
+        blocks=((1, block),),
+        out_blocks=((0, block),),
+    )
     came_back = lax.all_to_all(returning, ("gx", "gy"), split_axis=0, concat_axis=0, tiled=True)
 
-    coarse_out = call(place_kernel, [smem(), vmem(), vmem()], [((B * ROWS, 128), F32)])(place, new, came_back)[0]
+    coarse_out = call(place_kernel, (place, new, came_back), [((B * ROWS, 128), F32)])[0]
     return coarse_out.reshape(coarse_state.shape), jnp.transpose(fine_new, (0, 2, 1, 3))
 
 

time: 106 us -> 81.1 us (0.77)
  local copies, waits for them, and re-layouts: 19.2 us -> 2.34 us
  blocking collectives: 24.4 us -> 16.6 us
  waiting for transfers between devices: 13.2 us -> 15.6 us
  Pallas kernels: 31 us -> 29.4 us
    unnamed x55 -> x23, local copies, waits for them, and re-layouts: 19 us -> 2.1 us
    all_to_all x1, blocking collectives: 24.4 us -> 16.6 us  [local(): lax.all_to_all(returning, ('gx', 'gy'), split_axis=0, concat_axis=0, tile...]
    pallas_call x5, Pallas kernels: 31 us -> 29.4 us  [call(): pl.pallas_call(kernel, grid=grid, in_specs=[blocks.get(i) or (smem() if a...]
    ppermute x3, waiting for transfers between devices: 0.01 us -> 1.41 us  [from_above(): return lax.ppermute(value, axis, [((i + 1) % n, i) for i in range(n)])]
  transfers between devices with their start and end apart: 7 -> 7, of which waited for: 1 -> 2; matrix products, arithmetic and copies ran while one was open for 3% -> 3% of each run, Pallas kernels for 1% -> 4%
where the time goes in v1:
time: 81.1 us; the launch traced here: 80 us
  Pallas kernels  29.4 us (36%)
  blocking collectives  16.6 us (20%)
  waiting for transfers between devices  15.6 us (19%)
  starting transfers between devices  13.9 us (17%)
  local copies, waits for them, and re-layouts  2.34 us (3%)
  other arithmetic  1.45 us (2%)
    pallas_call x5, Pallas kernels, call(): pl.pallas_call(kernel, grid=grid, in_specs=[blocks.get(i) or (smem() if a...  29.4 us
    all_to_all x1, blocking collectives, local(): lax.all_to_all(returning, ('gx', 'gy'), split_axis=0, concat_axis=0, tile...  16.6 us
    all_to_all x1, waiting for transfers between devices, local(): lax.all_to_all(outgoing, ('gx', 'gy'), split_axis=0, concat_axis=0, tiled...  14.1 us
    ppermute x3, starting transfers between devices, from_above(): return lax.ppermute(value, axis, [((i + 1) % n, i) for i in range(n)])  5.6 us
    all_to_all x1, starting transfers between devices, local(): lax.all_to_all(outgoing, ('gx', 'gy'), split_axis=0, concat_axis=0, tiled...  4.77 us
    ppermute x3, starting transfers between devices, from_below(): return lax.ppermute(value, axis, [(i, (i + 1) % n) for i in range(n)])  3.5 us
    unnamed x23, local copies, waits for them, and re-layouts  2.1 us
  transfers between devices with their start and end apart: 7, of which 2 were waited for; matrix products, arithmetic and copies ran while one was open for 3% of the time, Pallas kernels for 4%

profile of v1, /device:TPU:4, one launch (start us, length us, event | category | flops | bytes accessed | tf_op | source)
XLA Modules:
  0.0 80.0 jit_solution(12197640968330880667)
XLA Ops:
  0.6 0.0 copy-start
  0.7 2.8 %shard_map.122 = (f32[160,128]{1,0:T(8,128)}, f32[160,128]{1,0:T(8,128)}, f32[160,128]{1,0:T(8,128)}, f32[160,128]{1,0:T(8,128)}, f32[160,128]{1,0:T(8,128)}, /*index=5*/f32[160,128]{1,0:T(8,128)}) custom-call(f32[2560,128]{1,0:T(8,128)} %bitcast.4), custom_call_target="tpu_custom_call" | custom-call | tf_op jit(solution)/shard_map/pallas_call | solution.py:376
  3.5 1.9 %collective-permute-start = (f32[160,128]{1,0:T(8,128)}, f32[160,128]{1,0:T(8,128)S(1)}, u32[]{:S(2)}, u32[]{:S(2)}) collective-permute-start(f32[160,128]{1,0:T(8,128)} %get-tuple-element.12), channel_id=1, source_target_pairs={{0,32},{32,64},{64,96},{96,0},{1,33},{33,65},{65,97},{97,1},{2,34}... | collective-permute-start | bytes 245768 | tf_op jit(solution)/shard_map/ppermute | solution.py:411
  5.4 2.2 %collective-permute-start.1 = (f32[160,128]{1,0:T(8,128)}, f32[160,128]{1,0:T(8,128)S(1)}, u32[]{:S(2)}, u32[]{:S(2)}) collective-permute-start(f32[160,128]{1,0:T(8,128)} %get-tuple-element.13), channel_id=1, source_target_pairs={{32,0},{64,32},{96,64},{0,96},{33,1},{65,33},{97,65},{1,97},{34,2}... | collective-permute-start | bytes 245768 | tf_op jit(solution)/shard_map/ppermute | solution.py:415
  7.6 1.6 %collective-permute-start.2 = (f32[160,128]{1,0:T(8,128)}, f32[160,128]{1,0:T(8,128)S(1)}, u32[]{:S(2)}, u32[]{:S(2)}) collective-permute-start(f32[160,128]{1,0:T(8,128)} %get-tuple-element.14), channel_id=1, source_target_pairs={{0,8},{8,16},{16,24},{24,0},{1,9},{9,17},{17,25},{25,1},{2,10},{10... | collective-permute-start | bytes 245768 | tf_op jit(solution)/shard_map/ppermute | solution.py:411
  9.1 1.7 %collective-permute-start.3 = (f32[160,128]{1,0:T(8,128)}, f32[160,128]{1,0:T(8,128)S(1)}, u32[]{:S(2)}, u32[]{:S(2)}) collective-permute-start(f32[160,128]{1,0:T(8,128)} %get-tuple-element.15), channel_id=1, source_target_pairs={{8,0},{16,8},{24,16},{0,24},{9,1},{17,9},{25,17},{1,25},{10,2},{18... | collective-permute-start | bytes 245768 | tf_op jit(solution)/shard_map/ppermute | solution.py:415
  10.8 0.1 constant_dynamic-slice_fusion
  10.9 0.1 copy.17
  11.0 0.1 reshape.31
  11.0 0.6 copy.18.jac_ref
  11.6 3.1 %shard_map.123.coef_ref = bf16[2,2,160,512]{3,2,1,0:T(8,128)(2,1)} custom-call(f32[3,10,10]{2,1,0:T(8,128)} %copy.18.jac_ref, bf16[736,512]{1,0:T(8,128)(2,1)} %constant.67.clone.const_ref), custom_call_target="tpu_custom_call" | custom-call | tf_op jit(solution)/shard_map/pallas_call | solution.py:376
  14.7 0.1 and_select_fusion
  14.8 1.8 %collective-permute-start.5 = (f32[160,128]{1,0:T(8,128)S(1)}, f32[160,128]{1,0:T(8,128)S(1)}, u32[]{:S(2)}, u32[]{:S(2)}) collective-permute-start(f32[160,128]{1,0:T(8,128)S(1)} %copy-done.10), channel_id=1, source_target_pairs={{1,0},{2,1},{3,2},{4,3},{5,4},{6,5},{7,6},{0,7},{9,8},{10,9},{11,1... | collective-permute-start | bytes 245768 | tf_op jit(solution)/shard_map/ppermute | solution.py:415
  16.6 0.6 pad_add_fusion.place_ref
  17.2 1.4 %collective-permute-done.5.z_hi = f32[160,128]{1,0:T(8,128)S(1)} collective-permute-done((f32[160,128]{1,0:T(8,128)S(1)}, f32[160,128]{1,0:T(8,128)S(1)}, u32[]{:S(2)}, u32[]{:S(2)}) %collective-permute-start.5) | collective-permute-done | bytes 81952 | tf_op jit(solution)/shard_map/ppermute | solution.py:415
  18.7 0.6 copy-done.7
  19.3 8.9 %shard_map.124 = (f32[2560,128]{1,0:T(8,128)}, f32[16,80,128]{2,1,0:T(8,128)}) custom-call(s32[32]{0:T(128)} %pad_add_fusion.place_ref, f32[2560,128]{1,0:T(8,128)} %bitcast.5, f32[160,128]{1,0:T(8,128)} %copy-done.2, f32[160,128]{1,0:T(8,128)} %copy-done.3, f32[160,128]{1,0:T(8,128)} %copy-done.4, f32[160,128]{1,0:T(8,128)} %copy-done.5, ...), custom_call_target="tpu_custom_call" | custom-call | tf_op jit(solution)/shard_map/pallas_call | solution.py:376
  28.2 4.8 %all-to-all-start = ((f32[16,80,128]{2,1,0:T(8,128)}), f32[16,80,128]{2,1,0:T(8,128)S(1)}, u32[]{:S(2)}, u32[]{:S(2)}) async-start(f32[16,80,128]{2,1,0:T(8,128)} %get-tuple-element.19), calls=%async_computation | async-start | bytes 1310720 | tf_op jit(solution)/shard_map/all_to_all | solution.py:433
  33.0 0.8 select_reduce_fusion.source_ref
  33.8 14.1 %all-to-all-done.arrived_ref = f32[16,80,128]{2,1,0:T(8,128)S(1)} async-done(((f32[16,80,128]{2,1,0:T(8,128)}), f32[16,80,128]{2,1,0:T(8,128)S(1)}, u32[]{:S(2)}, u32[]{:S(2)}) %all-to-all-start) | async-done | bytes 655392 | tf_op jit(solution)/shard_map/all_to_all | solution.py:433
  47.9 0.8 %copy-done.1 = f32[16,80,128]{2,1,0:T(8,128)} copy-done((f32[16,80,128]{2,1,0:T(8,128)}, f32[16,80,128]{2,1,0:T(8,128)S(1)}, u32[]{:S(2)}) %copy-start.1) | copy-done | bytes 655384
  48.7 8.6 %shard_map.125 = (f32[16,10,16,256]{3,2,1,0:T(8,128)}, f32[16,40,128]{2,1,0:T(8,128)}) custom-call(s32[16]{0:T(128)} %select_reduce_fusion.source_ref, f32[16,10,16,256]{3,2,1,0:T(8,128)} %bitcast.6, f32[16,80,128]{2,1,0:T(8,128)} %copy-done.1, bf16[2,2,160,512]{3,2,1,0:T(8,128)(2,1)} %shard_map.123.coef_ref, bf16[160,160]{1,0:T(8,128)(2,1)} %constant.68.clone.up_ref, ...), custom_call_target="tpu_custom_call" | custom-call | tf_op jit(solution)/shard_map/pallas_call | solution.py:376
  57.4 16.6 %all_to_all.10.back_ref = f32[16,40,128]{2,1,0:T(8,128)} all-to-all(f32[16,40,128]{2,1,0:T(8,128)} %get-tuple-element.20), channel_id=1, replica_groups=mesh['gx'=4,'gy'=4,'gz'=8] {'gx','gy'}, dimensions={0} | all-to-all | bytes 655360 | tf_op jit(solution)/shard_map/all_to_all | solution.py:453
  74.0 6.0 %shard_map.126 = f32[2560,128]{1,0:T(8,128)} custom-call(s32[32]{0:T(128)} %pad_add_fusion.place_ref, f32[2560,128]{1,0:T(8,128)} %get-tuple-element.18.new_ref, f32[16,40,128]{2,1,0:T(8,128)} %all_to_all.10.back_ref), custom_call_target="tpu_custom_call" | custom-call | tf_op jit(solution)/shard_map/pallas_call | solution.py:376
  (27 shorter events, 0.1 us)
Async XLA Ops:
  0.6 10.2 %copy-start = (s32[1024,3]{0,1:T(4,128)S(1)}, s32[1024,3]{0,1:T(4,128)}, u32[]{:S(2)}) copy-start(s32[1024,3]{0,1:T(4,128)} %param.15) | copy-start | bytes 36868
  0.6 10.4 %copy-start.8 = (f32[3,10,10]{2,0,1:T(4,128)S(1)}, f32[3,10,10]{2,0,1:T(4,128)}, u32[]{:S(2)}) copy-start(f32[3,10,10]{2,0,1:T(4,128)} %param.13) | copy-start | bytes 3604
  0.7 14.1 %copy-start.9 = (s32[1024]{0:T(1024)S(1)}, s32[1024]{0:T(1024)}, u32[]{:S(2)}) copy-start(s32[1024]{0:T(1024)} %param.14) | copy-start | bytes 12292
  3.5 11.4 %copy-start.10 = (f32[160,128]{1,0:T(8,128)S(1)}, f32[160,128]{1,0:T(8,128)}, u32[]{:S(2)}) copy-start(f32[160,128]{1,0:T(8,128)} %get-tuple-element.17) | copy-start | bytes 245764
  3.5 11.4 %collective-permute-start = (f32[160,128]{1,0:T(8,128)}, f32[160,128]{1,0:T(8,128)S(1)}, u32[]{:S(2)}, u32[]{:S(2)}) collective-permute-start(f32[160,128]{1,0:T(8,128)} %get-tuple-element.12), channel_id=1, source_target_pairs={{0,32},{32,64},{64,96},{96,0},{1,33},{33,65},{65,97},{97,1},{2,34}... | collective-permute-start | bytes 245768 | tf_op jit(solution)/shard_map/ppermute | solution.py:411
  5.4 11.8 %collective-permute-start.1 = (f32[160,128]{1,0:T(8,128)}, f32[160,128]{1,0:T(8,128)S(1)}, u32[]{:S(2)}, u32[]{:S(2)}) collective-permute-start(f32[160,128]{1,0:T(8,128)} %get-tuple-element.13), channel_id=1, source_target_pairs={{32,0},{64,32},{96,64},{0,96},{33,1},{65,33},{97,65},{1,97},{34,2}... | collective-permute-start | bytes 245768 | tf_op jit(solution)/shard_map/ppermute | solution.py:415
  7.6 9.6 %collective-permute-start.2 = (f32[160,128]{1,0:T(8,128)}, f32[160,128]{1,0:T(8,128)S(1)}, u32[]{:S(2)}, u32[]{:S(2)}) collective-permute-start(f32[160,128]{1,0:T(8,128)} %get-tuple-element.14), channel_id=1, source_target_pairs={{0,8},{8,16},{16,24},{24,0},{1,9},{9,17},{17,25},{25,1},{2,10},{10... | collective-permute-start | bytes 245768 | tf_op jit(solution)/shard_map/ppermute | solution.py:411
  9.1 8.1 %collective-permute-start.3 = (f32[160,128]{1,0:T(8,128)}, f32[160,128]{1,0:T(8,128)S(1)}, u32[]{:S(2)}, u32[]{:S(2)}) collective-permute-start(f32[160,128]{1,0:T(8,128)} %get-tuple-element.15), channel_id=1, source_target_pairs={{8,0},{16,8},{24,16},{0,24},{9,1},{17,9},{25,17},{1,25},{10,2},{18... | collective-permute-start | bytes 245768 | tf_op jit(solution)/shard_map/ppermute | solution.py:415
  10.8 6.4 %collective-permute-start.4 = (f32[160,128]{1,0:T(8,128)}, f32[160,128]{1,0:T(8,128)S(1)}, u32[]{:S(2)}, u32[]{:S(2)}) collective-permute-start(f32[160,128]{1,0:T(8,128)} %get-tuple-element.16), channel_id=1, source_target_pairs={{0,1},{1,2},{2,3},{3,4},{4,5},{5,6},{6,7},{7,0},{8,9},{9,10},{10,1... | collective-permute-start | bytes 245768 | tf_op jit(solution)/shard_map/ppermute | solution.py:411
  14.8 3.8 %copy-start.2 = (f32[160,128]{1,0:T(8,128)}, f32[160,128]{1,0:T(8,128)S(1)}, u32[]{:S(2)}) copy-start(f32[160,128]{1,0:T(8,128)S(1)} %collective-permute-done.x_lo) | copy-start | bytes 245764
  14.8 3.8 %collective-permute-start.5 = (f32[160,128]{1,0:T(8,128)S(1)}, f32[160,128]{1,0:T(8,128)S(1)}, u32[]{:S(2)}, u32[]{:S(2)}) collective-permute-start(f32[160,128]{1,0:T(8,128)S(1)} %copy-done.10), channel_id=1, source_target_pairs={{1,0},{2,1},{3,2},{4,3},{5,4},{6,5},{7,6},{0,7},{9,8},{10,9},{11,1... | collective-permute-start | bytes 245768 | tf_op jit(solution)/shard_map/ppermute | solution.py:415
  17.2 1.5 %copy-start.3 = (f32[160,128]{1,0:T(8,128)}, f32[160,128]{1,0:T(8,128)S(1)}, u32[]{:S(2)}) copy-start(f32[160,128]{1,0:T(8,128)S(1)} %collective-permute-done.1.x_hi) | copy-start | bytes 245764
  17.2 1.5 %copy-start.4 = (f32[160,128]{1,0:T(8,128)}, f32[160,128]{1,0:T(8,128)S(1)}, u32[]{:S(2)}) copy-start(f32[160,128]{1,0:T(8,128)S(1)} %collective-permute-done.2.y_lo) | copy-start | bytes 245764
  17.2 1.4 %copy-start.5 = (f32[160,128]{1,0:T(8,128)}, f32[160,128]{1,0:T(8,128)S(1)}, u32[]{:S(2)}) copy-start(f32[160,128]{1,0:T(8,128)S(1)} %collective-permute-done.3.y_hi) | copy-start | bytes 245764
  17.2 1.4 %copy-start.6 = (f32[160,128]{1,0:T(8,128)}, f32[160,128]{1,0:T(8,128)S(1)}, u32[]{:S(2)}) copy-start(f32[160,128]{1,0:T(8,128)S(1)} %collective-permute-done.4.z_lo) | copy-start | bytes 245764
  18.7 0.6 copy-start.7
  28.2 19.7 %all-to-all-start = ((f32[16,80,128]{2,1,0:T(8,128)}), f32[16,80,128]{2,1,0:T(8,128)S(1)}, u32[]{:S(2)}, u32[]{:S(2)}) async-start(f32[16,80,128]{2,1,0:T(8,128)} %get-tuple-element.19), calls=%async_computation | async-start | bytes 1310720 | tf_op jit(solution)/shard_map/all_to_all | solution.py:433
  47.9 0.8 %copy-start.1 = (f32[16,80,128]{2,1,0:T(8,128)}, f32[16,80,128]{2,1,0:T(8,128)S(1)}, u32[]{:S(2)}) copy-start(f32[16,80,128]{2,1,0:T(8,128)S(1)} %all-to-all-done.arrived_ref) | copy-start | bytes 1966084

commit v2 on v1

v2 whole, which is shorter than its diff:
```python
import functools

import jax
import jax.numpy as jnp
import ml_dtypes
import numpy as np
from jax import lax
from jax.experimental import pallas as pl
from jax.experimental.pallas import tpu as pltpu
from jax.sharding import PartitionSpec as P

F = 10
B = 16
BOXES = 8
H = 8
FSLOTS = 16
LINES = 8
GROUP = 16
ROWS = F * B
HALF = F * H
F32 = jnp.float32
BF16 = jnp.bfloat16
MIB = 1024 * 1024
PITCH = ROWS + 8
BATCH = 8


def dot(a, b):
    return jnp.dot(a, b, preferred_element_type=F32)


def split(v):
    hi = v.astype(BF16)
    return hi, (v - hi.astype(F32)).astype(BF16)


def lanes_of(shape):
    return lax.broadcasted_iota(jnp.int32, shape, len(shape) - 1)


CONST = {
    "ghost": (slice(0, 128), slice(0, 768)),
    "up": (slice(128, 288), slice(0, 160)),
    "pair": (slice(128, 208), slice(256, 576)),
    "face": (slice(288, 416), slice(0, 256)),
    "mean": (slice(128, 384), slice(640, 768)),
}


def fine_constants():
    up = np.zeros((ROWS, 2 * HALF), np.float32)
    pair = np.zeros((HALF, 2 * ROWS), np.float32)
    for f in range(F):
        for x in range(B):
            for part in range(2):
                up[f * B + x, part * HALF + f * H + x // 2] = 1
                pair[f * H + x // 2, part * ROWS + f * B + x] = 0.125
    ghost = np.zeros((128, 768), np.float32)
    face = np.zeros((128, 256), np.float32)
    mean = np.zeros((256, 128), np.float32)
    for part in range(2):
        for t in range(2):
            for j in range(B):
                low, col = part * 64 + t * 32 + j // 2, t * 384
                ghost[low, col + j] = 1
                ghost[low + 8, col + 112 + j] = 1
                ghost[low + 16, col + 128 + j * B] = 1
                ghost[low + 24, col + 128 + j * B + B - 1] = 1
        for y in range(B):
            for z in range(B):
                face[part * 64 + y // 2 * H + z // 2, y * B + z] = 1
                mean[y * B + z, y // 2 * H + z // 2] = 1
    every = np.zeros((416, 768), np.float32)
    for name, value in (("ghost", ghost), ("up", up), ("pair", pair), ("face", face), ("mean", mean)):
        rows, cols = CONST[name]
        every[rows, cols] = value
    return every.astype(ml_dtypes.bfloat16)


def device_index():
    return (lax.axis_index("gx") * lax.axis_size("gy") + lax.axis_index("gy")) * lax.axis_size("gz") + lax.axis_index("gz")


def box_place(owner_ref, offset_ref, w):
    box = device_index() * BOXES + w
    return (owner_ref[box] // (FSLOTS * LINES), *(offset_ref[d, box] for d in range(3)))


def coefficients(jac_ref, pad_ref, outs):
    pad_ref[...] = jnp.zeros(pad_ref.shape, F32)
    for d in range(3):
        for g in range(F):
            pad_ref[d, g : g + 1, 0:F] = jac_ref[g, d : d + 1, :]
    row, lane = (lax.broadcasted_iota(jnp.int32, (128, 128), d) for d in range(2))
    eye = jnp.where((row[:16] == lane[:16]) & (row[:16] < F), 0.125, 0.0).astype(F32)
    scaled = [0.125 * pad_ref[d] for d in range(3)]
    row, col = (lax.broadcasted_iota(jnp.int32, (128, 512), d) for d in range(2))
    block, inner = col // ROWS, col % ROWS // B
    ghost = 3 * ROWS
    target = jnp.where(col < ghost, inner + jnp.where(block == 0, 0, 16 + 16 * block), (col + 16) % 32)
    one = lambda cond: jnp.where(cond, 1.0, 0.0).astype(F32)
    first = one(row == target).astype(BF16)
    second = one((col < ROWS) & (row == 16 + inner)).astype(BF16)
    row, col = (lax.broadcasted_iota(jnp.int32, (ROWS, 512), d) for d in range(2))
    here, there = row % B, col % B
    edge = jnp.where(col < ghost + 16, 0, B - 1)
    distance = jnp.where(col < ROWS, there - here - 1, jnp.where(col < ghost, there - here, here - edge))
    mask_first = one(distance == 0)
    mask_second = one((col < ROWS) & (there + 1 == here))
    row, col = (lax.broadcasted_iota(jnp.int32, (ROWS, 128), d) for d in range(2))
    rows = one(row // B == col).astype(BF16)
    pad = jnp.zeros((112, 512), BF16)
    for (s, a, b), out in zip(((1, 0, 2), (0, 1, 2)), outs):
        coef = (
            (eye - scaled[s])
            + pltpu.roll(eye + scaled[s], 16, 1)
            - pltpu.roll(scaled[a], 32, 1)
            - pltpu.roll(scaled[b], 48, 1)
        )
        for part, value in enumerate(split(coef)):
            wide1 = jnp.concatenate([dot(value, first).astype(BF16), pad], axis=0)
            wide2 = jnp.concatenate([dot(value, second).astype(BF16), pad], axis=0)
            out[part] = (dot(rows, wide1) * mask_first + dot(rows, wide2) * mask_second).astype(BF16)


def faces_kernel(coarse_ref, x_lo, x_hi, y_lo, y_hi, z_lo, z_hi):
    x_lo[...] = coarse_ref[0:ROWS, :]
    x_hi[...] = coarse_ref[(B - 1) * ROWS : B * ROWS, :]
    for x in range(B):
        y_lo[x * F : x * F + F, :] = coarse_ref[pl.ds(x * ROWS, F, stride=B), :]
        y_hi[x * F : x * F + F, :] = coarse_ref[pl.ds(x * ROWS + B - 1, F, stride=B), :]
    lane = lanes_of((ROWS, 128))
    low = jnp.zeros((ROWS, 128), F32)
    high = jnp.zeros((ROWS, 128), F32)
    for x in range(B):
        plane = coarse_ref[x * ROWS : (x + 1) * ROWS, :]
        low = jnp.where(lane == x, pltpu.roll(plane, x, 1), low)
        high = jnp.where(lane == x, pltpu.roll(plane, x + 1, 1), high)
    z_lo[...] = low
    z_hi[...] = high


def product(coef_ref, hi_ref, lo_ref, total_ref):
    both = dot(coef_ref[...].reshape(2 * ROWS, 512), hi_ref[...])
    total_ref[...] = both[:ROWS] + both[ROWS:] + dot(coef_ref[0], lo_ref[...])


def put_parts(hi_ref, lo_ref, cols, parts):
    for at, value in parts:
        hi, lo = split(value)
        hi_ref[at : at + value.shape[0], cols] = hi
        lo_ref[at : at + value.shape[0], cols] = lo


def coarse_kernel(
    owner_ref, offset_ref, coarse_ref, x_lo, x_hi, y_lo, y_hi, z_lo, z_hi, jac_ref, new_ref, out_ref, fine_coef_ref, old_ref,
    mid_ref, hi_ref, lo_ref, rest_ref, total_ref, coef_ref, pad_ref
):
    coefficients(jac_ref, pad_ref, (coef_ref, fine_coef_ref))
    lane = lanes_of((B, 128))
    ghost_zero = jnp.zeros((16 - F, 128), F32)
    for pair in range(B // 2):
        for side in range(2):
            x = 2 * pair + side
            cols = slice(side * 128, side * 128 + 128)
            for f in range(F):
                row = slice(f * B, f * B + B)
                here = x * ROWS + f * B
                p = coarse_ref[here : here + B, :]
                xm = coarse_ref[here - ROWS : here - ROWS + B, :] if x > 0 else x_lo[row, :]
                xp = coarse_ref[here + ROWS : here + ROWS + B, :] if x < B - 1 else x_hi[row, :]
                zm = jnp.where(lane == 0, pltpu.roll(z_lo[row, :], (128 - x) % 128, 1), pltpu.roll(p, 1, 1))
                zp = jnp.where(lane == 127, pltpu.roll(z_hi[row, :], 127 - x, 1), pltpu.roll(p, 127, 1))
                put_parts(
                    hi_ref.at[pair],
                    lo_ref.at[pair],
                    cols,
                    ((f * B, p), (ROWS + f * B, xp - xm), (2 * ROWS + f * B, zp - zm)),
                )
                rest_ref[pair, row, cols] = 0.25 * p + 0.125 * ((xp + xm) + (zp + zm))
                old_ref[x * PITCH + f * B : x * PITCH + f * B + B, :] = p
            low = jnp.concatenate([y_lo[x * F : x * F + F, :], ghost_zero], axis=0)
            high = jnp.concatenate([y_hi[x * F : x * F + F, :], ghost_zero], axis=0)
            put_parts(hi_ref.at[pair], lo_ref.at[pair], cols, ((3 * ROWS, low), (3 * ROWS + 16, high)))
    for pair in range(B // 2):
        product(coef_ref, hi_ref.at[pair], lo_ref.at[pair], total_ref.at[pair])
    for pair in range(B // 2):
        for side in range(2):
            x = 2 * pair + side
            cols = slice(side * 128, side * 128 + 128)
            for f in range(F):
                row = slice(f * B, f * B + B)
                here = slice(x * ROWS + f * B, x * ROWS + f * B + B)
                new = rest_ref[pair, row, cols] + total_ref[pair, row, cols]
                new_ref[here, :] = new
                mid_ref[x * PITCH + f * B : x * PITCH + f * B + B, :] = 0.5 * (coarse_ref[here, :] + new)

    lane8 = lanes_of((8, 128))
    within = lane8 % 32
    base = jnp.where(within < 16, within % 8, jnp.where(within < 24, -1, 8))
    window = lane8 % 8

    def box(w, _):
        member, ox, oy, oz = box_place(owner_ref, offset_ref, w)
        z0 = w * B + oz
        pick = base + z0
        pick_x = window + z0
        corner = ox * PITCH + oy - 1
        for f in range(F):
            acc = jnp.zeros((8, 128), F32)
            for t, ref in enumerate((old_ref, mid_ref)):
                for y in range(H + 2):
                    rows = ref[pl.ds(corner + f * B + y, H, stride=PITCH), :]
                    moved = jnp.take_along_axis(rows, pick, axis=1, mode="promise_in_bounds")
                    if y == 0:
                        put = (lane8 >= 32 * t) & (lane8 < 32 * t + 8)
                    elif y == H + 1:
                        put = (lane8 >= 32 * t + 8) & (lane8 < 32 * t + 16)
                    else:
                        put = (lane8 == 32 * t + 15 + y) | (lane8 == 32 * t + 23 + y)
                    acc = jnp.where(put, moved, acc)
            out_ref[member, f * 8 : f * 8 + 8, :] = acc
        for t, ref in enumerate((old_ref, mid_ref)):
            for side, x in enumerate((ox - 1, ox + H)):
                first = jnp.zeros((8, 128), F32)
                second = jnp.zeros((8, 128), F32)
                for y in range(H):
                    put = (lane8 >= 64 + y * 8) & (lane8 < 72 + y * 8)
                    at = x * PITCH + oy + y
                    rows = ref[pl.ds(at, 8, stride=B), :]
                    first = jnp.where(put, jnp.take_along_axis(rows, pick_x, axis=1, mode="promise_in_bounds"), first)
                    tail = jnp.concatenate(
                        [ref[pl.ds(at + 8 * B, F - 8, stride=B), :], jnp.zeros((16 - F, 128), F32)], axis=0
                    )
                    second = jnp.where(
                        put, jnp.take_along_axis(tail, pick_x, axis=1, mode="promise_in_bounds"), second
                    )
                at = (2 * t + side) * 16
                old = out_ref[member, at : at + 16, :]
                out_ref[member, at : at + 16, :] = jnp.where(
                    lanes_of((16, 128)) < 64, old, jnp.concatenate([first, second], axis=0)
                )
        return 0

    lax.fori_loop(0, BOXES, box, 0, unroll=2)


def fine_kernel(
    owner_ref, fine_ref, arrived_ref, coef_ref, const_ref, out_ref, back_ref, hi_ref, lo_ref, wide_ref, rest_ref, total_ref, value_ref, face_out_ref, parts_ref, mixed_ref, back_scratch, source_ref
):
    for slot in range(FSLOTS):
        source_ref[slot] = -1
    device = device_index()
    line = lax.axis_index("gz")
    for member in range(GROUP):
        for w in range(BOXES):
            holder = owner_ref[(member * LINES + line) * BOXES + w]
            source_ref[jnp.where(holder // FSLOTS == device, holder % FSLOTS, FSLOTS)] = member
    held = sum(jnp.where(source_ref[slot] >= 0, 1, 0) for slot in range(FSLOTS))
    batches = (held + BATCH - 1) // BATCH
    constant = {name: const_ref.at[at] for name, at in CONST.items()}

    def batch(i, _):
        first_slot = i * BATCH
        sources = [source_ref[first_slot + k] for k in range(BATCH)]
        lane = lanes_of((B, 128))
        column = lane % B
        for k in range(BATCH):
            message = arrived_ref.at[jnp.maximum(sources[k], 0)]
            for at in range(0, HALF, 16):
                value = message[at : at + 16, :]
                hi, lo = split(value)
                parts_ref[k, at : at + 16, :] = hi
                parts_ref[k, HALF + at : HALF + at + 16, :] = lo
                if at < 64:
                    hi = hi.astype(F32)
                    mixed_ref[k, ROWS + at : ROWS + at + 16, :] = jnp.where(
                        lane < 64, pltpu.roll(value - hi, 64, 1), hi
                    ).astype(BF16)
        for k in range(BATCH):
            lifted = dot(constant["up"][...], parts_ref[k])
            for f in range(F):
                value = lifted[f * B : f * B + B]
                hi = value.astype(BF16).astype(F32)
                mixed_ref[k, f * B : f * B + B, :] = jnp.where(lane < 64, hi, pltpu.roll(value - hi, 64, 1)).astype(
                    BF16
                )
        for k in range(BATCH):
            wide_ref[k] = dot(mixed_ref[k, 0:ROWS, :], constant["ghost"][...])
            face_out_ref[k] = dot(mixed_ref[k, ROWS : ROWS + 64, :], constant["face"][...])
        for t in range(2):
            at = 384 * t
            for k in range(BATCH):
                for f in range(F):
                    row = slice(f * B, f * B + B)
                    if t == 0:
                        a, b = fine_ref[first_slot + k, f, :, 0:128], fine_ref[first_slot + k, f, :, 128:256]
                    else:
                        a, b = value_ref[k, row, 0:128], value_ref[k, row, 128:256]
                    gy = wide_ref[k, row, at : at + 128]
                    gz_a = wide_ref[k, row, at + 128 : at + 256]
                    gz_b = wide_ref[k, row, at + 256 : at + 384]
                    a_up, b_up = pltpu.roll(a, 112, 1), pltpu.roll(b, 112, 1)
                    a_down, b_down = pltpu.roll(a, 16, 1), pltpu.roll(b, 16, 1)
                    yp = (jnp.where(lane < 112, a_up, b_up), jnp.where(lane < 112, b_up, gy))
                    ym = (jnp.where(lane < 16, gy, a_down), jnp.where(lane < 16, a_down, b_down))
                    zp = (
                        jnp.where(column == B - 1, gz_a, pltpu.roll(a, 127, 1)),
                        jnp.where(column == B - 1, gz_b, pltpu.roll(b, 127, 1)),
                    )
                    zm = (
                        jnp.where(column == 0, gz_a, pltpu.roll(a, 1, 1)),
                        jnp.where(column == 0, gz_b, pltpu.roll(b, 1, 1)),
                    )
                    for h, v in enumerate((a, b)):
                        cols = slice(128 * h, 128 * h + 128)
                        put_parts(
                            hi_ref.at[k],
                            lo_ref.at[k],
                            cols,
                            ((f * B, v), (ROWS + f * B, yp[h] - ym[h]), (2 * ROWS + f * B, zp[h] - zm[h])),
                        )
                        rest_ref[k, row, cols] = 0.25 * v + 0.125 * ((yp[h] + ym[h]) + (zp[h] + zm[h]))
                put_parts(
                    hi_ref.at[k], lo_ref.at[k], slice(None), ((3 * ROWS, face_out_ref[k, 32 * t : 32 * t + 32, :]),)
                )
            for k in range(BATCH):
                product(coef_ref, hi_ref.at[k], lo_ref.at[k], total_ref.at[k])
            for k in range(BATCH):
                for f in range(F):
                    row = slice(f * B, f * B + B)
                    value = rest_ref[k, row, :] + total_ref[k, row, :]
                    if t == 0:
                        value_ref[k, row, :] = value
                    else:
                        out_ref[first_slot + k, f] = jnp.where(sources[k] >= 0, value, 0.0)
                        hi, lo = split(value)
                        hi_ref[k, row, :] = hi
                        hi_ref[k, ROWS + f * B : ROWS + f * B + B, :] = lo
        for k in range(BATCH):
            paired = dot(constant["pair"][...], hi_ref[k, 0 : 2 * ROWS, :])
            hi, lo = split(paired)
            means = dot(hi, constant["mean"][...]) + dot(lo, constant["mean"][...])
            back_scratch[k] = jnp.where(
                lanes_of((HALF // 2, 128)) < 64, means[: HALF // 2], pltpu.roll(means[HALF // 2 :], 64, 1)
            )

        for k in range(BATCH):

            @pl.when(sources[k] >= 0)
            def _():
                back_ref[sources[k]] = back_scratch[k]

        return 0

    lax.fori_loop(0, batches, batch, 0)

    def empty(i, _):
        for k in range(BATCH):
            out_ref[i * BATCH + k] = jnp.zeros(out_ref.shape[1:], F32)
        return 0

    lax.fori_loop(batches, FSLOTS // BATCH, empty, 0)


def place_kernel(owner_ref, offset_ref, new_ref, back_ref, out_ref, work_ref, sems):
    for x in range(B):
        work_ref[x * PITCH : x * PITCH + ROWS, :] = new_ref[x * ROWS : (x + 1) * ROWS, :]
    lane = lanes_of((8, 128))

    def box(w, _):
        member, ox, oy, oz = box_place(owner_ref, offset_ref, w)
        z0 = w * B + oz
        inside = (lane >= z0) & (lane < z0 + H)
        pick = jnp.where(inside, lane - z0, 0)
        corner = ox * PITCH + oy
        for f in range(F):
            tile = back_ref[member, f % 5 * 8 : f % 5 * 8 + 8, :]
            rows = [pl.ds(corner + f * B + y, H, stride=PITCH) for y in range(H)]
            before = [work_ref[r, :] for r in rows]
            for y in range(H):
                moved = jnp.take_along_axis(tile, pick + (f // 5 * 64 + y * 8), axis=1, mode="promise_in_bounds")
                work_ref[rows[y], :] = jnp.where(inside, moved, before[y])
        return 0

    lax.fori_loop(0, BOXES, box, 0)
    copies = [
        pltpu.make_async_copy(
            work_ref.at[x * PITCH : x * PITCH + ROWS, :], out_ref.at[x * ROWS : (x + 1) * ROWS, :], sems.at[x]
        )
        for x in range(B)
    ]
    for copy in copies:
        copy.start()
    for copy in copies:
        copy.wait()


def call(kernel, operands, outs, limit, scratch=(), out_space=pltpu.VMEM):
    spaces = [pltpu.SMEM if a.dtype == jnp.int32 else pltpu.VMEM for a in operands]
    return pl.pallas_call(
        kernel,
        in_specs=[pl.BlockSpec(memory_space=space) for space in spaces],
        out_specs=[pl.BlockSpec(memory_space=out_space) for _ in outs],
        out_shape=[jax.ShapeDtypeStruct(*out) for out in outs],
        scratch_shapes=list(scratch),
        compiler_params=pltpu.CompilerParams(vmem_limit_bytes=limit * MIB),
    )(*operands)


def local(coarse_state, fine_state, flux_jacobians, fine_owner, fine_offset):
    rows = coarse_state.reshape(B * ROWS, 128)
    fine_rows = jnp.transpose(fine_state, (0, 2, 1, 3))
    offset = jnp.transpose(fine_offset, (1, 0))
    jacobians = jnp.transpose(flux_jacobians, (1, 0, 2))

    face = ((ROWS, 128), F32)
    x_first, x_last, y_first, y_last, z_first, z_last = call(faces_kernel, (rows,), [face] * 6, 4)

    def from_below(value, axis):
        n = lax.axis_size(axis)
        return lax.ppermute(value, axis, [(i, (i + 1) % n) for i in range(n)])

    def from_above(value, axis):
        n = lax.axis_size(axis)
        return lax.ppermute(value, axis, [((i + 1) % n, i) for i in range(n)])

    halo = (
        from_below(x_last, "gx"),
        from_above(x_first, "gx"),
        from_below(y_last, "gy"),
        from_above(y_first, "gy"),
        from_below(z_last, "gz"),
        from_above(z_first, "gz"),
    )
    new, outgoing, coef = call(
        coarse_kernel,
        (fine_owner, offset, rows, *halo, jacobians),
        [((B * ROWS, 128), F32), ((GROUP, HALF, 128), F32), ((2, ROWS, 512), BF16)],
        14,
        [pltpu.VMEM((B * PITCH, 128), F32)] * 2
        + [pltpu.VMEM((B // 2, 512, 256), BF16)] * 2
        + [pltpu.VMEM((B // 2, ROWS, 256), F32)] * 2
        + [pltpu.VMEM((2, ROWS, 512), BF16), pltpu.VMEM((3, 16, 128), F32)],
    )
    arrived = lax.all_to_all(outgoing, ("gx", "gy"), split_axis=0, concat_axis=0, tiled=True)

    fine_new, returning = call(
        fine_kernel,
        (fine_owner, fine_rows, arrived, coef, fine_constants()),
        [((FSLOTS, F, B, 256), F32), ((GROUP, HALF // 2, 128), F32)],
        20,
        [pltpu.VMEM((BATCH, 512, 256), BF16)] * 2
        + [pltpu.VMEM((BATCH, ROWS, 768), F32)]
        + [pltpu.VMEM((BATCH, ROWS, 256), F32)] * 3
        + [
            pltpu.VMEM((BATCH, 64, 256), F32),
            pltpu.VMEM((BATCH, 2 * HALF, 128), BF16),
            pltpu.VMEM((BATCH, ROWS + 64, 128), BF16),
            pltpu.VMEM((BATCH, HALF // 2, 128), F32),
            pltpu.SMEM((FSLOTS + 1,), jnp.int32),
        ],
    )
    came_back = lax.all_to_all(returning, ("gx", "gy"), split_axis=0, concat_axis=0, tiled=True)

    coarse_out = call(
        place_kernel,
        (fine_owner, offset, new, came_back),
        [((B * ROWS, 128), F32)],
        4,
        [pltpu.VMEM((B * PITCH, 128), F32), pltpu.SemaphoreType.DMA((B,))],
        pl.ANY,
    )[0]
    return coarse_out.reshape(coarse_state.shape), jnp.transpose(fine_new, (0, 2, 1, 3))


def solution(mesh):
    in_specs = (P("gx", None, "gy", "gz"), P(("gx", "gy", "gz"), None, None, None), P(), P(), P())
    out_specs = (P("gx", None, "gy", "gz"), P(("gx", "gy", "gz"), None, None, None))
    return jax.shard_map(local, mesh=mesh, in_specs=in_specs, out_specs=out_specs, check_vma=False)
```

time: 81.1 us -> 72.8 us (0.90)
  blocking collectives: 16.6 us -> 36.3 us
  waiting for transfers between devices: 15.6 us -> 2.12 us
  Pallas kernels: 29.4 us -> 19.7 us
  starting transfers between devices: 13.9 us -> 9.17 us
  local copies, waits for them, and re-layouts: 2.34 us -> 3.85 us
  other arithmetic: 1.45 us -> 0 us
    all_to_all x0 -> x1, blocking collectives: none -> 19.2 us  [local(): lax.all_to_all(outgoing, ('gx', 'gy'), split_axis=0, concat_axis=0, tiled...]
    all_to_all x1 -> x0, waiting for transfers between devices: 14.1 us -> none  [local(): lax.all_to_all(outgoing, ('gx', 'gy'), split_axis=0, concat_axis=0, tiled...]
    pallas_call x5 -> x4, Pallas kernels: 29.4 us -> 19.7 us  [call(): pl.pallas_call(kernel, in_specs=[pl.BlockSpec(memory_space=space) for spa...]
    all_to_all x1 -> x0, starting transfers between devices: 4.77 us -> none  [local(): lax.all_to_all(outgoing, ('gx', 'gy'), split_axis=0, concat_axis=0, tiled...]
    unnamed x23 -> x16, local copies, waits for them, and re-layouts: 2.1 us -> 3.85 us
    ppermute x3, waiting for transfers between devices: 0.01 us -> 1.75 us  [from_below(): return lax.ppermute(value, axis, [(i, (i + 1) % n) for i in range(n)])]
    ppermute x3, waiting for transfers between devices: 1.41 us -> 0.37 us  [from_above(): return lax.ppermute(value, axis, [((i + 1) % n, i) for i in range(n)])]
  transfers between devices with their start and end apart: 7 -> 6, of which waited for: 2 -> 3; matrix products, arithmetic and copies ran while one was open for 3% -> 0% of each run, Pallas kernels for 4% -> 0%
where the time goes in v2:
time: 72.8 us; the launch traced here: 71.9 us
  blocking collectives  36.3 us (50%)
  Pallas kernels  19.7 us (27%)
  starting transfers between devices  9.17 us (13%)
  local copies, waits for them, and re-layouts  3.85 us (5%)
  waiting for transfers between devices  2.12 us (3%)
    pallas_call x4, Pallas kernels, call(): pl.pallas_call(kernel, in_specs=[pl.BlockSpec(memory_space=space) for spa...  19.7 us
    all_to_all x1, blocking collectives, local(): lax.all_to_all(outgoing, ('gx', 'gy'), split_axis=0, concat_axis=0, tiled...  19.2 us
    all_to_all x1, blocking collectives, local(): lax.all_to_all(returning, ('gx', 'gy'), split_axis=0, concat_axis=0, tile...  17.2 us
    ppermute x3, starting transfers between devices, from_above(): return lax.ppermute(value, axis, [((i + 1) % n, i) for i in range(n)])  5.61 us
    unnamed x16, local copies, waits for them, and re-layouts  3.85 us
    ppermute x3, starting transfers between devices, from_below(): return lax.ppermute(value, axis, [(i, (i + 1) % n) for i in range(n)])  3.56 us
    ppermute x3, waiting for transfers between devices, from_below(): return lax.ppermute(value, axis, [(i, (i + 1) % n) for i in range(n)])  1.75 us
  transfers between devices with their start and end apart: 6, of which 3 were waited for; matrix products, arithmetic and copies ran while one was open for 0% of the time, Pallas kernels for 0%

profile of v2, /device:TPU:4, one launch (start us, length us, event | category | flops | bytes accessed | tf_op | source)
XLA Modules:
  0.0 71.9 jit_solution(7961841097575631956)
XLA Ops:
  0.6 0.0 copy-start
  0.6 1.3 %copy-done = f32[16,10,16,128]{3,2,1,0:T(8,128)S(1)} copy-done((f32[16,10,16,128]{3,2,1,0:T(8,128)S(1)}, f32[16,10,16,128]{3,2,1,0:T(8,128)}, u32[]{:S(2)}) %copy-start) | copy-done | bytes 1310744
  2.0 0.8 %shard_map.77 = (f32[160,128]{1,0:T(8,128)S(1)}, f32[160,128]{1,0:T(8,128)S(1)}, f32[160,128]{1,0:T(8,128)S(1)}, f32[160,128]{1,0:T(8,128)S(1)}, f32[160,128]{1,0:T(8,128)S(1)}, /*index=5*/f32[160,128]{1,0:T(8,128)S(1)}) custom-call(f32[2560,128]{1,0:T(8,128)S(1)} %bitcast.6), custom_call_target="tpu_custom_call" | custom-call | tf_op jit(solution)/shard_map/pallas_call | solution.py:401
  2.7 2.0 %collective-permute-start = (f32[160,128]{1,0:T(8,128)S(1)}, f32[160,128]{1,0:T(8,128)S(1)}, u32[]{:S(2)}, u32[]{:S(2)}) collective-permute-start(f32[160,128]{1,0:T(8,128)S(1)} %get-tuple-element.13), channel_id=1, source_target_pairs={{0,32},{32,64},{64,96},{96,0},{1,33},{33,65},{65,97},{97,1},{2,34}... | collective-permute-start | bytes 245768 | tf_op jit(solution)/shard_map/ppermute | solution.py:422
  4.7 2.2 %collective-permute-start.1 = (f32[160,128]{1,0:T(8,128)S(1)}, f32[160,128]{1,0:T(8,128)S(1)}, u32[]{:S(2)}, u32[]{:S(2)}) collective-permute-start(f32[160,128]{1,0:T(8,128)S(1)} %get-tuple-element.14), channel_id=1, source_target_pairs={{32,0},{64,32},{96,64},{0,96},{33,1},{65,33},{97,65},{1,97},{34,2}... | collective-permute-start | bytes 245768 | tf_op jit(solution)/shard_map/ppermute | solution.py:426
  6.9 1.6 %collective-permute-start.2 = (f32[160,128]{1,0:T(8,128)S(1)}, f32[160,128]{1,0:T(8,128)S(1)}, u32[]{:S(2)}, u32[]{:S(2)}) collective-permute-start(f32[160,128]{1,0:T(8,128)S(1)} %get-tuple-element.15), channel_id=1, source_target_pairs={{0,8},{8,16},{16,24},{24,0},{1,9},{9,17},{17,25},{25,1},{2,10},{10... | collective-permute-start | bytes 245768 | tf_op jit(solution)/shard_map/ppermute | solution.py:422
  8.5 1.7 %collective-permute-start.3 = (f32[160,128]{1,0:T(8,128)S(1)}, f32[160,128]{1,0:T(8,128)S(1)}, u32[]{:S(2)}, u32[]{:S(2)}) collective-permute-start(f32[160,128]{1,0:T(8,128)S(1)} %get-tuple-element.16), channel_id=1, source_target_pairs={{8,0},{16,8},{24,16},{0,24},{9,1},{17,9},{25,17},{1,25},{10,2},{18... | collective-permute-start | bytes 245768 | tf_op jit(solution)/shard_map/ppermute | solution.py:426
  10.1 0.0 collective-permute-start.4
  10.1 0.0 collective-permute-done.x_lo
  10.1 1.7 %collective-permute-start.5 = (f32[160,128]{1,0:T(8,128)S(1)}, f32[160,128]{1,0:T(8,128)S(1)}, u32[]{:S(2)}, u32[]{:S(2)}) collective-permute-start(f32[160,128]{1,0:T(8,128)S(1)} %get-tuple-element.18), channel_id=1, source_target_pairs={{1,0},{2,1},{3,2},{4,3},{5,4},{6,5},{7,6},{0,7},{9,8},{10,9},{11,1... | collective-permute-start | bytes 245768 | tf_op jit(solution)/shard_map/ppermute | solution.py:426
  11.9 0.0 collective-permute-done.1.x_hi
  11.9 0.7 collective-permute-done.2.y_lo
  12.6 0.4 collective-permute-done.3.y_hi
  12.9 1.1 %collective-permute-done.4.z_lo = f32[160,128]{1,0:T(8,128)S(1)} collective-permute-done((f32[160,128]{1,0:T(8,128)S(1)}, f32[160,128]{1,0:T(8,128)S(1)}, u32[]{:S(2)}, u32[]{:S(2)}) %collective-permute-start.4) | collective-permute-done | bytes 81952 | tf_op jit(solution)/shard_map/ppermute | solution.py:422
  14.0 0.0 collective-permute-done.5.z_hi
  14.0 0.0 copy-start.4
  14.0 0.7 copy-done.4
  14.7 0.7 %copy-done.7 = f32[3,10,10]{2,0,1:T(4,128)S(1)} copy-done((f32[3,10,10]{2,0,1:T(4,128)S(1)}, f32[3,10,10]{2,0,1:T(4,128)}, u32[]{:S(2)}) %copy-start.7) | copy-done | bytes 1224
  15.5 5.8 %shard_map.78 = (f32[2560,128]{1,0:T(8,128)S(1)}, f32[16,80,128]{2,1,0:T(8,128)S(1)}, bf16[2,160,512]{2,1,0:T(8,128)(2,1)S(1)}) custom-call(s32[1024]{0:T(1024)S(1)} %copy-done.6, s32[3,1024]{1,0:T(4,128)S(1)} %bitcast.9, f32[2560,128]{1,0:T(8,128)S(1)} %bitcast.7, f32[160,128]{1,0:T(8,128)S(1)} %collective-permute-done.x_lo, ...), custom_call_target="tpu_custom_call" | custom-call | tf_op jit(solution)/shard_map/pallas_call | solution.py:401
  21.3 19.2 %all_to_all.10.arrived_ref = f32[16,80,128]{2,1,0:T(8,128)S(1)} all-to-all(f32[16,80,128]{2,1,0:T(8,128)S(1)} %get-tuple-element.20), channel_id=1, replica_groups=mesh['gx'=4,'gy'=4,'gz'=8] {'gx','gy'}, dimensions={0} | all-to-all | bytes 1310720 | tf_op jit(solution)/shard_map/all_to_all | solution.py:446
  40.5 1.1 %copy-done.3 = bf16[416,768]{1,0:T(8,128)(2,1)S(1)} copy-done((bf16[416,768]{1,0:T(8,128)(2,1)S(1)}, bf16[416,768]{1,0:T(8,128)(2,1)}, u32[]{:S(2)}) %copy-start.3) | copy-done | bytes 639000
  41.6 8.6 %shard_map.79 = (f32[16,10,16,256]{3,2,1,0:T(8,128)}, f32[16,40,128]{2,1,0:T(8,128)S(1)}) custom-call(s32[1024]{0:T(1024)S(1)} %copy-done.6, f32[16,10,16,256]{3,2,1,0:T(8,128)S(1)} %bitcast.8, f32[16,80,128]{2,1,0:T(8,128)S(1)} %all_to_all.10.arrived_ref, bf16[2,160,512]{2,1,0:T(8,128)(2,1)S(1)} %get-tuple-element.21.coef_ref, bf16[416,768]{1,0:T(8,128)(2,1)S(1)} %copy-done.3), custom_call_target="tpu_custom_call" | custom-call | tf_op jit(solution)/shard_map/pallas_call | solution.py:401
  50.2 17.2 %all_to_all.11.back_ref = f32[16,40,128]{2,1,0:T(8,128)S(1)} all-to-all(f32[16,40,128]{2,1,0:T(8,128)S(1)} %get-tuple-element.22), channel_id=1, replica_groups=mesh['gx'=4,'gy'=4,'gz'=8] {'gx','gy'}, dimensions={0} | all-to-all | bytes 655360 | tf_op jit(solution)/shard_map/all_to_all | solution.py:464
  67.3 4.5 %shard_map.80 = f32[2560,128]{1,0:T(8,128)} custom-call(s32[1024]{0:T(1024)S(1)} %copy-done.6, s32[3,1024]{1,0:T(4,128)S(1)} %bitcast.10, f32[2560,128]{1,0:T(8,128)S(1)} %get-tuple-element.19.new_ref, f32[16,40,128]{2,1,0:T(8,128)S(1)} %all_to_all.11.back_ref), custom_call_target="tpu_custom_call" | custom-call | tf_op jit(solution)/shard_map/pallas_call | solution.py:401
  (10 shorter events, 0.0 us)
Async XLA Ops:
  0.6 1.3 %copy-start = (f32[16,10,16,128]{3,2,1,0:T(8,128)S(1)}, f32[16,10,16,128]{3,2,1,0:T(8,128)}, u32[]{:S(2)}) copy-start(f32[16,10,16,128]{3,2,1,0:T(8,128)} %param.6) | copy-start | bytes 3932164
  1.9 12.1 %copy-start.1 = (f32[16,10,16,128]{3,2,1,0:T(8,128)S(1)}, f32[16,10,16,128]{3,2,1,0:T(8,128)}, u32[]{:S(2)}) copy-start(f32[16,10,16,128]{3,2,1,0:T(8,128)} %param.6) | copy-start | bytes 3932164
  1.9 12.1 %copy-start.6 = (s32[1024]{0:T(1024)S(1)}, s32[1024]{0:T(1024)}, u32[]{:S(2)}) copy-start(s32[1024]{0:T(1024)} %owner_ref.5) | copy-start | bytes 12292
  2.7 7.4 %collective-permute-start = (f32[160,128]{1,0:T(8,128)S(1)}, f32[160,128]{1,0:T(8,128)S(1)}, u32[]{:S(2)}, u32[]{:S(2)}) collective-permute-start(f32[160,128]{1,0:T(8,128)S(1)} %get-tuple-element.13), channel_id=1, source_target_pairs={{0,32},{32,64},{64,96},{96,0},{1,33},{33,65},{65,97},{97,1},{2,34}... | collective-permute-start | bytes 245768 | tf_op jit(solution)/shard_map/ppermute | solution.py:422
  4.7 7.2 %collective-permute-start.1 = (f32[160,128]{1,0:T(8,128)S(1)}, f32[160,128]{1,0:T(8,128)S(1)}, u32[]{:S(2)}, u32[]{:S(2)}) collective-permute-start(f32[160,128]{1,0:T(8,128)S(1)} %get-tuple-element.14), channel_id=1, source_target_pairs={{32,0},{64,32},{96,64},{0,96},{33,1},{65,33},{97,65},{1,97},{34,2}... | collective-permute-start | bytes 245768 | tf_op jit(solution)/shard_map/ppermute | solution.py:426
  6.9 5.7 %collective-permute-start.2 = (f32[160,128]{1,0:T(8,128)S(1)}, f32[160,128]{1,0:T(8,128)S(1)}, u32[]{:S(2)}, u32[]{:S(2)}) collective-permute-start(f32[160,128]{1,0:T(8,128)S(1)} %get-tuple-element.15), channel_id=1, source_target_pairs={{0,8},{8,16},{16,24},{24,0},{1,9},{9,17},{17,25},{25,1},{2,10},{10... | collective-permute-start | bytes 245768 | tf_op jit(solution)/shard_map/ppermute | solution.py:422
  8.5 4.4 %collective-permute-start.3 = (f32[160,128]{1,0:T(8,128)S(1)}, f32[160,128]{1,0:T(8,128)S(1)}, u32[]{:S(2)}, u32[]{:S(2)}) collective-permute-start(f32[160,128]{1,0:T(8,128)S(1)} %get-tuple-element.16), channel_id=1, source_target_pairs={{8,0},{16,8},{24,16},{0,24},{9,1},{17,9},{25,17},{1,25},{10,2},{18... | collective-permute-start | bytes 245768 | tf_op jit(solution)/shard_map/ppermute | solution.py:426
  10.1 3.9 %collective-permute-start.4 = (f32[160,128]{1,0:T(8,128)S(1)}, f32[160,128]{1,0:T(8,128)S(1)}, u32[]{:S(2)}, u32[]{:S(2)}) collective-permute-start(f32[160,128]{1,0:T(8,128)S(1)} %get-tuple-element.17), channel_id=1, source_target_pairs={{0,1},{1,2},{2,3},{3,4},{4,5},{5,6},{6,7},{7,0},{8,9},{9,10},{10,1... | collective-permute-start | bytes 245768 | tf_op jit(solution)/shard_map/ppermute | solution.py:422
  10.1 3.9 %collective-permute-start.5 = (f32[160,128]{1,0:T(8,128)S(1)}, f32[160,128]{1,0:T(8,128)S(1)}, u32[]{:S(2)}, u32[]{:S(2)}) collective-permute-start(f32[160,128]{1,0:T(8,128)S(1)} %get-tuple-element.18), channel_id=1, source_target_pairs={{1,0},{2,1},{3,2},{4,3},{5,4},{6,5},{7,6},{0,7},{9,8},{10,9},{11,1... | collective-permute-start | bytes 245768 | tf_op jit(solution)/shard_map/ppermute | solution.py:426
  14.0 0.7 %copy-start.4 = (s32[1024,3]{0,1:T(4,128)S(1)}, s32[1024,3]{0,1:T(4,128)}, u32[]{:S(2)}) copy-start(s32[1024,3]{0,1:T(4,128)} %param.10) | copy-start | bytes 36868
  14.7 0.7 %copy-start.7 = (f32[3,10,10]{2,0,1:T(4,128)S(1)}, f32[3,10,10]{2,0,1:T(4,128)}, u32[]{:S(2)}) copy-start(f32[3,10,10]{2,0,1:T(4,128)} %param.8) | copy-start | bytes 3604
  15.5 25.0 %copy-start.2 = (f32[16,16,10,256]{3,1,2,0:T(8,128)S(1)}, f32[16,16,10,256]{3,1,2,0:T(8,128)}, u32[]{:S(2)}) copy-start(f32[16,16,10,256]{3,1,2,0:T(8,128)} %param.7) | copy-start | bytes 7864324
  40.5 1.1 %copy-start.3 = (bf16[416,768]{1,0:T(8,128)(2,1)S(1)}, bf16[416,768]{1,0:T(8,128)(2,1)}, u32[]{:S(2)}) copy-start(bf16[416,768]{1,0:T(8,128)(2,1)} %constant.2.clone.const_ref) | copy-start | bytes 1916932
  41.6 25.8 %copy-start.5 = (s32[1024,3]{0,1:T(4,128)S(1)}, s32[1024,3]{0,1:T(4,128)}, u32[]{:S(2)}) copy-start(s32[1024,3]{0,1:T(4,128)} %param.10) | copy-start | bytes 36868

commit v3 on v2

--- a/solution.py
+++ b/solution.py
@@ -40,21 +40,12 @@
 
 CONST = {
     "ghost": (slice(0, 128), slice(0, 768)),
-    "up": (slice(128, 288), slice(0, 160)),
-    "pair": (slice(128, 208), slice(256, 576)),
-    "face": (slice(288, 416), slice(0, 256)),
-    "mean": (slice(128, 384), slice(640, 768)),
+    "face": (slice(0, 128), slice(768, 1024)),
+    "mean": (slice(0, 256), slice(1024, 1152)),
 }
 
 
 def fine_constants():
-    up = np.zeros((ROWS, 2 * HALF), np.float32)
-    pair = np.zeros((HALF, 2 * ROWS), np.float32)
-    for f in range(F):
-        for x in range(B):
-            for part in range(2):
-                up[f * B + x, part * HALF + f * H + x // 2] = 1
-                pair[f * H + x // 2, part * ROWS + f * B + x] = 0.125
     ghost = np.zeros((128, 768), np.float32)
     face = np.zeros((128, 256), np.float32)
     mean = np.zeros((256, 128), np.float32)
@@ -69,9 +60,9 @@
         for y in range(B):
             for z in range(B):
                 face[part * 64 + y // 2 * H + z // 2, y * B + z] = 1
-                mean[y * B + z, y // 2 * H + z // 2] = 1
-    every = np.zeros((416, 768), np.float32)
-    for name, value in (("ghost", ghost), ("up", up), ("pair", pair), ("face", face), ("mean", mean)):
+                mean[y * B + z, y // 2 * H + z // 2] = 0.125
+    every = np.zeros((256, 1152), np.float32)
+    for name, value in (("ghost", ghost), ("face", face), ("mean", mean)):
         rows, cols = CONST[name]
         every[rows, cols] = value
     return every.astype(ml_dtypes.bfloat16)
@@ -83,7 +74,13 @@
 
 def box_place(owner_ref, offset_ref, w):
     box = device_index() * BOXES + w
-    return (owner_ref[box] // (FSLOTS * LINES), *(offset_ref[d, box] for d in range(3)))
+    return (lax.shift_right_logical(owner_ref[box], 7), *(offset_ref[d, box] for d in range(3)))
+
+
+def fetch(src, dst, sem):
+    copy = pltpu.make_async_copy(src, dst, sem)
+    copy.start()
+    return copy
 
 
 def coefficients(jac_ref, pad_ref, outs):
@@ -153,9 +150,13 @@
 
 
 def coarse_kernel(
-    owner_ref, offset_ref, coarse_ref, x_lo, x_hi, y_lo, y_hi, z_lo, z_hi, jac_ref, new_ref, out_ref, fine_coef_ref, old_ref,
-    mid_ref, hi_ref, lo_ref, rest_ref, total_ref, coef_ref, pad_ref
+    owner_hbm, offset_hbm, coarse_ref, x_lo, x_hi, y_lo, y_hi, z_lo, z_hi, jac_hbm, new_ref, out_ref, fine_coef_ref, old_ref,
+    mid_ref, hi_ref, lo_ref, rest_ref, total_ref, coef_ref, pad_ref,
+    owner_ref, offset_ref, jac_ref, sems
 ):
+    fetch_owner = fetch(owner_hbm, owner_ref, sems.at[0])
+    fetch_offset = fetch(offset_hbm, offset_ref, sems.at[1])
+    fetch(jac_hbm, jac_ref, sems.at[2]).wait()
     coefficients(jac_ref, pad_ref, (coef_ref, fine_coef_ref))
     lane = lanes_of((B, 128))
     ghost_zero = jnp.zeros((16 - F, 128), F32)
@@ -195,6 +196,8 @@
                 new_ref[here, :] = new
                 mid_ref[x * PITCH + f * B : x * PITCH + f * B + B, :] = 0.5 * (coarse_ref[here, :] + new)
 
+    fetch_owner.wait()
+    fetch_offset.wait()
     lane8 = lanes_of((8, 128))
     within = lane8 % 32
     base = jnp.where(within < 16, within % 8, jnp.where(within < 24, -1, 8))
@@ -246,45 +249,55 @@
 
 
 def fine_kernel(
-    owner_ref, fine_ref, arrived_ref, coef_ref, const_ref, out_ref, back_ref, hi_ref, lo_ref, wide_ref, rest_ref, total_ref, value_ref, face_out_ref, parts_ref, mixed_ref, back_scratch, source_ref
+    owner_hbm, fine_hbm, arrived_ref, coef_ref, const_ref, out_hbm, back_ref, hi_ref, lo_ref, wide_ref, rest_ref,
+    total_ref, value_ref, face_out_ref, spread_ref, mixed_ref, mean_ref, source_ref, owner_ref, fine_ref, out_ref, sems
 ):
+    fetch_owner = fetch(owner_hbm, owner_ref, sems.at[0])
+    batches_at = [slice(i * BATCH, i * BATCH + BATCH) for i in range(FSLOTS // BATCH)]
+    fetch_fine = [fetch(fine_hbm.at[at], fine_ref.at[at], sems.at[1 + i]) for i, at in enumerate(batches_at)]
     for slot in range(FSLOTS):
         source_ref[slot] = -1
-    device = device_index()
+    first_here = device_index() * FSLOTS
     line = lax.axis_index("gz")
+    fetch_owner.wait()
     for member in range(GROUP):
         for w in range(BOXES):
             holder = owner_ref[(member * LINES + line) * BOXES + w]
-            source_ref[jnp.where(holder // FSLOTS == device, holder % FSLOTS, FSLOTS)] = member
+            source_ref[jnp.minimum(holder ^ first_here, FSLOTS)] = member
     held = sum(jnp.where(source_ref[slot] >= 0, 1, 0) for slot in range(FSLOTS))
     batches = (held + BATCH - 1) // BATCH
     constant = {name: const_ref.at[at] for name, at in CONST.items()}
+    for copy in fetch_fine:
+        copy.wait()
+
+    def write_out(i):
+        at = pl.ds(i * BATCH, BATCH)
+        return pltpu.make_async_copy(out_ref.at[at], out_hbm.at[at], sems.at[3 + i])
 
     def batch(i, _):
         first_slot = i * BATCH
         sources = [source_ref[first_slot + k] for k in range(BATCH)]
         lane = lanes_of((B, 128))
         column = lane % B
+        lane8 = lanes_of((8, 128))
         for k in range(BATCH):
             message = arrived_ref.at[jnp.maximum(sources[k], 0)]
-            for at in range(0, HALF, 16):
+            for at in range(0, 64, 16):
                 value = message[at : at + 16, :]
-                hi, lo = split(value)
-                parts_ref[k, at : at + 16, :] = hi
-                parts_ref[k, HALF + at : HALF + at + 16, :] = lo
-                if at < 64:
-                    hi = hi.astype(F32)
-                    mixed_ref[k, ROWS + at : ROWS + at + 16, :] = jnp.where(
-                        lane < 64, pltpu.roll(value - hi, 64, 1), hi
-                    ).astype(BF16)
+                hi = value.astype(BF16).astype(F32)
+                mixed_ref[k, ROWS + at : ROWS + at + 16, :] = jnp.where(
+                    lane < 64, pltpu.roll(value - hi, 64, 1), hi
+                ).astype(BF16)
+            for f in range(F):
+                value = message[f * H : f * H + H, :]
+                hi = value.astype(BF16).astype(F32)
+                both = jnp.where(lane8 < 64, hi, pltpu.roll(value - hi, 64, 1))
+                spread_ref[k, pl.ds(f * B, H, stride=2), :] = both
+                spread_ref[k, pl.ds(f * B + 1, H, stride=2), :] = both
         for k in range(BATCH):
-            lifted = dot(constant["up"][...], parts_ref[k])
             for f in range(F):
-                value = lifted[f * B : f * B + B]
-                hi = value.astype(BF16).astype(F32)
-                mixed_ref[k, f * B : f * B + B, :] = jnp.where(lane < 64, hi, pltpu.roll(value - hi, 64, 1)).astype(
-                    BF16
-                )
+                row = slice(f * B, f * B + B)
+                mixed_ref[k, row, :] = spread_ref[k, row, :].astype(BF16)
         for k in range(BATCH):
             wide_ref[k] = dot(mixed_ref[k, 0:ROWS, :], constant["ghost"][...])
             face_out_ref[k] = dot(mixed_ref[k, ROWS : ROWS + 64, :], constant["face"][...])
@@ -337,19 +350,23 @@
                         hi, lo = split(value)
                         hi_ref[k, row, :] = hi
                         hi_ref[k, ROWS + f * B : ROWS + f * B + B, :] = lo
+        write_out(i).start()
         for k in range(BATCH):
-            paired = dot(constant["pair"][...], hi_ref[k, 0 : 2 * ROWS, :])
-            hi, lo = split(paired)
-            means = dot(hi, constant["mean"][...]) + dot(lo, constant["mean"][...])
-            back_scratch[k] = jnp.where(
-                lanes_of((HALF // 2, 128)) < 64, means[: HALF // 2], pltpu.roll(means[HALF // 2 :], 64, 1)
+            mean_ref[k] = dot(hi_ref[k, 0:ROWS, :], constant["mean"][...]) + dot(
+                hi_ref[k, ROWS : 2 * ROWS, :], constant["mean"][...]
             )
-
         for k in range(BATCH):
 
             @pl.when(sources[k] >= 0)
             def _():
-                back_ref[sources[k]] = back_scratch[k]
+                for f in range(F // 2):
+                    halves = [
+                        mean_ref[k, pl.ds(g * B, H, stride=2), :] + mean_ref[k, pl.ds(g * B + 1, H, stride=2), :]
+                        for g in (f, f + F // 2)
+                    ]
+                    back_ref[sources[k], f * H : f * H + H, :] = jnp.where(
+                        lane8 < 64, halves[0], pltpu.roll(halves[1], 64, 1)
+                    )
 
         return 0
 
@@ -358,14 +375,21 @@
     def empty(i, _):
         for k in range(BATCH):
             out_ref[i * BATCH + k] = jnp.zeros(out_ref.shape[1:], F32)
+        write_out(i).start()
         return 0
 
     lax.fori_loop(batches, FSLOTS // BATCH, empty, 0)
-
-
-def place_kernel(owner_ref, offset_ref, new_ref, back_ref, out_ref, work_ref, sems):
+    for i in range(FSLOTS // BATCH):
+        write_out(i).wait()
+
+
+def place_kernel(owner_hbm, offset_hbm, new_ref, back_ref, out_ref, work_ref, sems, owner_ref, offset_ref):
+    fetch_owner = fetch(owner_hbm, owner_ref, sems.at[B])
+    fetch_offset = fetch(offset_hbm, offset_ref, sems.at[B + 1])
     for x in range(B):
         work_ref[x * PITCH : x * PITCH + ROWS, :] = new_ref[x * ROWS : (x + 1) * ROWS, :]
+    fetch_owner.wait()
+    fetch_offset.wait()
     lane = lanes_of((8, 128))
 
     def box(w, _):
@@ -396,12 +420,15 @@
         copy.wait()
 
 
-def call(kernel, operands, outs, limit, scratch=(), out_space=pltpu.VMEM):
-    spaces = [pltpu.SMEM if a.dtype == jnp.int32 else pltpu.VMEM for a in operands]
+INDEX = [pltpu.SMEM((BOXES * LINES * GROUP,), jnp.int32), pltpu.SMEM((3, BOXES * LINES * GROUP), jnp.int32)]
+
+
+def call(kernel, operands, outs, limit, scratch=(), hbm=(), hbm_outs=()):
+    space = lambda cond: pl.BlockSpec(memory_space=pltpu.HBM if cond else pltpu.VMEM)
     return pl.pallas_call(
         kernel,
-        in_specs=[pl.BlockSpec(memory_space=space) for space in spaces],
-        out_specs=[pl.BlockSpec(memory_space=out_space) for _ in outs],
+        in_specs=[space(i in hbm) for i in range(len(operands))],
+        out_specs=[space(i in hbm_outs) for i in range(len(outs))],
         out_shape=[jax.ShapeDtypeStruct(*out) for out in outs],
         scratch_shapes=list(scratch),
         compiler_params=pltpu.CompilerParams(vmem_limit_bytes=limit * MIB),
@@ -441,7 +468,10 @@
         [pltpu.VMEM((B * PITCH, 128), F32)] * 2
         + [pltpu.VMEM((B // 2, 512, 256), BF16)] * 2
         + [pltpu.VMEM((B // 2, ROWS, 256), F32)] * 2
-        + [pltpu.VMEM((2, ROWS, 512), BF16), pltpu.VMEM((3, 16, 128), F32)],
+        + [pltpu.VMEM((2, ROWS, 512), BF16), pltpu.VMEM((3, 16, 128), F32)]
+        + INDEX
+        + [pltpu.VMEM((F, 3, F), F32), pltpu.SemaphoreType.DMA((3,))],
+        hbm=(0, 1, 9),
     )
     arrived = lax.all_to_all(outgoing, ("gx", "gy"), split_axis=0, concat_axis=0, tiled=True)
 
@@ -449,17 +479,23 @@
         fine_kernel,
         (fine_owner, fine_rows, arrived, coef, fine_constants()),
         [((FSLOTS, F, B, 256), F32), ((GROUP, HALF // 2, 128), F32)],
-        20,
+        24,
         [pltpu.VMEM((BATCH, 512, 256), BF16)] * 2
         + [pltpu.VMEM((BATCH, ROWS, 768), F32)]
         + [pltpu.VMEM((BATCH, ROWS, 256), F32)] * 3
         + [
             pltpu.VMEM((BATCH, 64, 256), F32),
-            pltpu.VMEM((BATCH, 2 * HALF, 128), BF16),
+            pltpu.VMEM((BATCH, ROWS, 128), F32),
             pltpu.VMEM((BATCH, ROWS + 64, 128), BF16),
-            pltpu.VMEM((BATCH, HALF // 2, 128), F32),
+            pltpu.VMEM((BATCH, ROWS, 128), F32),
             pltpu.SMEM((FSLOTS + 1,), jnp.int32),
+            INDEX[0],
+            pltpu.VMEM((FSLOTS, F, B, 256), F32),
+            pltpu.VMEM((FSLOTS, F, B, 256), F32),
+            pltpu.SemaphoreType.DMA((1 + 2 * (FSLOTS // BATCH),)),
         ],
+        hbm=(0, 1),
+        hbm_outs=(0,),
     )
     came_back = lax.all_to_all(returning, ("gx", "gy"), split_axis=0, concat_axis=0, tiled=True)
 
@@ -468,8 +504,9 @@
         (fine_owner, offset, new, came_back),
         [((B * ROWS, 128), F32)],
         4,
-        [pltpu.VMEM((B * PITCH, 128), F32), pltpu.SemaphoreType.DMA((B,))],
-        pl.ANY,
+        [pltpu.VMEM((B * PITCH, 128), F32), pltpu.SemaphoreType.DMA((B + 2,))] + INDEX,
+        hbm=(0, 1),
+        hbm_outs=(0,),
     )[0]
     return coarse_out.reshape(coarse_state.shape), jnp.transpose(fine_new, (0, 2, 1, 3))
 

time: 72.8 us -> 69.1 us (0.949)
  Pallas kernels: 19.7 us -> 17.3 us
  blocking collectives: 36.3 us -> 35.1 us
    pallas_call x4, Pallas kernels: 19.7 us -> 17.3 us  [call(): pl.pallas_call(kernel, in_specs=[space(i in hbm) for i in range(len(opera...]
    all_to_all x1, blocking collectives: 17.2 us -> 15.9 us  [local(): lax.all_to_all(returning, ('gx', 'gy'), split_axis=0, concat_axis=0, tile...]
where the time goes in v3:
time: 69.1 us; the launch traced here: 68.2 us
  blocking collectives  35.1 us (51%)
  Pallas kernels  17.3 us (25%)
  starting transfers between devices  9.17 us (13%)
  local copies, waits for them, and re-layouts  3.83 us (6%)
  waiting for transfers between devices  2.12 us (3%)
    all_to_all x1, blocking collectives, local(): lax.all_to_all(outgoing, ('gx', 'gy'), split_axis=0, concat_axis=0, tiled...  19.2 us
    pallas_call x4, Pallas kernels, call(): pl.pallas_call(kernel, in_specs=[space(i in hbm) for i in range(len(opera...  17.3 us
    all_to_all x1, blocking collectives, local(): lax.all_to_all(returning, ('gx', 'gy'), split_axis=0, concat_axis=0, tile...  15.9 us
    ppermute x3, starting transfers between devices, from_above(): return lax.ppermute(value, axis, [((i + 1) % n, i) for i in range(n)])  5.61 us
    unnamed x16, local copies, waits for them, and re-layouts  3.83 us
    ppermute x3, starting transfers between devices, from_below(): return lax.ppermute(value, axis, [(i, (i + 1) % n) for i in range(n)])  3.56 us
    ppermute x3, waiting for transfers between devices, from_below(): return lax.ppermute(value, axis, [(i, (i + 1) % n) for i in range(n)])  1.75 us
  transfers between devices with their start and end apart: 6, of which 3 were waited for; matrix products, arithmetic and copies ran while one was open for 0% of the time, Pallas kernels for 0%

profile of v3, /device:TPU:4, one launch (start us, length us, event | category | flops | bytes accessed | tf_op | source)
XLA Modules:
  0.0 68.2 jit_solution(9397346486744037099)
XLA Ops:
  0.6 0.0 copy-start
  0.6 1.3 %copy-done = f32[16,10,16,128]{3,2,1,0:T(8,128)S(1)} copy-done((f32[16,10,16,128]{3,2,1,0:T(8,128)S(1)}, f32[16,10,16,128]{3,2,1,0:T(8,128)}, u32[]{:S(2)}) %copy-start) | copy-done | bytes 1310744
  2.0 0.8 %shard_map.77 = (f32[160,128]{1,0:T(8,128)S(1)}, f32[160,128]{1,0:T(8,128)S(1)}, f32[160,128]{1,0:T(8,128)S(1)}, f32[160,128]{1,0:T(8,128)S(1)}, f32[160,128]{1,0:T(8,128)S(1)}, /*index=5*/f32[160,128]{1,0:T(8,128)S(1)}) custom-call(f32[2560,128]{1,0:T(8,128)S(1)} %bitcast.6), custom_call_target="tpu_custom_call" | custom-call | tf_op jit(solution)/shard_map/pallas_call | solution.py:428
  2.7 2.0 %collective-permute-start = (f32[160,128]{1,0:T(8,128)S(1)}, f32[160,128]{1,0:T(8,128)S(1)}, u32[]{:S(2)}, u32[]{:S(2)}) collective-permute-start(f32[160,128]{1,0:T(8,128)S(1)} %get-tuple-element.13), channel_id=1, source_target_pairs={{0,32},{32,64},{64,96},{96,0},{1,33},{33,65},{65,97},{97,1},{2,34}... | collective-permute-start | bytes 245768 | tf_op jit(solution)/shard_map/ppermute | solution.py:449
  4.7 2.2 %collective-permute-start.1 = (f32[160,128]{1,0:T(8,128)S(1)}, f32[160,128]{1,0:T(8,128)S(1)}, u32[]{:S(2)}, u32[]{:S(2)}) collective-permute-start(f32[160,128]{1,0:T(8,128)S(1)} %get-tuple-element.14), channel_id=1, source_target_pairs={{32,0},{64,32},{96,64},{0,96},{33,1},{65,33},{97,65},{1,97},{34,2}... | collective-permute-start | bytes 245768 | tf_op jit(solution)/shard_map/ppermute | solution.py:453
  6.9 1.6 %collective-permute-start.2 = (f32[160,128]{1,0:T(8,128)S(1)}, f32[160,128]{1,0:T(8,128)S(1)}, u32[]{:S(2)}, u32[]{:S(2)}) collective-permute-start(f32[160,128]{1,0:T(8,128)S(1)} %get-tuple-element.15), channel_id=1, source_target_pairs={{0,8},{8,16},{16,24},{24,0},{1,9},{9,17},{17,25},{25,1},{2,10},{10... | collective-permute-start | bytes 245768 | tf_op jit(solution)/shard_map/ppermute | solution.py:449
  8.5 1.7 %collective-permute-start.3 = (f32[160,128]{1,0:T(8,128)S(1)}, f32[160,128]{1,0:T(8,128)S(1)}, u32[]{:S(2)}, u32[]{:S(2)}) collective-permute-start(f32[160,128]{1,0:T(8,128)S(1)} %get-tuple-element.16), channel_id=1, source_target_pairs={{8,0},{16,8},{24,16},{0,24},{9,1},{17,9},{25,17},{1,25},{10,2},{18... | collective-permute-start | bytes 245768 | tf_op jit(solution)/shard_map/ppermute | solution.py:453
  10.1 0.0 collective-permute-start.4
  10.1 0.0 collective-permute-done.x_lo
  10.1 1.7 %collective-permute-start.5 = (f32[160,128]{1,0:T(8,128)S(1)}, f32[160,128]{1,0:T(8,128)S(1)}, u32[]{:S(2)}, u32[]{:S(2)}) collective-permute-start(f32[160,128]{1,0:T(8,128)S(1)} %get-tuple-element.18), channel_id=1, source_target_pairs={{1,0},{2,1},{3,2},{4,3},{5,4},{6,5},{7,6},{0,7},{9,8},{10,9},{11,1... | collective-permute-start | bytes 245768 | tf_op jit(solution)/shard_map/ppermute | solution.py:453
  11.9 0.0 collective-permute-done.1.x_hi
  11.9 0.7 collective-permute-done.2.y_lo
  12.6 0.4 collective-permute-done.3.y_hi
  12.9 1.1 %collective-permute-done.4.z_lo = f32[160,128]{1,0:T(8,128)S(1)} collective-permute-done((f32[160,128]{1,0:T(8,128)S(1)}, f32[160,128]{1,0:T(8,128)S(1)}, u32[]{:S(2)}, u32[]{:S(2)}) %collective-permute-start.4) | collective-permute-done | bytes 81952 | tf_op jit(solution)/shard_map/ppermute | solution.py:449
  14.0 0.0 collective-permute-done.5.z_hi
  14.0 0.0 copy-start.4
  14.0 0.7 %copy-done.4 = s32[1024,3]{0,1:T(4,128)S(1)} copy-done((s32[1024,3]{0,1:T(4,128)S(1)}, s32[1024,3]{0,1:T(4,128)}, u32[]{:S(2)}) %copy-start.4) | copy-done | bytes 12312
  14.7 0.7 %copy-done.7 = f32[3,10,10]{2,0,1:T(4,128)S(1)} copy-done((f32[3,10,10]{2,0,1:T(4,128)S(1)}, f32[3,10,10]{2,0,1:T(4,128)}, u32[]{:S(2)}) %copy-start.7) | copy-done | bytes 1224
  15.5 5.0 %shard_map.78 = (f32[2560,128]{1,0:T(8,128)S(1)}, f32[16,80,128]{2,1,0:T(8,128)S(1)}, bf16[2,160,512]{2,1,0:T(8,128)(2,1)S(1)}) custom-call(s32[1024]{0:T(1024)S(1)} %copy-done.6, s32[3,1024]{1,0:T(4,128)S(1)} %bitcast.9, f32[2560,128]{1,0:T(8,128)S(1)} %bitcast.7, f32[160,128]{1,0:T(8,128)S(1)} %collective-permute-done.x_lo, ...), custom_call_target="tpu_custom_call" | custom-call | tf_op jit(solution)/shard_map/pallas_call | solution.py:428
  20.5 19.2 %all_to_all.10.arrived_ref = f32[16,80,128]{2,1,0:T(8,128)S(1)} all-to-all(f32[16,80,128]{2,1,0:T(8,128)S(1)} %get-tuple-element.20), channel_id=1, replica_groups=mesh['gx'=4,'gy'=4,'gz'=8] {'gx','gy'}, dimensions={0} | all-to-all | bytes 1310720 | tf_op jit(solution)/shard_map/all_to_all | solution.py:476
  39.7 1.1 %copy-done.3 = bf16[256,1152]{1,0:T(8,128)(2,1)S(1)} copy-done((bf16[256,1152]{1,0:T(8,128)(2,1)S(1)}, bf16[256,1152]{1,0:T(8,128)(2,1)}, u32[]{:S(2)}) %copy-start.3) | copy-done | bytes 589848
  40.8 7.1 %shard_map.79 = (f32[16,10,16,256]{3,2,1,0:T(8,128)}, f32[16,40,128]{2,1,0:T(8,128)S(1)}) custom-call(s32[1024]{0:T(1024)S(1)} %copy-done.6, f32[16,10,16,256]{3,2,1,0:T(8,128)S(1)} %bitcast.8, f32[16,80,128]{2,1,0:T(8,128)S(1)} %all_to_all.10.arrived_ref, bf16[2,160,512]{2,1,0:T(8,128)(2,1)S(1)} %get-tuple-element.21.coef_ref, bf16[256,1152]{1,0:T(8,128)(2,1)S(1)} %copy-done.3), custom_call_target="tpu_custom_call" | custom-call | tf_op jit(solution)/shard_map/pallas_call | solution.py:428
  47.8 15.9 %all_to_all.11.back_ref = f32[16,40,128]{2,1,0:T(8,128)S(1)} all-to-all(f32[16,40,128]{2,1,0:T(8,128)S(1)} %get-tuple-element.22), channel_id=1, replica_groups=mesh['gx'=4,'gy'=4,'gz'=8] {'gx','gy'}, dimensions={0} | all-to-all | bytes 655360 | tf_op jit(solution)/shard_map/all_to_all | solution.py:500
  63.8 4.4 %shard_map.80 = f32[2560,128]{1,0:T(8,128)} custom-call(s32[1024]{0:T(1024)S(1)} %copy-done.6, s32[3,1024]{1,0:T(4,128)S(1)} %bitcast.10, f32[2560,128]{1,0:T(8,128)S(1)} %get-tuple-element.19.new_ref, f32[16,40,128]{2,1,0:T(8,128)S(1)} %all_to_all.11.back_ref), custom_call_target="tpu_custom_call" | custom-call | tf_op jit(solution)/shard_map/pallas_call | solution.py:428
  (10 shorter events, 0.0 us)
Async XLA Ops:
  0.6 1.3 %copy-start = (f32[16,10,16,128]{3,2,1,0:T(8,128)S(1)}, f32[16,10,16,128]{3,2,1,0:T(8,128)}, u32[]{:S(2)}) copy-start(f32[16,10,16,128]{3,2,1,0:T(8,128)} %param.6) | copy-start | bytes 3932164
  1.9 12.1 %copy-start.1 = (f32[16,10,16,128]{3,2,1,0:T(8,128)S(1)}, f32[16,10,16,128]{3,2,1,0:T(8,128)}, u32[]{:S(2)}) copy-start(f32[16,10,16,128]{3,2,1,0:T(8,128)} %param.6) | copy-start | bytes 3932164
  1.9 12.1 %copy-start.6 = (s32[1024]{0:T(1024)S(1)}, s32[1024]{0:T(1024)}, u32[]{:S(2)}) copy-start(s32[1024]{0:T(1024)} %owner_hbm.5) | copy-start | bytes 12292
  2.7 7.4 %collective-permute-start = (f32[160,128]{1,0:T(8,128)S(1)}, f32[160,128]{1,0:T(8,128)S(1)}, u32[]{:S(2)}, u32[]{:S(2)}) collective-permute-start(f32[160,128]{1,0:T(8,128)S(1)} %get-tuple-element.13), channel_id=1, source_target_pairs={{0,32},{32,64},{64,96},{96,0},{1,33},{33,65},{65,97},{97,1},{2,34}... | collective-permute-start | bytes 245768 | tf_op jit(solution)/shard_map/ppermute | solution.py:449
  4.7 7.2 %collective-permute-start.1 = (f32[160,128]{1,0:T(8,128)S(1)}, f32[160,128]{1,0:T(8,128)S(1)}, u32[]{:S(2)}, u32[]{:S(2)}) collective-permute-start(f32[160,128]{1,0:T(8,128)S(1)} %get-tuple-element.14), channel_id=1, source_target_pairs={{32,0},{64,32},{96,64},{0,96},{33,1},{65,33},{97,65},{1,97},{34,2}... | collective-permute-start | bytes 245768 | tf_op jit(solution)/shard_map/ppermute | solution.py:453
  6.9 5.7 %collective-permute-start.2 = (f32[160,128]{1,0:T(8,128)S(1)}, f32[160,128]{1,0:T(8,128)S(1)}, u32[]{:S(2)}, u32[]{:S(2)}) collective-permute-start(f32[160,128]{1,0:T(8,128)S(1)} %get-tuple-element.15), channel_id=1, source_target_pairs={{0,8},{8,16},{16,24},{24,0},{1,9},{9,17},{17,25},{25,1},{2,10},{10... | collective-permute-start | bytes 245768 | tf_op jit(solution)/shard_map/ppermute | solution.py:449
  8.5 4.4 %collective-permute-start.3 = (f32[160,128]{1,0:T(8,128)S(1)}, f32[160,128]{1,0:T(8,128)S(1)}, u32[]{:S(2)}, u32[]{:S(2)}) collective-permute-start(f32[160,128]{1,0:T(8,128)S(1)} %get-tuple-element.16), channel_id=1, source_target_pairs={{8,0},{16,8},{24,16},{0,24},{9,1},{17,9},{25,17},{1,25},{10,2},{18... | collective-permute-start | bytes 245768 | tf_op jit(solution)/shard_map/ppermute | solution.py:453
  10.1 3.9 %collective-permute-start.4 = (f32[160,128]{1,0:T(8,128)S(1)}, f32[160,128]{1,0:T(8,128)S(1)}, u32[]{:S(2)}, u32[]{:S(2)}) collective-permute-start(f32[160,128]{1,0:T(8,128)S(1)} %get-tuple-element.17), channel_id=1, source_target_pairs={{0,1},{1,2},{2,3},{3,4},{4,5},{5,6},{6,7},{7,0},{8,9},{9,10},{10,1... | collective-permute-start | bytes 245768 | tf_op jit(solution)/shard_map/ppermute | solution.py:449
  10.1 3.9 %collective-permute-start.5 = (f32[160,128]{1,0:T(8,128)S(1)}, f32[160,128]{1,0:T(8,128)S(1)}, u32[]{:S(2)}, u32[]{:S(2)}) collective-permute-start(f32[160,128]{1,0:T(8,128)S(1)} %get-tuple-element.18), channel_id=1, source_target_pairs={{1,0},{2,1},{3,2},{4,3},{5,4},{6,5},{7,6},{0,7},{9,8},{10,9},{11,1... | collective-permute-start | bytes 245768 | tf_op jit(solution)/shard_map/ppermute | solution.py:453
  14.0 0.7 %copy-start.4 = (s32[1024,3]{0,1:T(4,128)S(1)}, s32[1024,3]{0,1:T(4,128)}, u32[]{:S(2)}) copy-start(s32[1024,3]{0,1:T(4,128)} %param.10) | copy-start | bytes 36868
  14.7 0.7 %copy-start.7 = (f32[3,10,10]{2,0,1:T(4,128)S(1)}, f32[3,10,10]{2,0,1:T(4,128)}, u32[]{:S(2)}) copy-start(f32[3,10,10]{2,0,1:T(4,128)} %param.8) | copy-start | bytes 3604
  15.5 24.2 %copy-start.2 = (f32[16,16,10,256]{3,1,2,0:T(8,128)S(1)}, f32[16,16,10,256]{3,1,2,0:T(8,128)}, u32[]{:S(2)}) copy-start(f32[16,16,10,256]{3,1,2,0:T(8,128)} %param.7) | copy-start | bytes 7864324
  39.7 1.1 %copy-start.3 = (bf16[256,1152]{1,0:T(8,128)(2,1)S(1)}, bf16[256,1152]{1,0:T(8,128)(2,1)}, u32[]{:S(2)}) copy-start(bf16[256,1152]{1,0:T(8,128)(2,1)} %constant.2.clone.const_ref) | copy-start | bytes 1769476
  40.8 23.0 %copy-start.5 = (s32[1024,3]{0,1:T(4,128)S(1)}, s32[1024,3]{0,1:T(4,128)}, u32[]{:S(2)}) copy-start(s32[1024,3]{0,1:T(4,128)} %param.10) | copy-start | bytes 36868

commit v4 on v3

--- a/solution.py
+++ b/solution.py
@@ -2,8 +2,6 @@
 
 import jax
 import jax.numpy as jnp
-import ml_dtypes
-import numpy as np
 from jax import lax
 from jax.experimental import pallas as pl
 from jax.experimental.pallas import tpu as pltpu
@@ -20,6 +18,7 @@
 HALF = F * H
 F32 = jnp.float32
 BF16 = jnp.bfloat16
+MESSAGE = HALF // 2 + 24
 MIB = 1024 * 1024
 PITCH = ROWS + 8
 BATCH = 8
@@ -38,34 +37,32 @@
     return lax.broadcasted_iota(jnp.int32, shape, len(shape) - 1)
 
 
-CONST = {
-    "ghost": (slice(0, 128), slice(0, 768)),
-    "face": (slice(0, 128), slice(768, 1024)),
-    "mean": (slice(0, 256), slice(1024, 1152)),
-}
-
-
-def fine_constants():
-    ghost = np.zeros((128, 768), np.float32)
-    face = np.zeros((128, 256), np.float32)
-    mean = np.zeros((256, 128), np.float32)
-    for part in range(2):
-        for t in range(2):
-            for j in range(B):
-                low, col = part * 64 + t * 32 + j // 2, t * 384
-                ghost[low, col + j] = 1
-                ghost[low + 8, col + 112 + j] = 1
-                ghost[low + 16, col + 128 + j * B] = 1
-                ghost[low + 24, col + 128 + j * B + B - 1] = 1
-        for y in range(B):
-            for z in range(B):
-                face[part * 64 + y // 2 * H + z // 2, y * B + z] = 1
-                mean[y * B + z, y // 2 * H + z // 2] = 0.125
-    every = np.zeros((256, 1152), np.float32)
-    for name, value in (("ghost", ghost), ("face", face), ("mean", mean)):
-        rows, cols = CONST[name]
-        every[rows, cols] = value
-    return every.astype(ml_dtypes.bfloat16)
+def fine_constants(ghost_ref, face_ref, mean_ref):
+    def one(cond):
+        return jnp.where(cond, 1.0, 0.0).astype(BF16)
+
+    row, col = (lax.broadcasted_iota(jnp.int32, (128, 384), d) for d in range(2))
+    cell = col - 128
+    y, z = cell // B, cell % B
+    target = jnp.where(
+        col < 16,
+        col // 2,
+        jnp.where(
+            col < 112,
+            -1,
+            jnp.where(
+                col < 128,
+                8 + (col - 112) // 2,
+                jnp.where(z == 0, 16 + y // 2, jnp.where(z == B - 1, 24 + y // 2, -1)),
+            ),
+        ),
+    )
+    for t in range(2):
+        ghost_ref[:, 384 * t : 384 * t + 384] = one(row % 64 == target + jnp.where(target < 0, -64, 32 * t))
+    row, col = (lax.broadcasted_iota(jnp.int32, (128, 256), d) for d in range(2))
+    face_ref[...] = one(row % 64 == col // B // 2 * H + col % B // 2)
+    row, col = (lax.broadcasted_iota(jnp.int32, (256, 128), d) for d in range(2))
+    mean_ref[...] = one(col == row // B // 2 * H + row % B // 2) * jnp.asarray(0.125, BF16)
 
 
 def device_index():
@@ -209,48 +206,45 @@
         pick = base + z0
         pick_x = window + z0
         corner = ox * PITCH + oy - 1
-        for f in range(F):
+        for f in range(F // 2):
             acc = jnp.zeros((8, 128), F32)
-            for t, ref in enumerate((old_ref, mid_ref)):
-                for y in range(H + 2):
-                    rows = ref[pl.ds(corner + f * B + y, H, stride=PITCH), :]
-                    moved = jnp.take_along_axis(rows, pick, axis=1, mode="promise_in_bounds")
-                    if y == 0:
-                        put = (lane8 >= 32 * t) & (lane8 < 32 * t + 8)
-                    elif y == H + 1:
-                        put = (lane8 >= 32 * t + 8) & (lane8 < 32 * t + 16)
-                    else:
-                        put = (lane8 == 32 * t + 15 + y) | (lane8 == 32 * t + 23 + y)
-                    acc = jnp.where(put, moved, acc)
+            for half in range(2):
+                for t, ref in enumerate((old_ref, mid_ref)):
+                    low = 64 * half + 32 * t
+                    for y in range(H + 2):
+                        rows = ref[pl.ds(corner + (f + 5 * half) * B + y, H, stride=PITCH), :]
+                        moved = jnp.take_along_axis(rows, pick, axis=1, mode="promise_in_bounds")
+                        if y == 0:
+                            put = (lane8 >= low) & (lane8 < low + 8)
+                        elif y == H + 1:
+                            put = (lane8 >= low + 8) & (lane8 < low + 16)
+                        else:
+                            put = (lane8 == low + 15 + y) | (lane8 == low + 23 + y)
+                        acc = jnp.where(put, moved, acc)
             out_ref[member, f * 8 : f * 8 + 8, :] = acc
-        for t, ref in enumerate((old_ref, mid_ref)):
-            for side, x in enumerate((ox - 1, ox + H)):
-                first = jnp.zeros((8, 128), F32)
-                second = jnp.zeros((8, 128), F32)
-                for y in range(H):
-                    put = (lane8 >= 64 + y * 8) & (lane8 < 72 + y * 8)
-                    at = x * PITCH + oy + y
-                    rows = ref[pl.ds(at, 8, stride=B), :]
-                    first = jnp.where(put, jnp.take_along_axis(rows, pick_x, axis=1, mode="promise_in_bounds"), first)
-                    tail = jnp.concatenate(
-                        [ref[pl.ds(at + 8 * B, F - 8, stride=B), :], jnp.zeros((16 - F, 128), F32)], axis=0
-                    )
-                    second = jnp.where(
-                        put, jnp.take_along_axis(tail, pick_x, axis=1, mode="promise_in_bounds"), second
-                    )
-                at = (2 * t + side) * 16
-                old = out_ref[member, at : at + 16, :]
-                out_ref[member, at : at + 16, :] = jnp.where(
-                    lanes_of((16, 128)) < 64, old, jnp.concatenate([first, second], axis=0)
-                )
+        tiles = [jnp.zeros((8, 128), F32)] * 3
+        for side, x in enumerate((ox - 1, ox + H)):
+            for y in range(H):
+                low = 64 * side + 8 * y
+                put = (lane8 >= low) & (lane8 < low + 8)
+                at = x * PITCH + oy + y
+                tails = [ref[pl.ds(at + 8 * B, F - 8, stride=B), :] for ref in (old_ref, mid_ref)]
+                values = [ref[pl.ds(at, 8, stride=B), :] for ref in (old_ref, mid_ref)]
+                values.append(jnp.concatenate(tails + [jnp.zeros((4, 128), F32)], axis=0))
+                for n, value in enumerate(values):
+                    moved = jnp.take_along_axis(value, pick_x, axis=1, mode="promise_in_bounds")
+                    tiles[n] = jnp.where(put, moved, tiles[n])
+        for n in range(3):
+            out_ref[member, HALF // 2 + 8 * n : HALF // 2 + 8 * n + 8, :] = tiles[n]
         return 0
 
     lax.fori_loop(0, BOXES, box, 0, unroll=2)
 
 
 def fine_kernel(
-    owner_hbm, fine_hbm, arrived_ref, coef_ref, const_ref, out_hbm, back_ref, hi_ref, lo_ref, wide_ref, rest_ref,
-    total_ref, value_ref, face_out_ref, spread_ref, mixed_ref, mean_ref, source_ref, owner_ref, fine_ref, out_ref, sems
+    owner_hbm, fine_hbm, arrived_ref, coef_ref, out_hbm, back_ref, hi_ref, lo_ref, wide_ref, rest_ref,
+    total_ref, value_ref, face_out_ref, spread_ref, mixed_ref, mean_ref, source_ref, owner_ref, fine_ref, out_ref,
+    ghost_ref, face_ref, pair_ref, sems
 ):
     fetch_owner = fetch(owner_hbm, owner_ref, sems.at[0])
     batches_at = [slice(i * BATCH, i * BATCH + BATCH) for i in range(FSLOTS // BATCH)]
@@ -266,7 +260,7 @@
             source_ref[jnp.minimum(holder ^ first_here, FSLOTS)] = member
     held = sum(jnp.where(source_ref[slot] >= 0, 1, 0) for slot in range(FSLOTS))
     batches = (held + BATCH - 1) // BATCH
-    constant = {name: const_ref.at[at] for name, at in CONST.items()}
+    fine_constants(ghost_ref, face_ref, pair_ref)
     for copy in fetch_fine:
         copy.wait()
 
@@ -282,16 +276,20 @@
         lane8 = lanes_of((8, 128))
         for k in range(BATCH):
             message = arrived_ref.at[jnp.maximum(sources[k], 0)]
-            for at in range(0, 64, 16):
-                value = message[at : at + 16, :]
+            tail = message[MESSAGE - 8 : MESSAGE, :]
+            for t in range(2):
+                at = HALF // 2 + 8 * t
+                value = jnp.concatenate([message[at : at + 8, :], pltpu.roll(tail, 6, 0) if t else tail], axis=0)
                 hi = value.astype(BF16).astype(F32)
-                mixed_ref[k, ROWS + at : ROWS + at + 16, :] = jnp.where(
-                    lane < 64, pltpu.roll(value - hi, 64, 1), hi
-                ).astype(BF16)
+                lo = pltpu.roll(value - hi, 64, 1)
+                at = ROWS + 32 * t
+                mixed_ref[k, at : at + 16, :] = jnp.where(lane < 64, hi, lo).astype(BF16)
+                mixed_ref[k, at + 16 : at + 32, :] = jnp.where(lane < 64, lo, hi).astype(BF16)
             for f in range(F):
-                value = message[f * H : f * H + H, :]
+                value = message[f % 5 * H : f % 5 * H + H, :]
                 hi = value.astype(BF16).astype(F32)
-                both = jnp.where(lane8 < 64, hi, pltpu.roll(value - hi, 64, 1))
+                lo = pltpu.roll(value - hi, 64, 1)
+                both = jnp.where(lane8 < 64, hi, lo) if f < 5 else jnp.where(lane8 < 64, lo, hi)
                 spread_ref[k, pl.ds(f * B, H, stride=2), :] = both
                 spread_ref[k, pl.ds(f * B + 1, H, stride=2), :] = both
         for k in range(BATCH):
@@ -299,8 +297,8 @@
                 row = slice(f * B, f * B + B)
                 mixed_ref[k, row, :] = spread_ref[k, row, :].astype(BF16)
         for k in range(BATCH):
-            wide_ref[k] = dot(mixed_ref[k, 0:ROWS, :], constant["ghost"][...])
-            face_out_ref[k] = dot(mixed_ref[k, ROWS : ROWS + 64, :], constant["face"][...])
+            wide_ref[k] = dot(mixed_ref[k, 0:ROWS, :], ghost_ref[...])
+            face_out_ref[k] = dot(mixed_ref[k, ROWS : ROWS + 64, :], face_ref[...])
         for t in range(2):
             at = 384 * t
             for k in range(BATCH):
@@ -352,8 +350,8 @@
                         hi_ref[k, ROWS + f * B : ROWS + f * B + B, :] = lo
         write_out(i).start()
         for k in range(BATCH):
-            mean_ref[k] = dot(hi_ref[k, 0:ROWS, :], constant["mean"][...]) + dot(
-                hi_ref[k, ROWS : 2 * ROWS, :], constant["mean"][...]
+            mean_ref[k] = dot(hi_ref[k, 0:ROWS, :], pair_ref[...]) + dot(
+                hi_ref[k, ROWS : 2 * ROWS, :], pair_ref[...]
             )
         for k in range(BATCH):
 
@@ -398,13 +396,16 @@
         inside = (lane >= z0) & (lane < z0 + H)
         pick = jnp.where(inside, lane - z0, 0)
         corner = ox * PITCH + oy
-        for f in range(F):
-            tile = back_ref[member, f % 5 * 8 : f % 5 * 8 + 8, :]
-            rows = [pl.ds(corner + f * B + y, H, stride=PITCH) for y in range(H)]
+        for group in range(2):
+            rows = [
+                pl.ds(corner + (group * 5 + f) * B + y, H, stride=PITCH) for f in range(F // 2) for y in range(H)
+            ]
             before = [work_ref[r, :] for r in rows]
-            for y in range(H):
-                moved = jnp.take_along_axis(tile, pick + (f // 5 * 64 + y * 8), axis=1, mode="promise_in_bounds")
-                work_ref[rows[y], :] = jnp.where(inside, moved, before[y])
+            for f in range(F // 2):
+                tile = back_ref[member, f * H : f * H + H, :]
+                for y in range(H):
+                    moved = jnp.take_along_axis(tile, pick + (group * 64 + y * 8), axis=1, mode="promise_in_bounds")
+                    work_ref[rows[f * H + y], :] = jnp.where(inside, moved, before[f * H + y])
         return 0
 
     lax.fori_loop(0, BOXES, box, 0)
@@ -463,7 +464,7 @@
     new, outgoing, coef = call(
         coarse_kernel,
         (fine_owner, offset, rows, *halo, jacobians),
-        [((B * ROWS, 128), F32), ((GROUP, HALF, 128), F32), ((2, ROWS, 512), BF16)],
+        [((B * ROWS, 128), F32), ((GROUP, MESSAGE, 128), F32), ((2, ROWS, 512), BF16)],
         14,
         [pltpu.VMEM((B * PITCH, 128), F32)] * 2
         + [pltpu.VMEM((B // 2, 512, 256), BF16)] * 2
@@ -477,7 +478,7 @@
 
     fine_new, returning = call(
         fine_kernel,
-        (fine_owner, fine_rows, arrived, coef, fine_constants()),
+        (fine_owner, fine_rows, arrived, coef),
         [((FSLOTS, F, B, 256), F32), ((GROUP, HALF // 2, 128), F32)],
         24,
         [pltpu.VMEM((BATCH, 512, 256), BF16)] * 2
@@ -492,6 +493,9 @@
             INDEX[0],
             pltpu.VMEM((FSLOTS, F, B, 256), F32),
             pltpu.VMEM((FSLOTS, F, B, 256), F32),
+            pltpu.VMEM((128, 768), BF16),
+            pltpu.VMEM((128, 256), BF16),
+            pltpu.VMEM((256, 128), BF16),
             pltpu.SemaphoreType.DMA((1 + 2 * (FSLOTS // BATCH),)),
         ],
         hbm=(0, 1),

time: 69.1 us -> 65.7 us (0.951)
  blocking collectives: 35.1 us -> 32.6 us
  local copies, waits for them, and re-layouts: 3.83 us -> 2.76 us
    all_to_all x1, blocking collectives: 19.2 us -> 17.8 us  [local(): lax.all_to_all(outgoing, ('gx', 'gy'), split_axis=0, concat_axis=0, tiled...]
    all_to_all x1, blocking collectives: 15.9 us -> 14.9 us  [local(): lax.all_to_all(returning, ('gx', 'gy'), split_axis=0, concat_axis=0, tile...]
    unnamed x16 -> x14, local copies, waits for them, and re-layouts: 3.83 us -> 2.76 us
where the time goes in v4:
time: 65.7 us; the launch traced here: 64.4 us
  blocking collectives  32.6 us (50%)
  Pallas kernels  17.1 us (26%)
  starting transfers between devices  9.17 us (14%)
  local copies, waits for them, and re-layouts  2.76 us (4%)
  waiting for transfers between devices  2.12 us (3%)
  between operations  0.68 us (1%)
    all_to_all x1, blocking collectives, local(): lax.all_to_all(outgoing, ('gx', 'gy'), split_axis=0, concat_axis=0, tiled...  17.8 us
    pallas_call x4, Pallas kernels, call(): pl.pallas_call(kernel, in_specs=[space(i in hbm) for i in range(len(opera...  17.1 us
    all_to_all x1, blocking collectives, local(): lax.all_to_all(returning, ('gx', 'gy'), split_axis=0, concat_axis=0, tile...  14.9 us
    ppermute x3, starting transfers between devices, from_above(): return lax.ppermute(value, axis, [((i + 1) % n, i) for i in range(n)])  5.61 us
    ppermute x3, starting transfers between devices, from_below(): return lax.ppermute(value, axis, [(i, (i + 1) % n) for i in range(n)])  3.56 us
    unnamed x14, local copies, waits for them, and re-layouts  2.76 us
    ppermute x3, waiting for transfers between devices, from_below(): return lax.ppermute(value, axis, [(i, (i + 1) % n) for i in range(n)])  1.75 us
  transfers between devices with their start and end apart: 6, of which 3 were waited for; matrix products, arithmetic and copies ran while one was open for 0% of the time, Pallas kernels for 0%

profile of v4, /device:TPU:4, one launch (start us, length us, event | category | flops | bytes accessed | tf_op | source)
XLA Modules:
  0.0 64.4 jit_solution(3714536266919969577)
XLA Ops:
  0.6 1.3 %copy-done = f32[16,10,16,128]{3,2,1,0:T(8,128)S(1)} copy-done((f32[16,10,16,128]{3,2,1,0:T(8,128)S(1)}, f32[16,10,16,128]{3,2,1,0:T(8,128)}, u32[]{:S(2)}) %copy-start) | copy-done | bytes 1310744
  2.0 0.8 %shard_map.68 = (f32[160,128]{1,0:T(8,128)S(1)}, f32[160,128]{1,0:T(8,128)S(1)}, f32[160,128]{1,0:T(8,128)S(1)}, f32[160,128]{1,0:T(8,128)S(1)}, f32[160,128]{1,0:T(8,128)S(1)}, /*index=5*/f32[160,128]{1,0:T(8,128)S(1)}) custom-call(f32[2560,128]{1,0:T(8,128)S(1)} %bitcast.6), custom_call_target="tpu_custom_call" | custom-call | tf_op jit(solution)/shard_map/pallas_call | solution.py:429
  2.7 2.0 %collective-permute-start = (f32[160,128]{1,0:T(8,128)S(1)}, f32[160,128]{1,0:T(8,128)S(1)}, u32[]{:S(2)}, u32[]{:S(2)}) collective-permute-start(f32[160,128]{1,0:T(8,128)S(1)} %get-tuple-element.13), channel_id=1, source_target_pairs={{0,32},{32,64},{64,96},{96,0},{1,33},{33,65},{65,97},{97,1},{2,34}... | collective-permute-start | bytes 245768 | tf_op jit(solution)/shard_map/ppermute | solution.py:450
  4.7 2.2 %collective-permute-start.1 = (f32[160,128]{1,0:T(8,128)S(1)}, f32[160,128]{1,0:T(8,128)S(1)}, u32[]{:S(2)}, u32[]{:S(2)}) collective-permute-start(f32[160,128]{1,0:T(8,128)S(1)} %get-tuple-element.14), channel_id=1, source_target_pairs={{32,0},{64,32},{96,64},{0,96},{33,1},{65,33},{97,65},{1,97},{34,2}... | collective-permute-start | bytes 245768 | tf_op jit(solution)/shard_map/ppermute | solution.py:454
  6.9 1.6 %collective-permute-start.2 = (f32[160,128]{1,0:T(8,128)S(1)}, f32[160,128]{1,0:T(8,128)S(1)}, u32[]{:S(2)}, u32[]{:S(2)}) collective-permute-start(f32[160,128]{1,0:T(8,128)S(1)} %get-tuple-element.15), channel_id=1, source_target_pairs={{0,8},{8,16},{16,24},{24,0},{1,9},{9,17},{17,25},{25,1},{2,10},{10... | collective-permute-start | bytes 245768 | tf_op jit(solution)/shard_map/ppermute | solution.py:450
  8.5 1.7 %collective-permute-start.3 = (f32[160,128]{1,0:T(8,128)S(1)}, f32[160,128]{1,0:T(8,128)S(1)}, u32[]{:S(2)}, u32[]{:S(2)}) collective-permute-start(f32[160,128]{1,0:T(8,128)S(1)} %get-tuple-element.16), channel_id=1, source_target_pairs={{8,0},{16,8},{24,16},{0,24},{9,1},{17,9},{25,17},{1,25},{10,2},{18... | collective-permute-start | bytes 245768 | tf_op jit(solution)/shard_map/ppermute | solution.py:454
  10.1 0.0 collective-permute-start.4
  10.1 0.0 collective-permute-done.x_lo
  10.1 1.7 %collective-permute-start.5 = (f32[160,128]{1,0:T(8,128)S(1)}, f32[160,128]{1,0:T(8,128)S(1)}, u32[]{:S(2)}, u32[]{:S(2)}) collective-permute-start(f32[160,128]{1,0:T(8,128)S(1)} %get-tuple-element.18), channel_id=1, source_target_pairs={{1,0},{2,1},{3,2},{4,3},{5,4},{6,5},{7,6},{0,7},{9,8},{10,9},{11,1... | collective-permute-start | bytes 245768 | tf_op jit(solution)/shard_map/ppermute | solution.py:454
  11.9 0.0 collective-permute-done.1.x_hi
  11.9 0.7 %collective-permute-done.2.y_lo = f32[160,128]{1,0:T(8,128)S(1)} collective-permute-done((f32[160,128]{1,0:T(8,128)S(1)}, f32[160,128]{1,0:T(8,128)S(1)}, u32[]{:S(2)}, u32[]{:S(2)}) %collective-permute-start.2) | collective-permute-done | bytes 81952 | tf_op jit(solution)/shard_map/ppermute | solution.py:450
  12.6 0.4 collective-permute-done.3.y_hi
  12.9 1.1 %collective-permute-done.4.z_lo = f32[160,128]{1,0:T(8,128)S(1)} collective-permute-done((f32[160,128]{1,0:T(8,128)S(1)}, f32[160,128]{1,0:T(8,128)S(1)}, u32[]{:S(2)}, u32[]{:S(2)}) %collective-permute-start.4) | collective-permute-done | bytes 81952 | tf_op jit(solution)/shard_map/ppermute | solution.py:450
  14.0 0.0 collective-permute-done.5.z_hi
  14.0 0.0 copy-done.5
  14.0 0.0 copy-start.3
  14.0 0.7 %copy-done.3 = s32[1024,3]{0,1:T(4,128)S(1)} copy-done((s32[1024,3]{0,1:T(4,128)S(1)}, s32[1024,3]{0,1:T(4,128)}, u32[]{:S(2)}) %copy-start.3) | copy-done | bytes 12312
  14.7 0.7 %copy-done.6 = f32[3,10,10]{2,0,1:T(4,128)S(1)} copy-done((f32[3,10,10]{2,0,1:T(4,128)S(1)}, f32[3,10,10]{2,0,1:T(4,128)}, u32[]{:S(2)}) %copy-start.6) | copy-done | bytes 1224
  15.5 4.9 %shard_map.69 = (f32[2560,128]{1,0:T(8,128)S(1)}, f32[16,64,128]{2,1,0:T(8,128)S(1)}, bf16[2,160,512]{2,1,0:T(8,128)(2,1)S(1)}) custom-call(s32[1024]{0:T(1024)S(1)} %copy-done.5, s32[3,1024]{1,0:T(4,128)S(1)} %bitcast.9, f32[2560,128]{1,0:T(8,128)S(1)} %bitcast.7, f32[160,128]{1,0:T(8,128)S(1)} %collective-permute-done.x_lo, ...), custom_call_target="tpu_custom_call" | custom-call | tf_op jit(solution)/shard_map/pallas_call | solution.py:429
  20.4 17.8 %all_to_all.10.arrived_ref = f32[16,64,128]{2,1,0:T(8,128)S(1)} all-to-all(f32[16,64,128]{2,1,0:T(8,128)S(1)} %get-tuple-element.20), channel_id=1, replica_groups=mesh['gx'=4,'gy'=4,'gz'=8] {'gx','gy'}, dimensions={0} | all-to-all | bytes 1048576 | tf_op jit(solution)/shard_map/all_to_all | solution.py:477
  38.2 7.0 %shard_map.70 = (f32[16,10,16,256]{3,2,1,0:T(8,128)}, f32[16,40,128]{2,1,0:T(8,128)S(1)}) custom-call(s32[1024]{0:T(1024)S(1)} %copy-done.5, f32[16,10,16,256]{3,2,1,0:T(8,128)S(1)} %bitcast.8, f32[16,64,128]{2,1,0:T(8,128)S(1)} %all_to_all.10.arrived_ref, bf16[2,160,512]{2,1,0:T(8,128)(2,1)S(1)} %get-tuple-element.21.coef_ref), custom_call_target="tpu_custom_call" | custom-call | tf_op jit(solution)/shard_map/pallas_call | solution.py:429
  45.1 14.9 %all_to_all.11.back_ref = f32[16,40,128]{2,1,0:T(8,128)S(1)} all-to-all(f32[16,40,128]{2,1,0:T(8,128)S(1)} %get-tuple-element.22), channel_id=1, replica_groups=mesh['gx'=4,'gy'=4,'gz'=8] {'gx','gy'}, dimensions={0} | all-to-all | bytes 655360 | tf_op jit(solution)/shard_map/all_to_all | solution.py:504
  60.0 0.0 copy-done.4
  60.0 4.4 %shard_map.71 = f32[2560,128]{1,0:T(8,128)} custom-call(s32[1024]{0:T(1024)S(1)} %copy-done.5, s32[3,1024]{1,0:T(4,128)S(1)} %bitcast.10, f32[2560,128]{1,0:T(8,128)S(1)} %get-tuple-element.19.new_ref, f32[16,40,128]{2,1,0:T(8,128)S(1)} %all_to_all.11.back_ref), custom_call_target="tpu_custom_call" | custom-call | tf_op jit(solution)/shard_map/pallas_call | solution.py:429
  (8 shorter events, 0.0 us)
Async XLA Ops:
  0.6 1.3 %copy-start = (f32[16,10,16,128]{3,2,1,0:T(8,128)S(1)}, f32[16,10,16,128]{3,2,1,0:T(8,128)}, u32[]{:S(2)}) copy-start(f32[16,10,16,128]{3,2,1,0:T(8,128)} %param.5) | copy-start | bytes 3932164
  1.9 12.1 %copy-start.1 = (f32[16,10,16,128]{3,2,1,0:T(8,128)S(1)}, f32[16,10,16,128]{3,2,1,0:T(8,128)}, u32[]{:S(2)}) copy-start(f32[16,10,16,128]{3,2,1,0:T(8,128)} %param.5) | copy-start | bytes 3932164
  1.9 12.1 %copy-start.5 = (s32[1024]{0:T(1024)S(1)}, s32[1024]{0:T(1024)}, u32[]{:S(2)}) copy-start(s32[1024]{0:T(1024)} %owner_hbm.5) | copy-start | bytes 12292
  2.7 7.4 %collective-permute-start = (f32[160,128]{1,0:T(8,128)S(1)}, f32[160,128]{1,0:T(8,128)S(1)}, u32[]{:S(2)}, u32[]{:S(2)}) collective-permute-start(f32[160,128]{1,0:T(8,128)S(1)} %get-tuple-element.13), channel_id=1, source_target_pairs={{0,32},{32,64},{64,96},{96,0},{1,33},{33,65},{65,97},{97,1},{2,34}... | collective-permute-start | bytes 245768 | tf_op jit(solution)/shard_map/ppermute | solution.py:450
  4.7 7.2 %collective-permute-start.1 = (f32[160,128]{1,0:T(8,128)S(1)}, f32[160,128]{1,0:T(8,128)S(1)}, u32[]{:S(2)}, u32[]{:S(2)}) collective-permute-start(f32[160,128]{1,0:T(8,128)S(1)} %get-tuple-element.14), channel_id=1, source_target_pairs={{32,0},{64,32},{96,64},{0,96},{33,1},{65,33},{97,65},{1,97},{34,2}... | collective-permute-start | bytes 245768 | tf_op jit(solution)/shard_map/ppermute | solution.py:454
  6.9 5.7 %collective-permute-start.2 = (f32[160,128]{1,0:T(8,128)S(1)}, f32[160,128]{1,0:T(8,128)S(1)}, u32[]{:S(2)}, u32[]{:S(2)}) collective-permute-start(f32[160,128]{1,0:T(8,128)S(1)} %get-tuple-element.15), channel_id=1, source_target_pairs={{0,8},{8,16},{16,24},{24,0},{1,9},{9,17},{17,25},{25,1},{2,10},{10... | collective-permute-start | bytes 245768 | tf_op jit(solution)/shard_map/ppermute | solution.py:450
  8.5 4.4 %collective-permute-start.3 = (f32[160,128]{1,0:T(8,128)S(1)}, f32[160,128]{1,0:T(8,128)S(1)}, u32[]{:S(2)}, u32[]{:S(2)}) collective-permute-start(f32[160,128]{1,0:T(8,128)S(1)} %get-tuple-element.16), channel_id=1, source_target_pairs={{8,0},{16,8},{24,16},{0,24},{9,1},{17,9},{25,17},{1,25},{10,2},{18... | collective-permute-start | bytes 245768 | tf_op jit(solution)/shard_map/ppermute | solution.py:454
  10.1 3.9 %collective-permute-start.4 = (f32[160,128]{1,0:T(8,128)S(1)}, f32[160,128]{1,0:T(8,128)S(1)}, u32[]{:S(2)}, u32[]{:S(2)}) collective-permute-start(f32[160,128]{1,0:T(8,128)S(1)} %get-tuple-element.17), channel_id=1, source_target_pairs={{0,1},{1,2},{2,3},{3,4},{4,5},{5,6},{6,7},{7,0},{8,9},{9,10},{10,1... | collective-permute-start | bytes 245768 | tf_op jit(solution)/shard_map/ppermute | solution.py:450
  10.1 3.9 %collective-permute-start.5 = (f32[160,128]{1,0:T(8,128)S(1)}, f32[160,128]{1,0:T(8,128)S(1)}, u32[]{:S(2)}, u32[]{:S(2)}) collective-permute-start(f32[160,128]{1,0:T(8,128)S(1)} %get-tuple-element.18), channel_id=1, source_target_pairs={{1,0},{2,1},{3,2},{4,3},{5,4},{6,5},{7,6},{0,7},{9,8},{10,9},{11,1... | collective-permute-start | bytes 245768 | tf_op jit(solution)/shard_map/ppermute | solution.py:454
  14.0 0.7 %copy-start.3 = (s32[1024,3]{0,1:T(4,128)S(1)}, s32[1024,3]{0,1:T(4,128)}, u32[]{:S(2)}) copy-start(s32[1024,3]{0,1:T(4,128)} %param.9) | copy-start | bytes 36868
  14.7 0.7 %copy-start.6 = (f32[3,10,10]{2,0,1:T(4,128)S(1)}, f32[3,10,10]{2,0,1:T(4,128)}, u32[]{:S(2)}) copy-start(f32[3,10,10]{2,0,1:T(4,128)} %param.7) | copy-start | bytes 3604
  15.5 22.7 %copy-start.2 = (f32[16,16,10,256]{3,1,2,0:T(8,128)S(1)}, f32[16,16,10,256]{3,1,2,0:T(8,128)}, u32[]{:S(2)}) copy-start(f32[16,16,10,256]{3,1,2,0:T(8,128)} %param.6) | copy-start | bytes 7864324
  38.2 21.8 %copy-start.4 = (s32[1024,3]{0,1:T(4,128)S(1)}, s32[1024,3]{0,1:T(4,128)}, u32[]{:S(2)}) copy-start(s32[1024,3]{0,1:T(4,128)} %param.9) | copy-start | bytes 36868

commit v5 on v4

--- a/solution.py
+++ b/solution.py
@@ -80,11 +80,7 @@
     return copy
 
 
-def coefficients(jac_ref, pad_ref, outs):
-    pad_ref[...] = jnp.zeros(pad_ref.shape, F32)
-    for d in range(3):
-        for g in range(F):
-            pad_ref[d, g : g + 1, 0:F] = jac_ref[g, d : d + 1, :]
+def coefficients(pad_ref, order, out):
     row, lane = (lax.broadcasted_iota(jnp.int32, (128, 128), d) for d in range(2))
     eye = jnp.where((row[:16] == lane[:16]) & (row[:16] < F), 0.125, 0.0).astype(F32)
     scaled = [0.125 * pad_ref[d] for d in range(3)]
@@ -104,17 +100,22 @@
     row, col = (lax.broadcasted_iota(jnp.int32, (ROWS, 128), d) for d in range(2))
     rows = one(row // B == col).astype(BF16)
     pad = jnp.zeros((112, 512), BF16)
-    for (s, a, b), out in zip(((1, 0, 2), (0, 1, 2)), outs):
-        coef = (
-            (eye - scaled[s])
-            + pltpu.roll(eye + scaled[s], 16, 1)
-            - pltpu.roll(scaled[a], 32, 1)
-            - pltpu.roll(scaled[b], 48, 1)
-        )
-        for part, value in enumerate(split(coef)):
-            wide1 = jnp.concatenate([dot(value, first).astype(BF16), pad], axis=0)
-            wide2 = jnp.concatenate([dot(value, second).astype(BF16), pad], axis=0)
-            out[part] = (dot(rows, wide1) * mask_first + dot(rows, wide2) * mask_second).astype(BF16)
+    s, a, b = order
+    coef = (
+        (eye - scaled[s])
+        + pltpu.roll(eye + scaled[s], 16, 1)
+        - pltpu.roll(scaled[a], 32, 1)
+        - pltpu.roll(scaled[b], 48, 1)
+    )
+    for part, value in enumerate(split(coef)):
+        wide1 = jnp.concatenate([dot(value, first).astype(BF16), pad], axis=0)
+        wide2 = jnp.concatenate([dot(value, second).astype(BF16), pad], axis=0)
+        out[part] = (dot(rows, wide1) * mask_first + dot(rows, wide2) * mask_second).astype(BF16)
+
+
+def prepare_kernel(pad_ref, coef_ref, ghost_ref, face_ref, mean_ref):
+    coefficients(pad_ref, (0, 1, 2), coef_ref)
+    fine_constants(ghost_ref, face_ref, mean_ref)
 
 
 def faces_kernel(coarse_ref, x_lo, x_hi, y_lo, y_hi, z_lo, z_hi):
@@ -147,14 +148,18 @@
 
 
 def coarse_kernel(
-    owner_hbm, offset_hbm, coarse_ref, x_lo, x_hi, y_lo, y_hi, z_lo, z_hi, jac_hbm, new_ref, out_ref, fine_coef_ref, old_ref,
-    mid_ref, hi_ref, lo_ref, rest_ref, total_ref, coef_ref, pad_ref,
+    owner_hbm, offset_hbm, coarse_ref, x_lo, x_hi, y_lo, y_hi, z_lo, z_hi, jac_hbm, new_ref, out_ref, pad_ref, old_ref,
+    mid_ref, hi_ref, lo_ref, rest_ref, total_ref, coef_ref,
     owner_ref, offset_ref, jac_ref, sems
 ):
     fetch_owner = fetch(owner_hbm, owner_ref, sems.at[0])
     fetch_offset = fetch(offset_hbm, offset_ref, sems.at[1])
     fetch(jac_hbm, jac_ref, sems.at[2]).wait()
-    coefficients(jac_ref, pad_ref, (coef_ref, fine_coef_ref))
+    pad_ref[...] = jnp.zeros(pad_ref.shape, F32)
+    for d in range(3):
+        for g in range(F):
+            pad_ref[d, g : g + 1, 0:F] = jac_ref[g, d : d + 1, :]
+    coefficients(pad_ref, (1, 0, 2), coef_ref)
     lane = lanes_of((B, 128))
     ghost_zero = jnp.zeros((16 - F, 128), F32)
     for pair in range(B // 2):
@@ -242,9 +247,9 @@
 
 
 def fine_kernel(
-    owner_hbm, fine_hbm, arrived_ref, coef_ref, out_hbm, back_ref, hi_ref, lo_ref, wide_ref, rest_ref,
+    owner_hbm, fine_hbm, arrived_ref, coef_ref, ghost_ref, face_ref, pair_ref, out_hbm, back_ref, hi_ref, lo_ref, wide_ref, rest_ref,
     total_ref, value_ref, face_out_ref, spread_ref, mixed_ref, mean_ref, source_ref, owner_ref, fine_ref, out_ref,
-    ghost_ref, face_ref, pair_ref, sems
+    sems
 ):
     fetch_owner = fetch(owner_hbm, owner_ref, sems.at[0])
     batches_at = [slice(i * BATCH, i * BATCH + BATCH) for i in range(FSLOTS // BATCH)]
@@ -260,7 +265,6 @@
             source_ref[jnp.minimum(holder ^ first_here, FSLOTS)] = member
     held = sum(jnp.where(source_ref[slot] >= 0, 1, 0) for slot in range(FSLOTS))
     batches = (held + BATCH - 1) // BATCH
-    fine_constants(ghost_ref, face_ref, pair_ref)
     for copy in fetch_fine:
         copy.wait()
 
@@ -461,24 +465,30 @@
         from_below(z_last, "gz"),
         from_above(z_first, "gz"),
     )
-    new, outgoing, coef = call(
+    new, outgoing, padded = call(
         coarse_kernel,
         (fine_owner, offset, rows, *halo, jacobians),
-        [((B * ROWS, 128), F32), ((GROUP, MESSAGE, 128), F32), ((2, ROWS, 512), BF16)],
+        [((B * ROWS, 128), F32), ((GROUP, MESSAGE, 128), F32), ((3, 16, 128), F32)],
         14,
         [pltpu.VMEM((B * PITCH, 128), F32)] * 2
         + [pltpu.VMEM((B // 2, 512, 256), BF16)] * 2
         + [pltpu.VMEM((B // 2, ROWS, 256), F32)] * 2
-        + [pltpu.VMEM((2, ROWS, 512), BF16), pltpu.VMEM((3, 16, 128), F32)]
+        + [pltpu.VMEM((2, ROWS, 512), BF16)]
         + INDEX
         + [pltpu.VMEM((F, 3, F), F32), pltpu.SemaphoreType.DMA((3,))],
         hbm=(0, 1, 9),
     )
+    prepared = call(
+        prepare_kernel,
+        (padded,),
+        [((2, ROWS, 512), BF16), ((128, 768), BF16), ((128, 256), BF16), ((256, 128), BF16)],
+        6,
+    )
     arrived = lax.all_to_all(outgoing, ("gx", "gy"), split_axis=0, concat_axis=0, tiled=True)
 
     fine_new, returning = call(
         fine_kernel,
-        (fine_owner, fine_rows, arrived, coef),
+        (fine_owner, fine_rows, arrived, *prepared),
         [((FSLOTS, F, B, 256), F32), ((GROUP, HALF // 2, 128), F32)],
         24,
         [pltpu.VMEM((BATCH, 512, 256), BF16)] * 2
@@ -493,9 +503,6 @@
             INDEX[0],
             pltpu.VMEM((FSLOTS, F, B, 256), F32),
             pltpu.VMEM((FSLOTS, F, B, 256), F32),
-            pltpu.VMEM((128, 768), BF16),
-            pltpu.VMEM((128, 256), BF16),
-            pltpu.VMEM((256, 128), BF16),
             pltpu.SemaphoreType.DMA((1 + 2 * (FSLOTS // BATCH),)),
         ],
         hbm=(0, 1),

time: 65.7 us -> 70.2 us (1.068); the launches traced: 64.4 us -> 70.1 us
  blocking collectives: 32.6 us -> 16.5 us
  waiting for transfers between devices: 2.12 us -> 12.6 us
  local copies, waits for them, and re-layouts: 2.76 us -> 8.99 us
  starting transfers between devices: 9.17 us -> 13.9 us
    all_to_all x1 -> x0, blocking collectives: 17.8 us -> none  [local(): lax.all_to_all(outgoing, ('gx', 'gy'), split_axis=0, concat_axis=0, tiled...]
    all_to_all x0 -> x1, waiting for transfers between devices: none -> 10.5 us  [local(): lax.all_to_all(outgoing, ('gx', 'gy'), split_axis=0, concat_axis=0, tiled...]
    unnamed x14 -> x32, local copies, waits for them, and re-layouts: 2.76 us -> 8.99 us
    all_to_all x0 -> x1, starting transfers between devices: none -> 4.75 us  [local(): lax.all_to_all(outgoing, ('gx', 'gy'), split_axis=0, concat_axis=0, tiled...]
    all_to_all x1, blocking collectives: 14.9 us -> 16.5 us  [local(): lax.all_to_all(returning, ('gx', 'gy'), split_axis=0, concat_axis=0, tile...]
    pallas_call x4 -> x5, Pallas kernels: 17.1 us -> 17.3 us  [call(): pl.pallas_call(kernel, in_specs=[space(i in hbm) for i in range(len(opera...]
  transfers between devices with their start and end apart: 6 -> 7, of which waited for: 3 -> 4; matrix products, arithmetic and copies ran while one was open for 0% -> 0% of each run, Pallas kernels for 0% -> 1%
where the time goes in v5:
time: 70.2 us; the launch traced here: 70.1 us
  Pallas kernels  17.3 us (25%)
  blocking collectives  16.5 us (24%)
  starting transfers between devices  13.9 us (20%)
  waiting for transfers between devices  12.6 us (18%)
  local copies, waits for them, and re-layouts  8.99 us (13%)
  between operations  0.73 us (1%)
    pallas_call x5, Pallas kernels, call(): pl.pallas_call(kernel, in_specs=[space(i in hbm) for i in range(len(opera...  17.3 us
    all_to_all x1, blocking collectives, local(): lax.all_to_all(returning, ('gx', 'gy'), split_axis=0, concat_axis=0, tile...  16.5 us
    all_to_all x1, waiting for transfers between devices, local(): lax.all_to_all(outgoing, ('gx', 'gy'), split_axis=0, concat_axis=0, tiled...  10.5 us
    unnamed x32, local copies, waits for them, and re-layouts  8.99 us
    ppermute x3, starting transfers between devices, from_above(): return lax.ppermute(value, axis, [((i + 1) % n, i) for i in range(n)])  5.61 us
    all_to_all x1, starting transfers between devices, local(): lax.all_to_all(outgoing, ('gx', 'gy'), split_axis=0, concat_axis=0, tiled...  4.75 us
    ppermute x3, starting transfers between devices, from_below(): return lax.ppermute(value, axis, [(i, (i + 1) % n) for i in range(n)])  3.56 us
    ppermute x3, waiting for transfers between devices, from_below(): return lax.ppermute(value, axis, [(i, (i + 1) % n) for i in range(n)])  1.75 us
  transfers between devices with their start and end apart: 7, of which 4 were waited for; matrix products, arithmetic and copies ran while one was open for 0% of the time, Pallas kernels for 1%

profile of v5, /device:TPU:4, one launch (start us, length us, event | category | flops | bytes accessed | tf_op | source)
XLA Modules:
  0.0 70.1 jit_solution(9718716074804315302)
XLA Ops:
  0.6 1.3 %copy-done = f32[16,10,16,128]{3,2,1,0:T(8,128)S(1)} copy-done((f32[16,10,16,128]{3,2,1,0:T(8,128)S(1)}, f32[16,10,16,128]{3,2,1,0:T(8,128)}, u32[]{:S(2)}) %copy-start) | copy-done | bytes 1310744
  2.0 0.8 %shard_map.68 = (f32[160,128]{1,0:T(8,128)S(1)}, f32[160,128]{1,0:T(8,128)S(1)}, f32[160,128]{1,0:T(8,128)S(1)}, f32[160,128]{1,0:T(8,128)S(1)}, f32[160,128]{1,0:T(8,128)S(1)}, /*index=5*/f32[160,128]{1,0:T(8,128)S(1)}) custom-call(f32[2560,128]{1,0:T(8,128)S(1)} %bitcast.6), custom_call_target="tpu_custom_call" | custom-call | tf_op jit(solution)/shard_map/pallas_call | solution.py:433
  2.7 2.0 %collective-permute-start = (f32[160,128]{1,0:T(8,128)S(1)}, f32[160,128]{1,0:T(8,128)S(1)}, u32[]{:S(2)}, u32[]{:S(2)}) collective-permute-start(f32[160,128]{1,0:T(8,128)S(1)} %get-tuple-element.17), channel_id=1, source_target_pairs={{0,32},{32,64},{64,96},{96,0},{1,33},{33,65},{65,97},{97,1},{2,34}... | collective-permute-start | bytes 245768 | tf_op jit(solution)/shard_map/ppermute | solution.py:454
  4.7 2.2 %collective-permute-start.1 = (f32[160,128]{1,0:T(8,128)S(1)}, f32[160,128]{1,0:T(8,128)S(1)}, u32[]{:S(2)}, u32[]{:S(2)}) collective-permute-start(f32[160,128]{1,0:T(8,128)S(1)} %get-tuple-element.18), channel_id=1, source_target_pairs={{32,0},{64,32},{96,64},{0,96},{33,1},{65,33},{97,65},{1,97},{34,2}... | collective-permute-start | bytes 245768 | tf_op jit(solution)/shard_map/ppermute | solution.py:458
  6.9 1.6 %collective-permute-start.2 = (f32[160,128]{1,0:T(8,128)S(1)}, f32[160,128]{1,0:T(8,128)S(1)}, u32[]{:S(2)}, u32[]{:S(2)}) collective-permute-start(f32[160,128]{1,0:T(8,128)S(1)} %get-tuple-element.19), channel_id=1, source_target_pairs={{0,8},{8,16},{16,24},{24,0},{1,9},{9,17},{17,25},{25,1},{2,10},{10... | collective-permute-start | bytes 245768 | tf_op jit(solution)/shard_map/ppermute | solution.py:454
  8.5 1.7 %collective-permute-start.3 = (f32[160,128]{1,0:T(8,128)S(1)}, f32[160,128]{1,0:T(8,128)S(1)}, u32[]{:S(2)}, u32[]{:S(2)}) collective-permute-start(f32[160,128]{1,0:T(8,128)S(1)} %get-tuple-element.20), channel_id=1, source_target_pairs={{8,0},{16,8},{24,16},{0,24},{9,1},{17,9},{25,17},{1,25},{10,2},{18... | collective-permute-start | bytes 245768 | tf_op jit(solution)/shard_map/ppermute | solution.py:458
  10.1 1.7 %collective-permute-start.5 = (f32[160,128]{1,0:T(8,128)S(1)}, f32[160,128]{1,0:T(8,128)S(1)}, u32[]{:S(2)}, u32[]{:S(2)}) collective-permute-start(f32[160,128]{1,0:T(8,128)S(1)} %get-tuple-element.22), channel_id=1, source_target_pairs={{1,0},{2,1},{3,2},{4,3},{5,4},{6,5},{7,6},{0,7},{9,8},{10,9},{11,1... | collective-permute-start | bytes 245768 | tf_op jit(solution)/shard_map/ppermute | solution.py:458
  11.9 0.7 collective-permute-done.2.y_lo
  12.9 1.1 %collective-permute-done.4.z_lo = f32[160,128]{1,0:T(8,128)S(1)} collective-permute-done((f32[160,128]{1,0:T(8,128)S(1)}, f32[160,128]{1,0:T(8,128)S(1)}, u32[]{:S(2)}, u32[]{:S(2)}) %collective-permute-start.4) | collective-permute-done | bytes 81952 | tf_op jit(solution)/shard_map/ppermute | solution.py:454
  14.0 0.7 %copy-done.10 = s32[1024,3]{0,1:T(4,128)S(1)} copy-done((s32[1024,3]{0,1:T(4,128)S(1)}, s32[1024,3]{0,1:T(4,128)}, u32[]{:S(2)}) %copy-start.10) | copy-done | bytes 12312
  14.7 0.7 %copy-done.15 = f32[3,10,10]{2,0,1:T(4,128)S(1)} copy-done((f32[3,10,10]{2,0,1:T(4,128)S(1)}, f32[3,10,10]{2,0,1:T(4,128)}, u32[]{:S(2)}) %copy-start.15) | copy-done | bytes 1224
  15.5 4.6 %shard_map.69 = (f32[2560,128]{1,0:T(8,128)S(1)}, f32[16,64,128]{2,1,0:T(8,128)S(1)}, f32[3,16,128]{2,1,0:T(8,128)S(1)}) custom-call(s32[1024]{0:T(1024)S(1)} %copy-done.12, s32[3,1024]{1,0:T(4,128)S(1)} %bitcast.9, f32[2560,128]{1,0:T(8,128)S(1)} %bitcast.7, f32[160,128]{1,0:T(8,128)S(1)} %collective-permute-done.x_lo, ...), custom_call_target="tpu_custom_call" | custom-call | tf_op jit(solution)/shard_map/pallas_call | solution.py:433
  20.1 1.0 %copy-done.3 = f32[2560,128]{1,0:T(8,128)} copy-done((f32[2560,128]{1,0:T(8,128)}, f32[2560,128]{1,0:T(8,128)S(1)}, u32[]{:S(2)}) %copy-start.3) | copy-done | bytes 1310744
  21.2 0.8 %copy-done.5 = f32[16,64,128]{2,1,0:T(8,128)} copy-done((f32[16,64,128]{2,1,0:T(8,128)}, f32[16,64,128]{2,1,0:T(8,128)S(1)}, u32[]{:S(2)}) %copy-start.5) | copy-done | bytes 524312
  22.6 4.7 %all-to-all-start = ((f32[16,64,128]{2,1,0:T(8,128)}), f32[16,64,128]{2,1,0:T(8,128)S(1)}, u32[]{:S(2)}, u32[]{:S(2)}) async-start(f32[16,64,128]{2,1,0:T(8,128)} %copy-done.5), calls=%async_computation | async-start | bytes 1048576 | tf_op jit(solution)/shard_map/all_to_all | solution.py:487
  27.3 0.7 %copy-done.14 = f32[3,16,128]{2,1,0:T(8,128)S(1)} copy-done((f32[3,16,128]{2,1,0:T(8,128)S(1)}, f32[3,16,128]{2,1,0:T(8,128)}, u32[]{:S(2)}) %copy-start.14) | copy-done | bytes 24600
  28.1 0.7 shard_map.70
  28.7 0.7 copy-done.6
  30.0 10.5 %all-to-all-done.arrived_ref = f32[16,64,128]{2,1,0:T(8,128)S(1)} async-done(((f32[16,64,128]{2,1,0:T(8,128)}), f32[16,64,128]{2,1,0:T(8,128)S(1)}, u32[]{:S(2)}, u32[]{:S(2)}) %all-to-all-start) | async-done | bytes 524320 | tf_op jit(solution)/shard_map/all_to_all | solution.py:487
  40.6 0.9 %copy-done.7 = bf16[128,768]{1,0:T(8,128)(2,1)S(1)} copy-done((bf16[128,768]{1,0:T(8,128)(2,1)S(1)}, bf16[128,768]{1,0:T(8,128)(2,1)}, u32[]{:S(2)}) %copy-start.7) | copy-done | bytes 196632
  41.5 0.8 %copy-done.9 = bf16[256,128]{1,0:T(8,128)(2,1)S(1)} copy-done((bf16[256,128]{1,0:T(8,128)(2,1)S(1)}, bf16[256,128]{1,0:T(8,128)(2,1)}, u32[]{:S(2)}) %copy-start.9) | copy-done | bytes 65560
  42.3 6.8 %shard_map.71 = (f32[16,10,16,256]{3,2,1,0:T(8,128)}, f32[16,40,128]{2,1,0:T(8,128)S(1)}) custom-call(s32[1024]{0:T(1024)S(1)} %copy-done.12, f32[16,10,16,256]{3,2,1,0:T(8,128)S(1)} %bitcast.8, f32[16,64,128]{2,1,0:T(8,128)S(1)} %all-to-all-done.arrived_ref, bf16[2,160,512]{2,1,0:T(8,128)(2,1)S(1)} %get-tuple-element.26.coef_ref, ...), custom_call_target="tpu_custom_call" | custom-call | tf_op jit(solution)/shard_map/pallas_call | solution.py:433
  49.2 16.5 %all_to_all.10.back_ref = f32[16,40,128]{2,1,0:T(8,128)S(1)} all-to-all(f32[16,40,128]{2,1,0:T(8,128)S(1)} %get-tuple-element.30), channel_id=1, replica_groups=mesh['gx'=4,'gy'=4,'gz'=8] {'gx','gy'}, dimensions={0} | all-to-all | bytes 655360 | tf_op jit(solution)/shard_map/all_to_all | solution.py:511
  65.7 4.4 %shard_map.72 = f32[2560,128]{1,0:T(8,128)} custom-call(s32[1024]{0:T(1024)S(1)} %copy-done.12, s32[3,1024]{1,0:T(4,128)S(1)} %bitcast.10, f32[2560,128]{1,0:T(8,128)S(1)} %copy-done.4, f32[16,40,128]{2,1,0:T(8,128)S(1)} %all_to_all.10.back_ref), custom_call_target="tpu_custom_call" | custom-call | tf_op jit(solution)/shard_map/pallas_call | solution.py:433
  (28 shorter events, 1.6 us)
Async XLA Ops:
  0.6 1.3 %copy-start = (f32[16,10,16,128]{3,2,1,0:T(8,128)S(1)}, f32[16,10,16,128]{3,2,1,0:T(8,128)}, u32[]{:S(2)}) copy-start(f32[16,10,16,128]{3,2,1,0:T(8,128)} %param.5) | copy-start | bytes 3932164
  1.9 12.1 %copy-start.1 = (f32[16,10,16,128]{3,2,1,0:T(8,128)S(1)}, f32[16,10,16,128]{3,2,1,0:T(8,128)}, u32[]{:S(2)}) copy-start(f32[16,10,16,128]{3,2,1,0:T(8,128)} %param.5) | copy-start | bytes 3932164
  1.9 12.1 %copy-start.12 = (s32[1024]{0:T(1024)S(1)}, s32[1024]{0:T(1024)}, u32[]{:S(2)}) copy-start(s32[1024]{0:T(1024)} %owner_hbm.5) | copy-start | bytes 12292
  2.7 7.4 %collective-permute-start = (f32[160,128]{1,0:T(8,128)S(1)}, f32[160,128]{1,0:T(8,128)S(1)}, u32[]{:S(2)}, u32[]{:S(2)}) collective-permute-start(f32[160,128]{1,0:T(8,128)S(1)} %get-tuple-element.17), channel_id=1, source_target_pairs={{0,32},{32,64},{64,96},{96,0},{1,33},{33,65},{65,97},{97,1},{2,34}... | collective-permute-start | bytes 245768 | tf_op jit(solution)/shard_map/ppermute | solution.py:454
  4.7 7.2 %collective-permute-start.1 = (f32[160,128]{1,0:T(8,128)S(1)}, f32[160,128]{1,0:T(8,128)S(1)}, u32[]{:S(2)}, u32[]{:S(2)}) collective-permute-start(f32[160,128]{1,0:T(8,128)S(1)} %get-tuple-element.18), channel_id=1, source_target_pairs={{32,0},{64,32},{96,64},{0,96},{33,1},{65,33},{97,65},{1,97},{34,2}... | collective-permute-start | bytes 245768 | tf_op jit(solution)/shard_map/ppermute | solution.py:458
  6.9 5.7 %collective-permute-start.2 = (f32[160,128]{1,0:T(8,128)S(1)}, f32[160,128]{1,0:T(8,128)S(1)}, u32[]{:S(2)}, u32[]{:S(2)}) collective-permute-start(f32[160,128]{1,0:T(8,128)S(1)} %get-tuple-element.19), channel_id=1, source_target_pairs={{0,8},{8,16},{16,24},{24,0},{1,9},{9,17},{17,25},{25,1},{2,10},{10... | collective-permute-start | bytes 245768 | tf_op jit(solution)/shard_map/ppermute | solution.py:454
  8.5 4.4 %collective-permute-start.3 = (f32[160,128]{1,0:T(8,128)S(1)}, f32[160,128]{1,0:T(8,128)S(1)}, u32[]{:S(2)}, u32[]{:S(2)}) collective-permute-start(f32[160,128]{1,0:T(8,128)S(1)} %get-tuple-element.20), channel_id=1, source_target_pairs={{8,0},{16,8},{24,16},{0,24},{9,1},{17,9},{25,17},{1,25},{10,2},{18... | collective-permute-start | bytes 245768 | tf_op jit(solution)/shard_map/ppermute | solution.py:458
  10.1 3.9 %collective-permute-start.4 = (f32[160,128]{1,0:T(8,128)S(1)}, f32[160,128]{1,0:T(8,128)S(1)}, u32[]{:S(2)}, u32[]{:S(2)}) collective-permute-start(f32[160,128]{1,0:T(8,128)S(1)} %get-tuple-element.21), channel_id=1, source_target_pairs={{0,1},{1,2},{2,3},{3,4},{4,5},{5,6},{6,7},{7,0},{8,9},{9,10},{10,1... | collective-permute-start | bytes 245768 | tf_op jit(solution)/shard_map/ppermute | solution.py:454
  10.1 3.9 %collective-permute-start.5 = (f32[160,128]{1,0:T(8,128)S(1)}, f32[160,128]{1,0:T(8,128)S(1)}, u32[]{:S(2)}, u32[]{:S(2)}) collective-permute-start(f32[160,128]{1,0:T(8,128)S(1)} %get-tuple-element.22), channel_id=1, source_target_pairs={{1,0},{2,1},{3,2},{4,3},{5,4},{6,5},{7,6},{0,7},{9,8},{10,9},{11,1... | collective-permute-start | bytes 245768 | tf_op jit(solution)/shard_map/ppermute | solution.py:458
  14.0 0.7 %copy-start.10 = (s32[1024,3]{0,1:T(4,128)S(1)}, s32[1024,3]{0,1:T(4,128)}, u32[]{:S(2)}) copy-start(s32[1024,3]{0,1:T(4,128)} %param.9) | copy-start | bytes 36868
  14.7 0.7 %copy-start.15 = (f32[3,10,10]{2,0,1:T(4,128)S(1)}, f32[3,10,10]{2,0,1:T(4,128)}, u32[]{:S(2)}) copy-start(f32[3,10,10]{2,0,1:T(4,128)} %param.7) | copy-start | bytes 3604
  15.5 25.1 %copy-start.2 = (f32[16,16,10,256]{3,1,2,0:T(8,128)S(1)}, f32[16,16,10,256]{3,1,2,0:T(8,128)}, u32[]{:S(2)}) copy-start(f32[16,16,10,256]{3,1,2,0:T(8,128)} %param.6) | copy-start | bytes 7864324
  20.1 1.1 %copy-start.3 = (f32[2560,128]{1,0:T(8,128)}, f32[2560,128]{1,0:T(8,128)S(1)}, u32[]{:S(2)}) copy-start(f32[2560,128]{1,0:T(8,128)S(1)} %get-tuple-element.23.new_ref) | copy-start | bytes 3932164
  21.2 0.8 %copy-start.5 = (f32[16,64,128]{2,1,0:T(8,128)}, f32[16,64,128]{2,1,0:T(8,128)S(1)}, u32[]{:S(2)}) copy-start(f32[16,64,128]{2,1,0:T(8,128)S(1)} %get-tuple-element.24) | copy-start | bytes 1572868
  22.0 0.6 copy-start.13
  22.6 18.0 %all-to-all-start = ((f32[16,64,128]{2,1,0:T(8,128)}), f32[16,64,128]{2,1,0:T(8,128)S(1)}, u32[]{:S(2)}, u32[]{:S(2)}) async-start(f32[16,64,128]{2,1,0:T(8,128)} %copy-done.5), calls=%async_computation | async-start | bytes 1048576 | tf_op jit(solution)/shard_map/all_to_all | solution.py:487
  27.3 0.7 %copy-start.14 = (f32[3,16,128]{2,1,0:T(8,128)S(1)}, f32[3,16,128]{2,1,0:T(8,128)}, u32[]{:S(2)}) copy-start(f32[3,16,128]{2,1,0:T(8,128)} %copy-done.13) | copy-start | bytes 73732
  28.7 0.7 copy-start.6
  29.4 0.6 copy-start.8
  40.5 0.9 %copy-start.7 = (bf16[128,768]{1,0:T(8,128)(2,1)S(1)}, bf16[128,768]{1,0:T(8,128)(2,1)}, u32[]{:S(2)}) copy-start(bf16[128,768]{1,0:T(8,128)(2,1)} %copy-done.6) | copy-start | bytes 589828
  41.5 0.8 %copy-start.9 = (bf16[256,128]{1,0:T(8,128)(2,1)S(1)}, bf16[256,128]{1,0:T(8,128)(2,1)}, u32[]{:S(2)}) copy-start(bf16[256,128]{1,0:T(8,128)(2,1)} %copy-done.8) | copy-start | bytes 196612
  42.3 23.3 %copy-start.4 = (f32[2560,128]{1,0:T(8,128)S(1)}, f32[2560,128]{1,0:T(8,128)}, u32[]{:S(2)}) copy-start(f32[2560,128]{1,0:T(8,128)} %copy-done.3) | copy-start | bytes 3932164
  42.3 23.3 %copy-start.11 = (s32[1024,3]{0,1:T(4,128)S(1)}, s32[1024,3]{0,1:T(4,128)}, u32[]{:S(2)}) copy-start(s32[1024,3]{0,1:T(4,128)} %param.9) | copy-start | bytes 36868
